TPU v7x, 32 devices: a whole 2x2x4 slice. The times are simulated.
32 devices in a mesh: groups: 2 (over x), ctx: 16 (over z, y, core).
Axes of the slice: x: 2, y: 2, z: 4, core: 2. Of those that a mesh axis runs over, the one named last changes fastest.
Arguments:
- queries: bfloat16 [2560, 4096], P(('groups', 'ctx')), parts along dimension 0, may hold values from -200 to 200
- fresh_key_value: bfloat16 [2, 2560, 512], P(None, ('groups', 'ctx')), parts along dimension 1, may hold values from -6 to 6
- cache_key_value: bfloat16 [2, 4096, 512], P(None, ('groups', 'ctx')), parts along dimension 1, may hold values from -6 to 6
- residual: bfloat16 [2560, 2048], P(('groups', 'ctx')), parts along dimension 0, may hold values from -6 to 6
- norm_gain: float32 [2048], replicated, may hold values from 0.5 to 2
- out_proj: bfloat16 [4096, 2048], P('ctx'), may hold values from -0.09375 to 0.09375
- w_gate_up: bfloat16 [32, 2048, 1536], P('ctx'), may hold values from -0.125 to 0.125
- w_down: bfloat16 [32, 768, 2048], P('ctx'), may hold values from -0.21875 to 0.21875
- route_ids: int32 [2560, 8], P(('groups', 'ctx')), parts along dimension 0, may hold values from 0 to 31, all different within a row; in each aligned block of 80 rows (0 to 79, 80 to 159, ...) at most 30 rows name the same one
- route_weights: float32 [2560, 8], P(('groups', 'ctx')), parts along dimension 0, may hold values from 0.05 to 1
- placement: int32 [32], replicated, may hold values from 0 to 31, each once
Outputs:
- hidden: bfloat16 [2560, 2048], P(('groups', 'ctx')), parts along dimension 0
- expert_out: bfloat16 [2560, 2048], P(('groups', 'ctx')), parts along dimension 0
There are 2 independent parts, one for each index of `groups`. A program takes and returns all parts, laid end to end along the dimension named above; an argument that names none is the same for every part. Nothing has to cross between parts.
Inputs may be any that keep to these rules, and one draw needn't show every extreme that they name: `route_ids`: among the rows of one index of ctx, no expert is named by more than 30 rows, a bound that some block reaches. `placement`: every slot once; slot s is the first index of w_gate_up and w_down.
All inputs are finite; a program needn't handle non-finite values.
Results may differ from a plain program's by a relative error of at most 0.017.
Values may be sent and summed in bfloat16 or wider, within the bound.
No kernel may reach another device: no remote copies, remote signals or barrier semaphores. Data moves between devices by JAX's collectives and lax.ppermute only.
A program may use at most 128 MiB of HBM per device.

v0:
```python
import jax
import jax.numpy as jnp
from jax import lax
from jax.sharding import PartitionSpec as P

D = 2048
QUERY_HEADS = 32
KEY_VALUE_HEADS = 4
HEAD_SIZE = 128
FF = 768
TOPK = 8


epsilon = 1e-06


def local(
    queries,
    fresh_key_value,
    cache_key_value,
    residual,
    norm_gain,
    out_proj,
    w_gate_up,
    w_down,
    route_ids,
    route_weights,
    placement,
):
    count_of_rows = queries.shape[0]
    query_group_width = QUERY_HEADS // KEY_VALUE_HEADS
    scale_for_scores = HEAD_SIZE ** (-0.5)
    heads_of_query = queries.reshape(count_of_rows, KEY_VALUE_HEADS, query_group_width, HEAD_SIZE)
    self_keys = fresh_key_value[0].reshape(count_of_rows, KEY_VALUE_HEADS, HEAD_SIZE)
    self_values = fresh_key_value[1].reshape(count_of_rows, KEY_VALUE_HEADS, HEAD_SIZE)
    self_score = (
        jnp.einsum("ejaz,ejz->eja", heads_of_query, self_keys, preferred_element_type=jnp.float32)
        * scale_for_scores
    )
    start_carry = (
        self_score,
        jnp.ones_like(self_score),
        jnp.broadcast_to(self_values.astype(jnp.float32)[:, :, None, :], heads_of_query.shape),
    )

    def absorb_block(carried, block_pair):
        running_max, totals, weighted_total = carried
        block_keys, block_values = block_pair
        scores = (
            jnp.einsum(
                "rkgd,jkd->rkgj", heads_of_query, block_keys, preferred_element_type=jnp.float32
            )
            * scale_for_scores
        )
        new_max = jnp.maximum(running_max, jnp.max(scores, axis=-1))
        reduce_factor = jnp.exp(running_max - new_max)
        weights = jnp.exp(scores - new_max[..., None])
        totals = totals * reduce_factor + jnp.sum(weights, axis=-1)
        weighted_total = weighted_total * reduce_factor[..., None] + jnp.einsum(
            "rkgj,jkd->rkgd",
            weights.astype(jnp.bfloat16),
            block_values,
            preferred_element_type=jnp.float32,
        )
        return ((new_max, totals, weighted_total), None)

    carried = start_carry
    rows_per_shard = lax.all_gather(cache_key_value, "ctx", axis=1, tiled=True)
    count_of_keys = rows_per_shard.shape[1]
    key_extent = 512
    piled_outputs = rows_per_shard.reshape(
        2, count_of_keys // key_extent, key_extent, KEY_VALUE_HEADS, HEAD_SIZE
    )
    carried, unused = lax.scan(absorb_block, carried, (piled_outputs[0], piled_outputs[1]))
    running_max, totals, weighted_total = carried
    attention = (
        (weighted_total / totals[..., None])
        .reshape(count_of_rows, QUERY_HEADS * HEAD_SIZE)
        .astype(jnp.bfloat16)
    )
    projected = jnp.dot(
        attention,
        lax.all_gather(out_proj, "ctx", axis=0, tiled=True),
        preferred_element_type=jnp.float32,
    )
    hidden = (residual.astype(jnp.float32) + projected).astype(jnp.bfloat16)
    hidden_wide = hidden.astype(jnp.float32)
    normed = (
        hidden_wide
        * lax.rsqrt(jnp.mean(hidden_wide * hidden_wide, axis=-1, keepdims=True) + epsilon)
        * norm_gain
    ).astype(jnp.bfloat16)
    expert_count = placement.shape[0]
    capacity = max(2, 3 * count_of_rows * TOPK // (2 * expert_count))
    expert_range = jnp.arange(expert_count, dtype=jnp.int32)
    slot_ids = jnp.sum(
        jnp.where(route_ids[..., None] == expert_range, placement, 0), axis=-1
    ).reshape(-1)
    assigned = count_of_rows * TOPK
    one_hot = (slot_ids[:, None] == expert_range[None, :]).astype(jnp.int32)
    ranks = jnp.sum(one_hot * (jnp.cumsum(one_hot, axis=0) - 1), axis=1)
    target = slot_ids * capacity + ranks
    source = (
        jnp.full((expert_count * capacity,), assigned, jnp.int32)
        .at[target]
        .set(jnp.arange(assigned, dtype=jnp.int32))
    )
    filled = source < assigned
    source_rows = jnp.minimum(source // TOPK, count_of_rows - 1)
    outgoing = jnp.where(filled[:, None], normed[source_rows], jnp.zeros((), jnp.bfloat16)).reshape(
        expert_count, capacity, D
    )
    incoming = lax.all_to_all(outgoing, "ctx", split_axis=0, concat_axis=0, tiled=True)
    local_count = w_gate_up.shape[0]
    grouped = incoming.reshape(-1, local_count, capacity, D)
    both = jnp.einsum("nemd,edf->nemf", grouped, w_gate_up, preferred_element_type=jnp.float32)
    active = (jax.nn.silu(both[..., :FF]) * both[..., FF:]).astype(jnp.bfloat16)
    produced = jnp.einsum(
        "nemf,efd->nemd", active, w_down, preferred_element_type=jnp.float32
    ).astype(jnp.bfloat16)
    returned = lax.all_to_all(
        produced.reshape(expert_count, capacity, D), "ctx", split_axis=0, concat_axis=0, tiled=True
    )
    routed = (
        returned.reshape(expert_count * capacity, D)[target]
        .reshape(count_of_rows, TOPK, D)
        .astype(jnp.float32)
    )
    gate_share = route_weights / jnp.sum(route_weights, axis=-1, keepdims=True)
    expert_out = jnp.sum(gate_share[..., None] * routed, axis=1).astype(jnp.bfloat16)
    return (hidden, expert_out)


def solution(mesh):
    in_specs = (
        P(("groups", "ctx"), None),
        P(None, ("groups", "ctx"), None),
        P(None, ("groups", "ctx"), None),
        P(("groups", "ctx"), None),
        P(),
        P("ctx", None),
        P("ctx", None, None),
        P("ctx", None, None),
        P(("groups", "ctx"), None),
        P(("groups", "ctx"), None),
        P(),
    )
    out_specs = (P(("groups", "ctx"), None), P(("groups", "ctx"), None))
    return jax.shard_map(local, mesh=mesh, in_specs=in_specs, out_specs=out_specs, check_vma=False)
```

profile of v0, /device:TPU:13, one launch (start us, length us, event | category | flops | bytes accessed | tf_op | source)
XLA Modules:
  0.0 445.3 jit_solution(2338805867204558841)
XLA Ops:
  7.2 0.7 all-gather.3.cloned.1.call-update
  7.9 0.7 all-gather.5.cloned.1.call-update
  8.7 0.8 select_reduce_fusion
  9.7 1.2 copy.67
  10.9 0.9 slice_convert_fusion
  12.2 0.5 fusion.47
  12.9 1.5 reduce-window.6
  15.0 4.1 scatter_custom_fusion
  19.3 42.3 %all-gather.3.cloned.1.call-done = bf16[2,2048,512]{2,1,0:T(8,128)(2,1)} async-done(((bf16[2,128,512]{2,1,0:T(8,128)(2,1)}), bf16[2,2048,512]{2,1,0:T(8,128)(2,1)}) %all-gather.3.cloned.1.call-update) | async-done | bytes 4194320 | tf_op jit(solution)/shard_map/all_gather | solution.py:68
  61.5 3.9 fusion.46
  65.4 4.0 squeeze.13
  69.4 2.1 squeeze.14
  71.6 39.0 %while.15 = (s32[]{:T(128)}, f32[80,4,8]{0,2,1:T(8,128)S(1)}, f32[80,4,8]{0,2,1:T(8,128)S(1)}, f32[80,4,8,128]{3,0,2,1:T(8,128)S(1)}, bf16[4,512,4,128]{3,2,1,0:...) while((s32[]{:T(128)}, f32[80,4,8]{0,2,1:T(8,128)S(1)}, ...), condition=%wide.region_3.4_spmd.clone, body=%wide.region_0.3_spmd.clone.sunk | while | flops 682237440 | bytes 43286664 | solution.py:74
  71.6 1.7 constant_dynamic-slice_fusion.3
  73.3 0.9 bitcast_reduce_fusion.2
  74.3 2.3 copy-done
  76.6 1.5 fusion.59
  78.1 3.3 fusion.61
  81.5 1.6 constant_dynamic-slice_fusion.3
  83.0 0.9 bitcast_reduce_fusion.2
  84.0 2.3 copy-done
  86.3 1.5 fusion.59
  87.8 3.4 fusion.61
  91.2 1.6 constant_dynamic-slice_fusion.3
  92.8 0.9 bitcast_reduce_fusion.2
  93.8 2.3 copy-done
  96.1 1.5 fusion.59
  97.6 3.3 fusion.61
  101.0 1.6 constant_dynamic-slice_fusion.3
  102.5 0.9 bitcast_reduce_fusion.2
  103.5 2.3 copy-done
  105.8 1.5 fusion.59
  107.3 3.3 fusion.61
  110.7 0.4 divide_convert_fusion
  111.3 75.9 %all-gather.5.cloned.1.call-done = bf16[4096,2048]{1,0:T(8,128)(2,1)} async-done(((bf16[256,2048]{1,0:T(8,128)(2,1)}), bf16[4096,2048]{1,0:T(8,128)(2,1)}) %all-gather.5.cloned.1.call-update) | async-done | bytes 16777232 | tf_op jit(solution)/shard_map/all_gather | solution.py:83
  187.2 8.9 %fusion.31 = (f32[80]{0:T(128)S(1)}, bf16[80,2048]{1,0:T(8,128)(2,1)S(1)}) fusion(bf16[4096,2048]{1,0:T(8,128)(2,1)} %all-gather.5.cloned.1.call-done, bf16[10,8,32,128]{3,2,1,0:T(8,128)(2,1)S(1)} %bitcast.103, bf16[80,2048]{1,0:T(8,128)(2,1)S(1)} %copy-done.2), kind=kOutput, calls=%fused_computation.40 | convolution fusion | flops 1343160192 | bytes 18088256 | tf_op jit(solution)/shard_map/dot_general | solution.py:81
  196.2 5.9 %gather_fusion = bf16[960,2048]{1,0:T(8,128)(2,1)} fusion(bf16[80,2048]{1,0:T(8,128)(2,1)S(1)} %fusion.33, s32[1024]{0:T(1024)S(1)} %pad_clamp_fusion.1), kind=kCustom, calls=%fused_computation | custom fusion | bytes 7868160 | tf_op jit(solution)/shard_map/gather | solution.py:110
  202.1 5.0 %gather.9 = bf16[32,30,2048]{2,1,0:T(8,128)(2,1)} reshape(bf16[960,2048]{1,0:T(8,128)(2,1)} %gather_fusion) | data formatting | bytes 7864320 | tf_op jit(solution)/shard_map/gather | solution.py:110
  207.2 2.5 broadcast_select_fusion
  209.7 98.4 %all_to_all.10 = bf16[32,30,2048]{2,1,0:T(8,128)(2,1)S(1)} all-to-all(bf16[32,30,2048]{2,1,0:T(8,128)(2,1)S(1)} %broadcast_select_fusion), channel_id=1, replica_groups=mesh['groups'=2,'ctx'=16] {'ctx'}, dimensions={0} | all-to-all | bytes 7864320 | tf_op jit(solution)/shard_map/all_to_all | solution.py:113
  308.1 9.5 %fusion.21 = f32[16,2,30,1536]{3,2,0,1:T(8,128)S(1)} fusion(bf16[2,2048,1536]{2,1,0:T(8,128)(2,1)} %param.19, bf16[16,2,30,2048]{3,2,1,0:T(8,128)(2,1)S(1)} %bitcast.102), kind=kOutput, calls=%fused_computation.28 | convolution fusion | flops 6039797760 | bytes 22413312 | tf_op jit(solution)/shard_map/nemd,edf->nemf/dot_general | solution.py:116
  317.6 3.8 convert_bitcast_fusion
  321.4 2.3 copy.62
  323.7 5.3 %all-to-all-start.1 = ((bf16[32,30,2048]{2,1,0:T(8,128)(2,1)}), bf16[32,30,2048]{2,1,0:T(8,128)(2,1)}, u32[]{:S(2)}, u32[]{:S(2)}) async-start(bf16[32,30,2048]{2,1,0:T(8,128)(2,1)} %bitcast.101), calls=%async_computation.1 | async-start | bytes 8388608 | tf_op jit(solution)/shard_map/all_to_all | solution.py:121
  329.2 92.3 %all-to-all-done.1 = bf16[32,30,2048]{2,1,0:T(8,128)(2,1)} async-done(((bf16[32,30,2048]{2,1,0:T(8,128)(2,1)}), bf16[32,30,2048]{2,1,0:T(8,128)(2,1)}, u32[]{:S(2)}, u32[]{:S(2)}) %all-to-all-start.1) | async-done | bytes 3932192 | tf_op jit(solution)/shard_map/all_to_all | solution.py:121
  421.5 5.0 %reshape.108 = bf16[960,2048]{1,0:T(8,128)(2,1)} reshape(bf16[32,30,2048]{2,1,0:T(8,128)(2,1)} %all-to-all-done.1) | data formatting | bytes 7864320 | tf_op jit(solution)/shard_map/reshape | solution.py:125
  426.5 9.0 %gather_fusion.1 = bf16[640,2048]{1,0:T(8,128)(2,1)S(1)} fusion(bf16[960,2048]{1,0:T(8,128)(2,1)} %reshape.108, s32[1024]{0:T(1024)S(1)} %pad_clamp_fusion), kind=kCustom, calls=%fused_computation.1 | custom fusion | bytes 5245440 | tf_op jit(solution)/shard_map/gather | solution.py:125
  435.5 2.9 fusion.20
  (62 shorter events, 2.2 us)
Async XLA Ops:
  7.2 54.4 %all-gather.3.cloned.1.call-start = ((), (), s32[]{:S(2)}) async-start(), calls=%async_computation.2 | async-start | bytes 4456448 | tf_op jit(solution)/shard_map/all_gather | solution.py:68
  7.9 179.3 %all-gather.5.cloned.1.call-start = ((), (), s32[]{:S(2)}) async-start(), calls=%async_computation.3 | async-start | bytes 17825792 | tf_op jit(solution)/shard_map/all_gather | solution.py:83
  71.6 115.6 %copy-start.2 = (bf16[80,2048]{1,0:T(8,128)(2,1)S(1)}, bf16[80,2048]{1,0:T(8,128)(2,1)}, u32[]{:S(2)}) copy-start(bf16[80,2048]{1,0:T(8,128)(2,1)} %param.16) | copy-start | bytes 983044
  74.3 2.3 copy-start
  84.0 2.3 copy-start
  93.7 2.3 copy-start
  103.5 2.3 copy-start
  187.2 8.9 %copy-start.4 = (f32[2048]{0:T(1024)S(1)}, f32[2048]{0:T(1024)}, u32[]{:S(2)}) copy-start(f32[2048]{0:T(1024)} %param.17) | copy-start | bytes 24580
  196.0 6.1 %copy-start.1 = (bf16[80,2048]{1,0:T(8,128)(2,1)}, bf16[80,2048]{1,0:T(8,128)(2,1)S(1)}, u32[]{:S(2)}) copy-start(bf16[80,2048]{1,0:T(8,128)(2,1)S(1)} %get-tuple-element.112) | copy-start | bytes 983044
  209.7 107.9 %slice-start = ((s8[6291456]{0:T(1024)(128)(4,1)}), s8[4194304]{0:T(1024)(128)(4,1)S(1)}, s32[]{:S(2)}) async-start(s8[6291456]{0:T(1024)(128)(4,1)} %bitcast.108), calls=%async_computation.4 | async-start | bytes 8388608
  308.1 9.5 %slice-start.1 = ((s8[6291456]{0:T(1024)(128)(4,1)}), s8[2097152]{0:T(1024)(128)(4,1)S(1)}, s32[]{:S(2)}) async-start(s8[6291456]{0:T(1024)(128)(4,1)} %bitcast.108), calls=%async_computation.5 | async-start | bytes 4194304
  323.7 5.3 %copy-start.3 = (f32[80,8]{0,1:T(8,128)S(1)}, f32[80,8]{0,1:T(8,128)}, u32[]{:S(2)}) copy-start(f32[80,8]{0,1:T(8,128)} %param.22) | copy-start | bytes 7684
  323.7 97.8 %all-to-all-start.1 = ((bf16[32,30,2048]{2,1,0:T(8,128)(2,1)}), bf16[32,30,2048]{2,1,0:T(8,128)(2,1)}, u32[]{:S(2)}, u32[]{:S(2)}) async-start(bf16[32,30,2048]{2,1,0:T(8,128)(2,1)} %bitcast.101), calls=%async_computation.1 | async-start | bytes 8388608 | tf_op jit(solution)/shard_map/all_to_all | solution.py:121
Sparse Core Ops, SparseCore 0:
  10.2 51.2 all-gather.2
  63.7 123.4 all-gather.4
where the time goes:
time: 446 us; the launch traced here: 445 us
  waiting for transfers between devices  212 us (48%)
  blocking collectives  98.4 us (22%)
  local copies, waits for them, and re-layouts  59.7 us (13%)
  matrix products  39.7 us (9%)
  other arithmetic  15.5 us (3%)
  between operations  14.3 us (3%)
  starting transfers between devices  5.41 us (1%)
    all_to_all x1, blocking collectives, local(): lax.all_to_all(outgoing, 'ctx', split_axis=0, concat_axis=0, tiled=True)  98.4 us
    all_to_all x1, waiting for transfers between devices, local(): lax.all_to_all(produced.reshape(expert_count, capacity, D), 'ctx', split_...  92.3 us
    all_gather x1, waiting for transfers between devices, local(): lax.all_gather(out_proj, 'ctx', axis=0, tiled=True)  75.9 us
    all_gather x1, waiting for transfers between devices, local(): rows_per_shard = lax.all_gather(cache_key_value, 'ctx', axis=1, tiled=True)  42.3 us
    dot_general x4, matrix products, absorb_block(): jnp.einsum('rkgj,jkd->rkgd', weights.astype(jnp.bfloat16), block_values,...  13.4 us
    gather x2, local copies, waits for them, and re-layouts, local(): normed[source_rows]  10.9 us
    dot_general x1, matrix products, local(): jnp.einsum('nemd,edf->nemf', grouped, w_gate_up, preferred_element_type=j...  9.46 us
    while x12, local copies, waits for them, and re-layouts  9.2 us
  transfers between devices with their start and end apart: 3, of which 3 were waited for; matrix products, arithmetic and copies ran while one was open for 11% of the time, Pallas kernels for 0%

commit v1 on v0

v1 whole, which is shorter than its diff:
```python
import functools
import math

import jax
import jax.numpy as jnp
from jax import lax
from jax.experimental import pallas as pl
from jax.experimental.pallas import tpu as pltpu
from jax.sharding import PartitionSpec as P

KEY_VALUE_HEADS = 4
HEAD_SIZE = 128
LANES = 128
EPSILON = 1e-06
MIB = 1 << 20


def rotation(inner, by):
    n = KEY_VALUE_HEADS
    return [(o * inner + t, ((o + by) % n) * inner + t) for o in range(n) for t in range(inner)]


def swap(inner, bit):
    return [
        (o * inner + t, o * inner + (t ^ bit)) for o in range(KEY_VALUE_HEADS) for t in range(inner)
    ]


def gather_inner(array, inner):
    pieces = {0: array}
    bit = inner // 2
    while bit:
        for j in list(pieces):
            pieces[j | bit] = lax.ppermute(pieces[j], "ctx", swap(inner, bit))
        bit //= 2
    return [pieces[j] for j in range(inner)]


def pack_kernel(inner, spot, queries, fresh, cache, ids, weights, placement, *outs):
    outer, place = spot[0], spot[1]
    rows = queries.shape[0]
    keys = cache.shape[1]
    group = queries.shape[1] // (KEY_VALUE_HEADS * HEAD_SIZE)
    per_device = group // inner
    experts = placement.shape[1]
    part = experts // KEY_VALUE_HEADS
    share = weights[...] / jnp.sum(weights[...], axis=-1, keepdims=True)
    expert = lax.broadcasted_iota(jnp.int32, (rows, experts), 1)
    gates = jnp.zeros((rows, experts), jnp.float32)
    for k in range(ids.shape[1]):
        gates += jnp.where(ids[:, k : k + 1] == expert, share[:, k : k + 1], 0.0)
    high = gates.astype(jnp.bfloat16)
    low = (gates - high.astype(jnp.float32)).astype(jnp.bfloat16)
    lane = lax.broadcasted_iota(jnp.int32, (LANES, experts), 0)
    slot = jnp.broadcast_to(placement[...], (LANES, experts))
    contract = (((1,), (1,)), ((), ()))
    for k in range(KEY_VALUE_HEADS):
        to = lax.rem(outer + k, KEY_VALUE_HEADS)
        kvg, qf = outs[2 * k], outs[2 * k + 1]
        column = pl.ds(pl.multiple_of(to * HEAD_SIZE, HEAD_SIZE), HEAD_SIZE)
        kvg[0:keys, :] = cache[0, :, column]
        kvg[keys : 2 * keys, :] = cache[1, :, column]
        first = to * part
        half = LANES // 2
        pick_high = jnp.where((slot == first + lane) & (lane < part), 1.0, 0.0)
        pick_low = jnp.where((slot == first + lane - half) & (lane >= half) & (lane < half + part), 1.0, 0.0)
        block = lax.dot_general(
            high, pick_high.astype(jnp.bfloat16), contract, preferred_element_type=jnp.float32
        ) + lax.dot_general(
            low, pick_low.astype(jnp.bfloat16), contract, preferred_element_type=jnp.float32
        )
        kvg[2 * keys :, :] = block.astype(jnp.bfloat16)
        for h in range(group):
            head = to * group + (place ^ (h // per_device)) * per_device + h % per_device
            qf[h * rows : (h + 1) * rows, :] = queries[
                :, pl.ds(pl.multiple_of(head * HEAD_SIZE, HEAD_SIZE), HEAD_SIZE)
            ]
        qf[group * rows : (group + 1) * rows, :] = fresh[0, :, column]
        qf[(group + 1) * rows :, :] = fresh[1, :, column]


def merge_kernel(keys, *refs):
    out = refs[-1]
    n = len(refs) - 1
    rows = refs[0].shape[0] - 2 * keys
    start = n * rows
    for k in range(n):
        out[k * rows : (k + 1) * rows, :] = refs[k][2 * keys :, :]
        out[start + k * keys : start + (k + 1) * keys, :] = refs[k][:keys, :]
        out[start + (n + k) * keys : start + (n + k + 1) * keys, :] = refs[k][keys : 2 * keys, :]


def attention_kernel(inner, group, rows, block_keys, qf, *refs):
    caches, projections, out = refs[:inner], refs[inner : 2 * inner], refs[2 * inner]
    keys, values, attention = refs[2 * inner + 1 :]
    for j in range(inner):
        start = caches[j].shape[0] - 2 * block_keys
        keys[j * block_keys : (j + 1) * block_keys, :] = caches[j][start : start + block_keys, :]
        values[j * block_keys : (j + 1) * block_keys, :] = caches[j][start + block_keys :, :]
    factor = HEAD_SIZE ** (-0.5) * math.log2(math.e)
    own_key = qf[group * rows : (group + 1) * rows, :].astype(jnp.float32)
    own_value = qf[(group + 1) * rows :, :].astype(jnp.float32)
    step = max(1, group // 2)
    for h0 in range(0, group, step):
        query = qf[h0 * rows : (h0 + step) * rows, :]
        own = (
            jnp.sum(
                query.astype(jnp.float32) * jnp.concatenate([own_key] * step, axis=0),
                axis=-1,
                keepdims=True,
            )
            * factor
        )
        scores = (
            lax.dot_general(
                query, keys[...], (((1,), (1,)), ((), ())), preferred_element_type=jnp.float32
            )
            * factor
        )
        peak = jnp.maximum(own, jnp.max(scores, axis=-1, keepdims=True))
        weights = jnp.exp2(scores - peak)
        own = jnp.exp2(own - peak)
        totals = jnp.sum(weights, axis=-1, keepdims=True) + own
        weighted = jnp.dot(
            weights.astype(jnp.bfloat16), values[...], preferred_element_type=jnp.float32
        )
        weighted = weighted + own * jnp.concatenate([own_value] * step, axis=0)
        result = (weighted / totals).astype(jnp.bfloat16)
        for h in range(step):
            attention[:, (h0 + h) * HEAD_SIZE : (h0 + h + 1) * HEAD_SIZE] = result[
                h * rows : (h + 1) * rows, :
            ]
    depth = projections[0].shape[0]
    total = jnp.zeros(out.shape, jnp.float32)
    for j in range(inner):
        total += jnp.dot(
            attention[:, j * depth : (j + 1) * depth],
            projections[j][...],
            preferred_element_type=jnp.float32,
        )
    out[...] = total.astype(out.dtype)


def norm_kernel(residual, gain, own, *refs):
    arrived, (hidden, normed) = refs[:-2], refs[-2:]
    total = own[...]
    for ref in arrived:
        total = total + ref[...].astype(jnp.float32)
    rounded = (residual[...].astype(jnp.float32) + total).astype(jnp.bfloat16)
    hidden[...] = rounded
    wide = rounded.astype(jnp.float32)
    scale = lax.rsqrt(jnp.mean(wide * wide, axis=-1, keepdims=True) + EPSILON)
    normed[...] = (wide * scale * gain[...]).astype(jnp.bfloat16)


def expert_kernel(inner, local, spot, *refs):
    pieces, gates = refs[:inner], refs[inner : 2 * inner]
    gate, up, down, keep, send, total, stacked = refs[2 * inner :]
    expert, tile = pl.program_id(0), pl.program_id(1)
    rows = pieces[0].shape[0]
    order = halves(inner)

    @pl.when((expert == 0) & (tile == 0))
    def first():
        for at, j in enumerate(order):
            stacked[at * rows : (at + 1) * rows, :] = pieces[j][...]
        total[...] = jnp.zeros_like(total)

    lane = lax.broadcasted_iota(jnp.int32, (rows, LANES), 1)
    column = spot[1] * local + expert
    mine = (lane == column) | (lane == column + LANES // 2)
    share = jnp.concatenate(
        [
            jnp.sum(
                jnp.where(mine, gates[j][...].astype(jnp.float32), 0.0), axis=-1, keepdims=True
            )
            for j in order
        ],
        axis=0,
    )
    rows_in = stacked[...]
    left = jnp.dot(rows_in, gate[0], preferred_element_type=jnp.float32)
    right = jnp.dot(rows_in, up[0], preferred_element_type=jnp.float32)
    active = (left / (1.0 + jnp.exp(-left)) * right * share).astype(jnp.bfloat16)
    total[...] += jnp.dot(active, down[0], preferred_element_type=jnp.float32)

    @pl.when((expert == pl.num_programs(0) - 1) & (tile == pl.num_programs(1) - 1))
    def last():
        half = keep.shape[0]
        keep[...] = total[:half, :].astype(keep.dtype)
        send[...] = total[half:, :].astype(send.dtype)


def halves(inner):
    order, bit = [0], inner // 2
    while bit:
        order = order + [j | bit for j in order]
        bit //= 2
    return order


def whole(shape):
    return pl.BlockSpec(shape, lambda *_: (0,) * len(shape))


def vmem(count):
    return [pl.BlockSpec(memory_space=pltpu.VMEM)] * count


def local_program(
    n,
    queries,
    fresh,
    cache,
    residual,
    gain,
    out_proj,
    w_gate_up,
    w_down,
    route_ids,
    route_weights,
    placement,
):
    bf16, f32 = jnp.bfloat16, jnp.float32
    outers = KEY_VALUE_HEADS
    inner = n // outers
    rows, width = residual.shape
    keys = cache.shape[1]
    group = queries.shape[1] // (outers * HEAD_SIZE)
    local, _, both = w_gate_up.shape
    ff = both // 2
    me = lax.axis_index("ctx")
    spot = jnp.stack([me // inner, me % inner]).astype(jnp.int32)
    smem = pl.BlockSpec(memory_space=pltpu.SMEM)

    def params(limit):
        return pltpu.CompilerParams(vmem_limit_bytes=limit * MIB)

    kvg_rows, qf_rows = 2 * keys + rows, (group + 2) * rows
    packed = pl.pallas_call(
        functools.partial(pack_kernel, inner),
        out_shape=[
            jax.ShapeDtypeStruct((size, HEAD_SIZE), bf16)
            for _ in range(outers)
            for size in (kvg_rows, qf_rows)
        ],
        in_specs=[smem] + vmem(6),
        out_specs=vmem(2 * outers),
        compiler_params=params(16),
        name="pack",
    )(spot, queries, fresh, cache, route_ids, route_weights, placement.reshape(1, -1))
    projections = gather_inner(out_proj, inner)
    kvg = [packed[0]] + [
        lax.ppermute(packed[2 * k], "ctx", rotation(inner, k)) for k in range(1, outers)
    ]
    qf = [packed[1]] + [
        lax.ppermute(packed[2 * k + 1], "ctx", rotation(inner, k)) for k in range(1, outers)
    ]
    merged = pl.pallas_call(
        functools.partial(merge_kernel, keys),
        out_shape=jax.ShapeDtypeStruct((outers * kvg_rows, HEAD_SIZE), bf16),
        in_specs=vmem(outers),
        out_specs=pl.BlockSpec(memory_space=pltpu.VMEM),
        name="merge",
    )(*kvg)
    caches = gather_inner(merged, inner)

    def attend(k):
        return pl.pallas_call(
            functools.partial(attention_kernel, inner, group, rows, outers * keys),
            out_shape=jax.ShapeDtypeStruct((rows, width), f32 if k == 0 else bf16),
            in_specs=vmem(1 + 2 * inner),
            out_specs=pl.BlockSpec(memory_space=pltpu.VMEM),
            scratch_shapes=[
                pltpu.VMEM((n * keys, HEAD_SIZE), bf16),
                pltpu.VMEM((n * keys, HEAD_SIZE), bf16),
                pltpu.VMEM((rows, group * HEAD_SIZE), bf16),
            ],
            compiler_params=params(40),
            cost_estimate=pl.CostEstimate(
                flops=4 * group * rows * n * keys * HEAD_SIZE
                + 2 * rows * group * HEAD_SIZE * width,
                bytes_accessed=6 * MIB,
                transcendentals=group * rows * n * keys,
            ),
            name="attention",
        )(qf[k], *caches, *projections)

    home = [
        lax.ppermute(attend(k), "ctx", rotation(inner, -k)) if k else attend(k)
        for k in [*range(1, outers), 0]
    ]
    hidden, normed = pl.pallas_call(
        norm_kernel,
        out_shape=[jax.ShapeDtypeStruct((rows, width), bf16)] * 2,
        in_specs=vmem(2 + outers),
        out_specs=vmem(2),
        compiler_params=params(16),
        name="norm",
    )(residual, gain.reshape(1, -1), home[-1], *home[:-1])

    tile = 256 if ff % 256 == 0 else ff
    tiles = ff // tile
    half = rows * inner // 2

    def experts(k, pieces):
        return pl.pallas_call(
            functools.partial(expert_kernel, inner, local),
            grid=(local, tiles),
            out_shape=[jax.ShapeDtypeStruct((half, width), bf16)] * 2,
            in_specs=[smem]
            + [whole((rows, width))] * inner
            + [pl.BlockSpec((rows, LANES), lambda *_: (k, 0))] * inner
            + [
                pl.BlockSpec((1, width, tile), lambda e, f: (e, 0, f)),
                pl.BlockSpec((1, width, tile), lambda e, f: (e, 0, f + tiles)),
                pl.BlockSpec((1, tile, width), lambda e, f: (e, f, 0)),
            ],
            out_specs=[whole((half, width))] * 2,
            scratch_shapes=[
                pltpu.VMEM((rows * inner, width), f32),
                pltpu.VMEM((rows * inner, width), bf16),
            ],
            compiler_params=params(48),
            cost_estimate=pl.CostEstimate(
                flops=6 * rows * inner * width * ff * local,
                bytes_accessed=6 * width * ff * local,
                transcendentals=rows * inner * ff * local,
            ),
            name="experts",
        )(spot, *pieces, *caches, w_gate_up, w_gate_up, w_down)

    def reduce_inner(keep, send):
        bit = 1
        while True:
            arrived = lax.ppermute(send, "ctx", swap(inner, bit))
            total = keep.astype(f32) + arrived.astype(f32)
            bit *= 2
            if bit == inner:
                return total
            middle = total.shape[0] // 2
            keep, send = total[:middle], total[middle:].astype(bf16)

    result = None
    order = [0] + list(range(1, outers))
    sources = [normed] + [
        lax.ppermute(normed, "ctx", rotation(inner, k)) for k in range(1, outers)
    ]
    for k in order:
        keep, send = experts(k, gather_inner(sources[k], inner))
        total = reduce_inner(keep, send)
        if k:
            total = lax.ppermute(total.astype(bf16), "ctx", rotation(inner, -k)).astype(f32)
        result = total if result is None else result + total
    return hidden, result.astype(bf16)


def solution(mesh):
    rows = P(("groups", "ctx"), None)
    middle = P(None, ("groups", "ctx"), None)
    in_specs = (
        rows,
        middle,
        middle,
        rows,
        P(),
        P("ctx", None),
        P("ctx", None, None),
        P("ctx", None, None),
        rows,
        rows,
        P(),
    )
    return jax.shard_map(
        functools.partial(local_program, mesh.shape["ctx"]),
        mesh=mesh,
        in_specs=in_specs,
        out_specs=(rows, rows),
        check_vma=False,
    )
```

time: 446 us -> 255 us (0.57)
  the two profiles are of different devices: /device:TPU:13 before, /device:TPU:0 now
where the time goes in v1:
time: 255 us
  waiting for transfers between devices  120 us (47%)
  Pallas kernels  69.7 us (27%)
  starting transfers between devices  52.3 us (21%)
  local copies, waits for them, and re-layouts  9.65 us (4%)
    pallas_call x4, Pallas kernels, experts(): pl.pallas_call(functools.partial(expert_kernel, inner, local), grid=(loca...  46.9 us
    ppermute x18, waiting for transfers between devices, gather_inner(): pieces[j | bit] = lax.ppermute(pieces[j], 'ctx', swap(inner, bit))  34.5 us
    ppermute x3, waiting for transfers between devices, local_program(): lax.ppermute(packed[2 * k + 1], 'ctx', rotation(inner, k))  25.4 us
    pallas_call x4, Pallas kernels, attend(): pl.pallas_call(functools.partial(attention_kernel, inner, group, rows, ou...  18.9 us
    ppermute x3, starting transfers between devices, local_program(): lax.ppermute(total.astype(bf16), 'ctx', rotation(inner, -k)).astype(f32)  18.4 us
    ppermute x3, waiting for transfers between devices, local_program(): lax.ppermute(normed, 'ctx', rotation(inner, k))  18.1 us
    ppermute x3, waiting for transfers between devices, local_program(): lax.ppermute(total.astype(bf16), 'ctx', rotation(inner, -k)).astype(f32)  15.7 us
    ppermute x8, waiting for transfers between devices, reduce_inner(): arrived = lax.ppermute(send, 'ctx', swap(inner, bit))  14.8 us
  transfers between devices with their start and end apart: 41, of which 15 were waited for; matrix products, arithmetic and copies ran while one was open for 1% of the time, Pallas kernels for 27%

profile of v1, /device:TPU:0, one launch (start us, length us, event | category | flops | bytes accessed | tf_op | source)
XLA Modules:
  0.0 254.7 jit_solution(14056859536289317006)
XLA Ops:
  0.6 3.0 %collective-permute-start.7 = (bf16[256,2048]{1,0:T(8,128)(2,1)}, bf16[256,2048]{1,0:T(8,128)(2,1)S(1)}, u32[]{:S(2)}, u32[]{:S(2)}) collective-permute-start(bf16[256,2048]{1,0:T(8,128)(2,1)} %refs_4_.7), channel_id=1, source_target_pairs={{0,2},{1,3},{2,0},{3,1},{4,6},{5,7},{6,4},{7,5},{8,10},{9,11},{10,... | collective-permute-start | bytes 3145736 | tf_op jit(solution)/shard_map/ppermute | solution.py:34
  3.7 23.4 %collective-permute-done.7.refs_6_ = bf16[256,2048]{1,0:T(8,128)(2,1)S(1)} collective-permute-done((bf16[256,2048]{1,0:T(8,128)(2,1)}, bf16[256,2048]{1,0:T(8,128)(2,1)S(1)}, u32[]{:S(2)}, u32[]{:S(2)}) %collective-permute-start.7) | collective-permute-done | bytes 1048608 | tf_op jit(solution)/shard_map/ppermute | solution.py:34
  28.7 1.1 copy-done.3
  29.8 0.9 copy-done.5
  30.7 0.9 copy-done.6
  32.3 1.2 pack.1
  36.2 1.8 collective-permute-start
  37.9 2.6 %collective-permute-start.1 = (bf16[336,128]{1,0:T(8,128)(2,1)S(1)}, bf16[336,128]{1,0:T(8,128)(2,1)S(1)}, u32[]{:S(2)}, u32[]{:S(2)}) collective-permute-start(bf16[336,128]{1,0:T(8,128)(2,1)S(1)} %get-tuple-element.23), channel_id=1, source_target_pairs={{0,8},{1,9},{2,10},{3,11},{4,12},{5,13},{6,14},{7,15},{8,0},{9,1},... | collective-permute-start | bytes 258056 | tf_op jit(solution)/shard_map/ppermute | solution.py:254
  40.5 1.3 collective-permute-start.2
  41.9 1.6 collective-permute-done.refs_1_
  43.5 3.5 %collective-permute-done.1.refs_2_ = bf16[336,128]{1,0:T(8,128)(2,1)S(1)} collective-permute-done((bf16[336,128]{1,0:T(8,128)(2,1)S(1)}, bf16[336,128]{1,0:T(8,128)(2,1)S(1)}, u32[]{:S(2)}, u32[]{:S(2)}) %collective-permute-start.1) | collective-permute-done | bytes 86048 | tf_op jit(solution)/shard_map/ppermute | solution.py:254
  47.6 1.8 merge.1.refs_0_.refs_4_
  49.4 1.5 collective-permute-start.4
  50.9 8.6 %collective-permute-done.4.refs_2_.refs_6_ = bf16[1344,128]{1,0:T(8,128)(2,1)S(1)} collective-permute-done((bf16[1344,128]{1,0:T(8,128)(2,1)}, bf16[1344,128]{1,0:T(8,128)(2,1)S(1)}, u32[]{:S(2)}, u32[]{:S(2)}) %collective-permute-start.4) | collective-permute-done | bytes 344096 | tf_op jit(solution)/shard_map/ppermute | solution.py:34
  59.6 3.2 %collective-permute-start.13 = (bf16[800,128]{1,0:T(8,128)(2,1)}, bf16[800,128]{1,0:T(8,128)(2,1)S(1)}, u32[]{:S(2)}, u32[]{:S(2)}) collective-permute-start(bf16[800,128]{1,0:T(8,128)(2,1)} %copy-done.12), channel_id=1, source_target_pairs={{0,12},{1,13},{2,14},{3,15},{4,0},{5,1},{6,2},{7,3},{8,4},{9,5},{1... | collective-permute-start | bytes 614408 | tf_op jit(solution)/shard_map/ppermute | solution.py:257
  62.8 5.3 %collective-permute-done.13.qf = bf16[800,128]{1,0:T(8,128)(2,1)S(1)} collective-permute-done((bf16[800,128]{1,0:T(8,128)(2,1)}, bf16[800,128]{1,0:T(8,128)(2,1)S(1)}, u32[]{:S(2)}, u32[]{:S(2)}) %collective-permute-start.13) | collective-permute-done | bytes 204832 | tf_op jit(solution)/shard_map/ppermute | solution.py:257
  68.1 1.2 collective-permute-start.11
  69.3 3.5 %collective-permute-start.9 = (bf16[800,128]{1,0:T(8,128)(2,1)}, bf16[800,128]{1,0:T(8,128)(2,1)S(1)}, u32[]{:S(2)}, u32[]{:S(2)}) collective-permute-start(bf16[800,128]{1,0:T(8,128)(2,1)} %copy-done.10), channel_id=1, source_target_pairs={{0,4},{1,5},{2,6},{3,7},{4,8},{5,9},{6,10},{7,11},{8,12},{9,13},{1... | collective-permute-start | bytes 614408 | tf_op jit(solution)/shard_map/ppermute | solution.py:257
  72.8 1.0 copy-done
  73.8 4.7 %attention.7 = bf16[80,2048]{1,0:T(8,128)(2,1)S(1)} custom-call(bf16[800,128]{1,0:T(8,128)(2,1)S(1)} %collective-permute-done.13.qf, bf16[1344,128]{1,0:T(8,128)(2,1)S(1)} %copy-done, bf16[1344,128]{1,0:T(8,128)(2,1)S(1)} %collective-permute-done.3.refs_1_.refs_5_, bf16[1344,128]{1,0:T(8,128)(2,1)S(1)} %collective-permute-done.4.refs_2_.refs_6_, ...), custom_call_target="tpu_custom_call" | custom-call | flops 1006632960 | bytes 6291456 | tf_op jit(solution)/shard_map/attention/pallas_call | solution.py:269
  78.6 20.1 %collective-permute-done.11.qf = bf16[800,128]{1,0:T(8,128)(2,1)S(1)} collective-permute-done((bf16[800,128]{1,0:T(8,128)(2,1)}, bf16[800,128]{1,0:T(8,128)(2,1)S(1)}, u32[]{:S(2)}, u32[]{:S(2)}) %collective-permute-start.11) | collective-permute-done | bytes 204832 | tf_op jit(solution)/shard_map/ppermute | solution.py:257
  98.7 4.7 %attention.6 = bf16[80,2048]{1,0:T(8,128)(2,1)S(1)} custom-call(bf16[800,128]{1,0:T(8,128)(2,1)S(1)} %collective-permute-done.11.qf, bf16[1344,128]{1,0:T(8,128)(2,1)S(1)} %copy-done, bf16[1344,128]{1,0:T(8,128)(2,1)S(1)} %collective-permute-done.3.refs_1_.refs_5_, bf16[1344,128]{1,0:T(8,128)(2,1)S(1)} %collective-permute-done.4.refs_2_.refs_6_, ...), custom_call_target="tpu_custom_call" | custom-call | flops 1006632960 | bytes 6291456 | tf_op jit(solution)/shard_map/attention/pallas_call | solution.py:269
  103.6 4.7 %attention.5 = bf16[80,2048]{1,0:T(8,128)(2,1)S(1)} custom-call(bf16[800,128]{1,0:T(8,128)(2,1)S(1)} %collective-permute-done.9.qf, bf16[1344,128]{1,0:T(8,128)(2,1)S(1)} %copy-done, bf16[1344,128]{1,0:T(8,128)(2,1)S(1)} %collective-permute-done.3.refs_1_.refs_5_, bf16[1344,128]{1,0:T(8,128)(2,1)S(1)} %collective-permute-done.4.refs_2_.refs_6_, ...), custom_call_target="tpu_custom_call" | custom-call | flops 1006632960 | bytes 6291456 | tf_op jit(solution)/shard_map/attention/pallas_call | solution.py:269
  108.6 4.7 %attention.4.own = f32[80,2048]{1,0:T(8,128)S(1)} custom-call(bf16[800,128]{1,0:T(8,128)(2,1)S(1)} %get-tuple-element.20.qf, bf16[1344,128]{1,0:T(8,128)(2,1)S(1)} %copy-done.1, bf16[1344,128]{1,0:T(8,128)(2,1)S(1)} %collective-permute-done.3.refs_1_.refs_5_, bf16[1344,128]{1,0:T(8,128)(2,1)S(1)} %collective-permute-done.4.refs_2_.refs_6_, ...), custom_call_target="tpu_custom_call" | custom-call | flops 1006632960 | bytes 6291456 | tf_op jit(solution)/shard_map/attention/pallas_call | solution.py:269
  113.4 1.6 collective-permute-done.12.refs_1_
  114.9 5.0 %collective-permute-done.10.refs_0_ = bf16[80,2048]{1,0:T(8,128)(2,1)S(1)} collective-permute-done((bf16[80,2048]{1,0:T(8,128)(2,1)S(1)}, bf16[80,2048]{1,0:T(8,128)(2,1)S(1)}, u32[]{:S(2)}, u32[]{:S(2)}) %collective-permute-start.10) | collective-permute-done | bytes 327712 | tf_op jit(solution)/shard_map/ppermute | solution.py:290
  119.9 0.9 norm.1
  121.4 1.5 collective-permute-start.16
  123.0 1.2 collective-permute-start.27
  124.2 2.1 collective-permute-start.34
  126.3 7.2 %collective-permute-done.20.refs_0_ = bf16[80,2048]{1,0:T(8,128)(2,1)S(1)} collective-permute-done((bf16[80,2048]{1,0:T(8,128)(2,1)S(1)}, bf16[80,2048]{1,0:T(8,128)(2,1)S(1)}, u32[]{:S(2)}, u32[]{:S(2)}) %collective-permute-start.20) | collective-permute-done | bytes 327712 | tf_op jit(solution)/shard_map/ppermute | solution.py:347
  133.5 1.5 collective-permute-start.22
  135.0 10.9 %collective-permute-done.27.refs_0_ = bf16[80,2048]{1,0:T(8,128)(2,1)S(1)} collective-permute-done((bf16[80,2048]{1,0:T(8,128)(2,1)S(1)}, bf16[80,2048]{1,0:T(8,128)(2,1)S(1)}, u32[]{:S(2)}, u32[]{:S(2)}) %collective-permute-start.27) | collective-permute-done | bytes 327712 | tf_op jit(solution)/shard_map/ppermute | solution.py:347
  145.9 1.6 collective-permute-start.29
  148.2 11.7 %experts.4 = (bf16[160,2048]{1,0:T(8,128)(2,1)S(1)}, bf16[160,2048]{1,0:T(8,128)(2,1)S(1)}) custom-call(s32[2]{0:T(128)S(1)} %pad_add_fusion.spot, bf16[80,2048]{1,0:T(8,128)(2,1)S(1)} %get-tuple-element.29.refs_0_, bf16[80,2048]{1,0:T(8,128)(2,1)S(1)} %collective-permute-done.15.refs_1_, bf16[80,2048]{1,0:T(8,128)(2,1)S(1)} %collective-permute-done.16.refs_2_, ...), custom_call_target="tpu_custom_call" | custom-call | flops 6039797760 | bytes 18874368 | tf_op jit(solution)/shard_map/experts/pallas_call | solution.py:307
  160.6 2.5 collective-permute-done.36.refs_2_
  163.6 11.7 %experts.5 = (bf16[160,2048]{1,0:T(8,128)(2,1)S(1)}, bf16[160,2048]{1,0:T(8,128)(2,1)S(1)}) custom-call(s32[2]{0:T(128)S(1)} %pad_add_fusion.spot, bf16[80,2048]{1,0:T(8,128)(2,1)S(1)} %collective-permute-done.20.refs_0_, bf16[80,2048]{1,0:T(8,128)(2,1)S(1)} %collective-permute-done.21.refs_1_, bf16[80,2048]{1,0:T(8,128)(2,1)S(1)} %collective-permute-done.22.refs_2_, ...), custom_call_target="tpu_custom_call" | custom-call | flops 6039797760 | bytes 18874368 | tf_op jit(solution)/shard_map/experts/pallas_call | solution.py:307
  175.4 11.7 %experts.6 = (bf16[160,2048]{1,0:T(8,128)(2,1)S(1)}, bf16[160,2048]{1,0:T(8,128)(2,1)S(1)}) custom-call(s32[2]{0:T(128)S(1)} %pad_add_fusion.spot, bf16[80,2048]{1,0:T(8,128)(2,1)S(1)} %collective-permute-done.27.refs_0_, bf16[80,2048]{1,0:T(8,128)(2,1)S(1)} %collective-permute-done.28.refs_1_, bf16[80,2048]{1,0:T(8,128)(2,1)S(1)} %collective-permute-done.29.refs_2_, ...), custom_call_target="tpu_custom_call" | custom-call | flops 6039797760 | bytes 18874368 | tf_op jit(solution)/shard_map/experts/pallas_call | solution.py:307
  187.7 11.7 %experts.7 = (bf16[160,2048]{1,0:T(8,128)(2,1)S(1)}, bf16[160,2048]{1,0:T(8,128)(2,1)S(1)}) custom-call(s32[2]{0:T(128)S(1)} %pad_add_fusion.spot, bf16[80,2048]{1,0:T(8,128)(2,1)S(1)} %collective-permute-done.34.refs_0_, bf16[80,2048]{1,0:T(8,128)(2,1)S(1)} %collective-permute-done.35.refs_1_, bf16[80,2048]{1,0:T(8,128)(2,1)S(1)} %collective-permute-done.36.refs_2_, ...), custom_call_target="tpu_custom_call" | custom-call | flops 6039797760 | bytes 18874368 | tf_op jit(solution)/shard_map/experts/pallas_call | solution.py:307
  199.7 1.7 collective-permute-start.19
  202.3 1.7 collective-permute-start.32
  204.7 12.6 %collective-permute-done.25 = bf16[80,2048]{1,0:T(8,128)(2,1)S(1)} collective-permute-done((bf16[80,2048]{1,0:T(8,128)(2,1)S(1)}, bf16[80,2048]{1,0:T(8,128)(2,1)S(1)}, u32[]{:S(2)}, u32[]{:S(2)}) %collective-permute-start.25) | collective-permute-done | bytes 327712 | tf_op jit(solution)/shard_map/ppermute | solution.py:336
  217.4 5.3 %collective-permute-start.26 = (bf16[80,2048]{1,0:T(8,128)(2,1)S(1)}, bf16[80,2048]{1,0:T(8,128)(2,1)S(1)}, u32[]{:S(2)}, u32[]{:S(2)}) collective-permute-start(bf16[80,2048]{1,0:T(8,128)(2,1)S(1)} %fusion.2), channel_id=1, source_target_pairs={{0,12},{1,13},{2,14},{3,15},{4,0},{5,1},{6,2},{7,3},{8,4},{9,5},{1... | collective-permute-start | bytes 983048 | tf_op jit(solution)/shard_map/ppermute | solution.py:353
  222.7 1.6 collective-permute-done.32
  224.4 6.0 %collective-permute-start.33 = (bf16[80,2048]{1,0:T(8,128)(2,1)S(1)}, bf16[80,2048]{1,0:T(8,128)(2,1)S(1)}, u32[]{:S(2)}, u32[]{:S(2)}) collective-permute-start(bf16[80,2048]{1,0:T(8,128)(2,1)S(1)} %fusion.1), channel_id=1, source_target_pairs={{0,8},{1,9},{2,10},{3,11},{4,12},{5,13},{6,14},{7,15},{8,0},{9,1},... | collective-permute-start | bytes 983048 | tf_op jit(solution)/shard_map/ppermute | solution.py:353
  231.0 7.1 %collective-permute-start.40 = (bf16[80,2048]{1,0:T(8,128)(2,1)S(1)}, bf16[80,2048]{1,0:T(8,128)(2,1)S(1)}, u32[]{:S(2)}, u32[]{:S(2)}) collective-permute-start(bf16[80,2048]{1,0:T(8,128)(2,1)S(1)} %fusion), channel_id=1, source_target_pairs={{0,4},{1,5},{2,6},{3,7},{4,8},{5,9},{6,10},{7,11},{8,12},{9,13},{1... | collective-permute-start | bytes 983048 | tf_op jit(solution)/shard_map/ppermute | solution.py:353
  238.1 15.7 %collective-permute-done.33 = bf16[80,2048]{1,0:T(8,128)(2,1)S(1)} collective-permute-done((bf16[80,2048]{1,0:T(8,128)(2,1)S(1)}, bf16[80,2048]{1,0:T(8,128)(2,1)S(1)}, u32[]{:S(2)}, u32[]{:S(2)}) %collective-permute-start.33) | collective-permute-done | bytes 327712 | tf_op jit(solution)/shard_map/ppermute | solution.py:353
  253.8 0.9 fusion.6
  (92 shorter events, 11.5 us)
Async XLA Ops:
  0.6 72.2 %copy-start.2 = (bf16[256,2048]{1,0:T(8,128)(2,1)S(1)}, bf16[256,2048]{1,0:T(8,128)(2,1)}, u32[]{:S(2)}) copy-start(bf16[256,2048]{1,0:T(8,128)(2,1)} %refs_4_.7) | copy-start | bytes 3145732
  0.6 26.4 %collective-permute-start.7 = (bf16[256,2048]{1,0:T(8,128)(2,1)}, bf16[256,2048]{1,0:T(8,128)(2,1)S(1)}, u32[]{:S(2)}, u32[]{:S(2)}) collective-permute-start(bf16[256,2048]{1,0:T(8,128)(2,1)} %refs_4_.7), channel_id=1, source_target_pairs={{0,2},{1,3},{2,0},{3,1},{4,6},{5,7},{6,4},{7,5},{8,10},{9,11},{10,... | collective-permute-start | bytes 3145736 | tf_op jit(solution)/shard_map/ppermute | solution.py:34
  3.7 69.2 %collective-permute-start.6 = (bf16[256,2048]{1,0:T(8,128)(2,1)}, bf16[256,2048]{1,0:T(8,128)(2,1)S(1)}, u32[]{:S(2)}, u32[]{:S(2)}) collective-permute-start(bf16[256,2048]{1,0:T(8,128)(2,1)} %refs_4_.7), channel_id=1, source_target_pairs={{0,1},{1,0},{2,3},{3,2},{4,5},{5,4},{6,7},{7,6},{8,9},{9,8},{10,11... | collective-permute-start | bytes 3145736 | tf_op jit(solution)/shard_map/ppermute | solution.py:34
  27.0 45.8 %collective-permute-start.8 = (bf16[256,2048]{1,0:T(8,128)(2,1)S(1)}, bf16[256,2048]{1,0:T(8,128)(2,1)}, u32[]{:S(2)}, u32[]{:S(2)}) collective-permute-start(bf16[256,2048]{1,0:T(8,128)(2,1)S(1)} %collective-permute-done.7.refs_6_), channel_id=1, source_target_pairs={{0,1},{1,0},{2,3},{3,2},{4,5},{5,4},{6,7},{7,6},{8,9},{9,8},{10,11... | collective-permute-start | bytes 3145736 | tf_op jit(solution)/shard_map/ppermute | solution.py:34
  28.7 1.1 copy-start.3
  36.2 7.3 %collective-permute-start = (bf16[336,128]{1,0:T(8,128)(2,1)S(1)}, bf16[336,128]{1,0:T(8,128)(2,1)S(1)}, u32[]{:S(2)}, u32[]{:S(2)}) collective-permute-start(bf16[336,128]{1,0:T(8,128)(2,1)S(1)} %get-tuple-element.22), channel_id=1, source_target_pairs={{0,4},{1,5},{2,6},{3,7},{4,8},{5,9},{6,10},{7,11},{8,12},{9,13},{1... | collective-permute-start | bytes 258056 | tf_op jit(solution)/shard_map/ppermute | solution.py:254
  37.9 9.0 %collective-permute-start.1 = (bf16[336,128]{1,0:T(8,128)(2,1)S(1)}, bf16[336,128]{1,0:T(8,128)(2,1)S(1)}, u32[]{:S(2)}, u32[]{:S(2)}) collective-permute-start(bf16[336,128]{1,0:T(8,128)(2,1)S(1)} %get-tuple-element.23), channel_id=1, source_target_pairs={{0,8},{1,9},{2,10},{3,11},{4,12},{5,13},{6,14},{7,15},{8,0},{9,1},... | collective-permute-start | bytes 258056 | tf_op jit(solution)/shard_map/ppermute | solution.py:254
  40.5 6.4 %collective-permute-start.2 = (bf16[336,128]{1,0:T(8,128)(2,1)S(1)}, bf16[336,128]{1,0:T(8,128)(2,1)S(1)}, u32[]{:S(2)}, u32[]{:S(2)}) collective-permute-start(bf16[336,128]{1,0:T(8,128)(2,1)S(1)} %get-tuple-element.24), channel_id=1, source_target_pairs={{0,12},{1,13},{2,14},{3,15},{4,0},{5,1},{6,2},{7,3},{8,4},{9,5},{1... | collective-permute-start | bytes 258056 | tf_op jit(solution)/shard_map/ppermute | solution.py:254
  43.5 4.1 %copy-start.13 = (bf16[336,128]{1,0:T(8,128)(2,1)}, bf16[336,128]{1,0:T(8,128)(2,1)S(1)}, u32[]{:S(2)}) copy-start(bf16[336,128]{1,0:T(8,128)(2,1)S(1)} %collective-permute-done.refs_1_) | copy-start | bytes 258052
  49.4 10.2 %collective-permute-start.4 = (bf16[1344,128]{1,0:T(8,128)(2,1)}, bf16[1344,128]{1,0:T(8,128)(2,1)S(1)}, u32[]{:S(2)}, u32[]{:S(2)}) collective-permute-start(bf16[1344,128]{1,0:T(8,128)(2,1)} %merge.1.refs_0_.refs_4_), channel_id=1, source_target_pairs={{0,2},{1,3},{2,0},{3,1},{4,6},{5,7},{6,4},{7,5},{8,10},{9,11},{10,... | collective-permute-start | bytes 1032200 | tf_op jit(solution)/shard_map/ppermute | solution.py:34
  50.9 18.3 %collective-permute-start.3 = (bf16[1344,128]{1,0:T(8,128)(2,1)}, bf16[1344,128]{1,0:T(8,128)(2,1)S(1)}, u32[]{:S(2)}, u32[]{:S(2)}) collective-permute-start(bf16[1344,128]{1,0:T(8,128)(2,1)} %merge.1.refs_0_.refs_4_), channel_id=1, source_target_pairs={{0,1},{1,0},{2,3},{3,2},{4,5},{5,4},{6,7},{7,6},{8,9},{9,8},{10,11... | collective-permute-start | bytes 1032200 | tf_op jit(solution)/shard_map/ppermute | solution.py:34
  59.6 13.2 %collective-permute-start.5 = (bf16[1344,128]{1,0:T(8,128)(2,1)S(1)}, bf16[1344,128]{1,0:T(8,128)(2,1)S(1)}, u32[]{:S(2)}, u32[]{:S(2)}) collective-permute-start(bf16[1344,128]{1,0:T(8,128)(2,1)S(1)} %collective-permute-done.4.refs_2_.refs_6_), channel_id=1, source_target_pairs={{0,1},{1,0},{2,3},{3,2},{4,5},{5,4},{6,7},{7,6},{8,9},{9,8},{10,11... | collective-permute-start | bytes 1032200 | tf_op jit(solution)/shard_map/ppermute | solution.py:34
  59.6 8.5 %collective-permute-start.13 = (bf16[800,128]{1,0:T(8,128)(2,1)}, bf16[800,128]{1,0:T(8,128)(2,1)S(1)}, u32[]{:S(2)}, u32[]{:S(2)}) collective-permute-start(bf16[800,128]{1,0:T(8,128)(2,1)} %copy-done.12), channel_id=1, source_target_pairs={{0,12},{1,13},{2,14},{3,15},{4,0},{5,1},{6,2},{7,3},{8,4},{9,5},{1... | collective-permute-start | bytes 614408 | tf_op jit(solution)/shard_map/ppermute | solution.py:257
  68.1 30.7 %collective-permute-start.11 = (bf16[800,128]{1,0:T(8,128)(2,1)}, bf16[800,128]{1,0:T(8,128)(2,1)S(1)}, u32[]{:S(2)}, u32[]{:S(2)}) collective-permute-start(bf16[800,128]{1,0:T(8,128)(2,1)} %copy-done.11), channel_id=1, source_target_pairs={{0,8},{1,9},{2,10},{3,11},{4,12},{5,13},{6,14},{7,15},{8,0},{9,1},... | collective-permute-start | bytes 614408 | tf_op jit(solution)/shard_map/ppermute | solution.py:257
  69.3 34.3 %collective-permute-start.9 = (bf16[800,128]{1,0:T(8,128)(2,1)}, bf16[800,128]{1,0:T(8,128)(2,1)S(1)}, u32[]{:S(2)}, u32[]{:S(2)}) collective-permute-start(bf16[800,128]{1,0:T(8,128)(2,1)} %copy-done.10), channel_id=1, source_target_pairs={{0,4},{1,5},{2,6},{3,7},{4,8},{5,9},{6,10},{7,11},{8,12},{9,13},{1... | collective-permute-start | bytes 614408 | tf_op jit(solution)/shard_map/ppermute | solution.py:257
  72.8 1.0 copy-start
  78.5 34.8 %collective-permute-start.14 = (bf16[80,2048]{1,0:T(8,128)(2,1)S(1)}, bf16[80,2048]{1,0:T(8,128)(2,1)S(1)}, u32[]{:S(2)}, u32[]{:S(2)}) collective-permute-start(bf16[80,2048]{1,0:T(8,128)(2,1)S(1)} %attention.7), channel_id=1, source_target_pairs={{0,4},{1,5},{2,6},{3,7},{4,8},{5,9},{6,10},{7,11},{8,12},{9,13},{1... | collective-permute-start | bytes 983048 | tf_op jit(solution)/shard_map/ppermute | solution.py:290
  103.5 5.1 %copy-start.1 = (bf16[1344,128]{1,0:T(8,128)(2,1)S(1)}, bf16[1344,128]{1,0:T(8,128)(2,1)}, u32[]{:S(2)}) copy-start(bf16[1344,128]{1,0:T(8,128)(2,1)} %merge.1.refs_0_.refs_4_) | copy-start | bytes 1032196
  103.5 11.4 %collective-permute-start.12 = (bf16[80,2048]{1,0:T(8,128)(2,1)S(1)}, bf16[80,2048]{1,0:T(8,128)(2,1)S(1)}, u32[]{:S(2)}, u32[]{:S(2)}) collective-permute-start(bf16[80,2048]{1,0:T(8,128)(2,1)S(1)} %attention.6), channel_id=1, source_target_pairs={{0,8},{1,9},{2,10},{3,11},{4,12},{5,13},{6,14},{7,15},{8,0},{9,1},... | collective-permute-start | bytes 983048 | tf_op jit(solution)/shard_map/ppermute | solution.py:290
  108.3 11.6 %collective-permute-start.10 = (bf16[80,2048]{1,0:T(8,128)(2,1)S(1)}, bf16[80,2048]{1,0:T(8,128)(2,1)S(1)}, u32[]{:S(2)}, u32[]{:S(2)}) collective-permute-start(bf16[80,2048]{1,0:T(8,128)(2,1)S(1)} %attention.5), channel_id=1, source_target_pairs={{0,12},{1,13},{2,14},{3,15},{4,0},{5,1},{6,2},{7,3},{8,4},{9,5},{1... | collective-permute-start | bytes 983048 | tf_op jit(solution)/shard_map/ppermute | solution.py:290
  108.6 11.4 %copy-start.4 = (bf16[80,2048]{1,0:T(8,128)(2,1)S(1)}, bf16[80,2048]{1,0:T(8,128)(2,1)}, u32[]{:S(2)}) copy-start(bf16[80,2048]{1,0:T(8,128)(2,1)} %residual.1) | copy-start | bytes 983044
  108.6 11.4 %copy-start.8 = (f32[2048]{0:T(1024)S(1)}, f32[2048]{0:T(1024)}, u32[]{:S(2)}) copy-start(f32[2048]{0:T(1024)} %param.15) | copy-start | bytes 24580
  120.9 12.6 %collective-permute-start.20 = (bf16[80,2048]{1,0:T(8,128)(2,1)S(1)}, bf16[80,2048]{1,0:T(8,128)(2,1)S(1)}, u32[]{:S(2)}, u32[]{:S(2)}) collective-permute-start(bf16[80,2048]{1,0:T(8,128)(2,1)S(1)} %get-tuple-element.29.refs_0_), channel_id=1, source_target_pairs={{0,4},{1,5},{2,6},{3,7},{4,8},{5,9},{6,10},{7,11},{8,12},{9,13},{1... | collective-permute-start | bytes 983048 | tf_op jit(solution)/shard_map/ppermute | solution.py:347
  121.4 13.5 %collective-permute-start.16 = (bf16[80,2048]{1,0:T(8,128)(2,1)S(1)}, bf16[80,2048]{1,0:T(8,128)(2,1)S(1)}, u32[]{:S(2)}, u32[]{:S(2)}) collective-permute-start(bf16[80,2048]{1,0:T(8,128)(2,1)S(1)} %get-tuple-element.29.refs_0_), channel_id=1, source_target_pairs={{0,2},{1,3},{2,0},{3,1},{4,6},{5,7},{6,4},{7,5},{8,10},{9,11},{10,... | collective-permute-start | bytes 983048 | tf_op jit(solution)/shard_map/ppermute | solution.py:34
  123.0 22.9 %collective-permute-start.27 = (bf16[80,2048]{1,0:T(8,128)(2,1)S(1)}, bf16[80,2048]{1,0:T(8,128)(2,1)S(1)}, u32[]{:S(2)}, u32[]{:S(2)}) collective-permute-start(bf16[80,2048]{1,0:T(8,128)(2,1)S(1)} %get-tuple-element.29.refs_0_), channel_id=1, source_target_pairs={{0,8},{1,9},{2,10},{3,11},{4,12},{5,13},{6,14},{7,15},{8,0},{9,1},... | collective-permute-start | bytes 983048 | tf_op jit(solution)/shard_map/ppermute | solution.py:347
  124.2 21.7 %collective-permute-start.34 = (bf16[80,2048]{1,0:T(8,128)(2,1)S(1)}, bf16[80,2048]{1,0:T(8,128)(2,1)S(1)}, u32[]{:S(2)}, u32[]{:S(2)}) collective-permute-start(bf16[80,2048]{1,0:T(8,128)(2,1)S(1)} %get-tuple-element.29.refs_0_), channel_id=1, source_target_pairs={{0,12},{1,13},{2,14},{3,15},{4,0},{5,1},{6,2},{7,3},{8,4},{9,5},{1... | collective-permute-start | bytes 983048 | tf_op jit(solution)/shard_map/ppermute | solution.py:347
  126.3 21.3 %collective-permute-start.15 = (bf16[80,2048]{1,0:T(8,128)(2,1)S(1)}, bf16[80,2048]{1,0:T(8,128)(2,1)S(1)}, u32[]{:S(2)}, u32[]{:S(2)}) collective-permute-start(bf16[80,2048]{1,0:T(8,128)(2,1)S(1)} %get-tuple-element.29.refs_0_), channel_id=1, source_target_pairs={{0,1},{1,0},{2,3},{3,2},{4,5},{5,4},{6,7},{7,6},{8,9},{9,8},{10,11... | collective-permute-start | bytes 983048 | tf_op jit(solution)/shard_map/ppermute | solution.py:34
  133.5 14.3 %collective-permute-start.22 = (bf16[80,2048]{1,0:T(8,128)(2,1)S(1)}, bf16[80,2048]{1,0:T(8,128)(2,1)S(1)}, u32[]{:S(2)}, u32[]{:S(2)}) collective-permute-start(bf16[80,2048]{1,0:T(8,128)(2,1)S(1)} %collective-permute-done.20.refs_0_), channel_id=1, source_target_pairs={{0,2},{1,3},{2,0},{3,1},{4,6},{5,7},{6,4},{7,5},{8,10},{9,11},{10,... | collective-permute-start | bytes 983048 | tf_op jit(solution)/shard_map/ppermute | solution.py:34
  135.0 13.2 %collective-permute-start.17 = (bf16[80,2048]{1,0:T(8,128)(2,1)S(1)}, bf16[80,2048]{1,0:T(8,128)(2,1)S(1)}, u32[]{:S(2)}, u32[]{:S(2)}) collective-permute-start(bf16[80,2048]{1,0:T(8,128)(2,1)S(1)} %collective-permute-done.16.refs_2_), channel_id=1, source_target_pairs={{0,1},{1,0},{2,3},{3,2},{4,5},{5,4},{6,7},{7,6},{8,9},{9,8},{10,11... | collective-permute-start | bytes 983048 | tf_op jit(solution)/shard_map/ppermute | solution.py:34
  145.9 14.0 %collective-permute-start.21 = (bf16[80,2048]{1,0:T(8,128)(2,1)S(1)}, bf16[80,2048]{1,0:T(8,128)(2,1)S(1)}, u32[]{:S(2)}, u32[]{:S(2)}) collective-permute-start(bf16[80,2048]{1,0:T(8,128)(2,1)S(1)} %collective-permute-done.20.refs_0_), channel_id=1, source_target_pairs={{0,1},{1,0},{2,3},{3,2},{4,5},{5,4},{6,7},{7,6},{8,9},{9,8},{10,11... | collective-permute-start | bytes 983048 | tf_op jit(solution)/shard_map/ppermute | solution.py:34
  145.9 14.6 %collective-permute-start.29 = (bf16[80,2048]{1,0:T(8,128)(2,1)S(1)}, bf16[80,2048]{1,0:T(8,128)(2,1)S(1)}, u32[]{:S(2)}, u32[]{:S(2)}) collective-permute-start(bf16[80,2048]{1,0:T(8,128)(2,1)S(1)} %collective-permute-done.27.refs_0_), channel_id=1, source_target_pairs={{0,2},{1,3},{2,0},{3,1},{4,6},{5,7},{6,4},{7,5},{8,10},{9,11},{10,... | collective-permute-start | bytes 983048 | tf_op jit(solution)/shard_map/ppermute | solution.py:34
  147.6 27.7 %collective-permute-start.28 = (bf16[80,2048]{1,0:T(8,128)(2,1)S(1)}, bf16[80,2048]{1,0:T(8,128)(2,1)S(1)}, u32[]{:S(2)}, u32[]{:S(2)}) collective-permute-start(bf16[80,2048]{1,0:T(8,128)(2,1)S(1)} %collective-permute-done.27.refs_0_), channel_id=1, source_target_pairs={{0,1},{1,0},{2,3},{3,2},{4,5},{5,4},{6,7},{7,6},{8,9},{9,8},{10,11... | collective-permute-start | bytes 983048 | tf_op jit(solution)/shard_map/ppermute | solution.py:34
  147.8 15.3 %collective-permute-start.36 = (bf16[80,2048]{1,0:T(8,128)(2,1)S(1)}, bf16[80,2048]{1,0:T(8,128)(2,1)S(1)}, u32[]{:S(2)}, u32[]{:S(2)}) collective-permute-start(bf16[80,2048]{1,0:T(8,128)(2,1)S(1)} %collective-permute-done.34.refs_0_), channel_id=1, source_target_pairs={{0,2},{1,3},{2,0},{3,1},{4,6},{5,7},{6,4},{7,5},{8,10},{9,11},{10,... | collective-permute-start | bytes 983048 | tf_op jit(solution)/shard_map/ppermute | solution.py:34
  148.2 14.9 %collective-permute-start.23 = (bf16[80,2048]{1,0:T(8,128)(2,1)S(1)}, bf16[80,2048]{1,0:T(8,128)(2,1)S(1)}, u32[]{:S(2)}, u32[]{:S(2)}) collective-permute-start(bf16[80,2048]{1,0:T(8,128)(2,1)S(1)} %collective-permute-done.22.refs_2_), channel_id=1, source_target_pairs={{0,1},{1,0},{2,3},{3,2},{4,5},{5,4},{6,7},{7,6},{8,9},{9,8},{10,11... | collective-permute-start | bytes 983048 | tf_op jit(solution)/shard_map/ppermute | solution.py:34
  159.9 27.7 %collective-permute-start.35 = (bf16[80,2048]{1,0:T(8,128)(2,1)S(1)}, bf16[80,2048]{1,0:T(8,128)(2,1)S(1)}, u32[]{:S(2)}, u32[]{:S(2)}) collective-permute-start(bf16[80,2048]{1,0:T(8,128)(2,1)S(1)} %collective-permute-done.34.refs_0_), channel_id=1, source_target_pairs={{0,1},{1,0},{2,3},{3,2},{4,5},{5,4},{6,7},{7,6},{8,9},{9,8},{10,11... | collective-permute-start | bytes 983048 | tf_op jit(solution)/shard_map/ppermute | solution.py:34
  160.5 39.0 %collective-permute-start.18 = (bf16[160,2048]{1,0:T(8,128)(2,1)S(1)}, bf16[160,2048]{1,0:T(8,128)(2,1)S(1)}, u32[]{:S(2)}, u32[]{:S(2)}) collective-permute-start(bf16[160,2048]{1,0:T(8,128)(2,1)S(1)} %get-tuple-element.31), channel_id=1, source_target_pairs={{0,1},{1,0},{2,3},{3,2},{4,5},{5,4},{6,7},{7,6},{8,9},{9,8},{10,11... | collective-permute-start | bytes 1966088 | tf_op jit(solution)/shard_map/ppermute | solution.py:336
  163.1 12.3 %collective-permute-start.30 = (bf16[80,2048]{1,0:T(8,128)(2,1)S(1)}, bf16[80,2048]{1,0:T(8,128)(2,1)S(1)}, u32[]{:S(2)}, u32[]{:S(2)}) collective-permute-start(bf16[80,2048]{1,0:T(8,128)(2,1)S(1)} %collective-permute-done.29.refs_2_), channel_id=1, source_target_pairs={{0,1},{1,0},{2,3},{3,2},{4,5},{5,4},{6,7},{7,6},{8,9},{9,8},{10,11... | collective-permute-start | bytes 983048 | tf_op jit(solution)/shard_map/ppermute | solution.py:34
  163.1 24.6 %collective-permute-start.37 = (bf16[80,2048]{1,0:T(8,128)(2,1)S(1)}, bf16[80,2048]{1,0:T(8,128)(2,1)S(1)}, u32[]{:S(2)}, u32[]{:S(2)}) collective-permute-start(bf16[80,2048]{1,0:T(8,128)(2,1)S(1)} %collective-permute-done.36.refs_2_), channel_id=1, source_target_pairs={{0,1},{1,0},{2,3},{3,2},{4,5},{5,4},{6,7},{7,6},{8,9},{9,8},{10,11... | collective-permute-start | bytes 983048 | tf_op jit(solution)/shard_map/ppermute | solution.py:34
  175.3 26.1 %collective-permute-start.24 = (bf16[160,2048]{1,0:T(8,128)(2,1)S(1)}, bf16[160,2048]{1,0:T(8,128)(2,1)S(1)}, u32[]{:S(2)}, u32[]{:S(2)}) collective-permute-start(bf16[160,2048]{1,0:T(8,128)(2,1)S(1)} %get-tuple-element.33), channel_id=1, source_target_pairs={{0,1},{1,0},{2,3},{3,2},{4,5},{5,4},{6,7},{7,6},{8,9},{9,8},{10,11... | collective-permute-start | bytes 1966088 | tf_op jit(solution)/shard_map/ppermute | solution.py:336
  187.1 15.0 %collective-permute-start.31 = (bf16[160,2048]{1,0:T(8,128)(2,1)S(1)}, bf16[160,2048]{1,0:T(8,128)(2,1)S(1)}, u32[]{:S(2)}, u32[]{:S(2)}) collective-permute-start(bf16[160,2048]{1,0:T(8,128)(2,1)S(1)} %get-tuple-element.35), channel_id=1, source_target_pairs={{0,1},{1,0},{2,3},{3,2},{4,5},{5,4},{6,7},{7,6},{8,9},{9,8},{10,11... | collective-permute-start | bytes 1966088 | tf_op jit(solution)/shard_map/ppermute | solution.py:336
  199.4 4.6 %collective-permute-start.38 = (bf16[160,2048]{1,0:T(8,128)(2,1)S(1)}, bf16[160,2048]{1,0:T(8,128)(2,1)S(1)}, u32[]{:S(2)}, u32[]{:S(2)}) collective-permute-start(bf16[160,2048]{1,0:T(8,128)(2,1)S(1)} %get-tuple-element.37), channel_id=1, source_target_pairs={{0,1},{1,0},{2,3},{3,2},{4,5},{5,4},{6,7},{7,6},{8,9},{9,8},{10,11... | collective-permute-start | bytes 1966088 | tf_op jit(solution)/shard_map/ppermute | solution.py:336
  199.7 38.3 %collective-permute-start.19 = (bf16[80,2048]{1,0:T(8,128)(2,1)S(1)}, bf16[80,2048]{1,0:T(8,128)(2,1)S(1)}, u32[]{:S(2)}, u32[]{:S(2)}) collective-permute-start(bf16[80,2048]{1,0:T(8,128)(2,1)S(1)} %slice.69), channel_id=1, source_target_pairs={{0,2},{1,3},{2,0},{3,1},{4,6},{5,7},{6,4},{7,5},{8,10},{9,11},{10,... | collective-permute-start | bytes 983048 | tf_op jit(solution)/shard_map/ppermute | solution.py:336
  201.6 15.7 %collective-permute-start.25 = (bf16[80,2048]{1,0:T(8,128)(2,1)S(1)}, bf16[80,2048]{1,0:T(8,128)(2,1)S(1)}, u32[]{:S(2)}, u32[]{:S(2)}) collective-permute-start(bf16[80,2048]{1,0:T(8,128)(2,1)S(1)} %slice.68), channel_id=1, source_target_pairs={{0,2},{1,3},{2,0},{3,1},{4,6},{5,7},{6,4},{7,5},{8,10},{9,11},{10,... | collective-permute-start | bytes 983048 | tf_op jit(solution)/shard_map/ppermute | solution.py:336
  202.3 22.0 %collective-permute-start.32 = (bf16[80,2048]{1,0:T(8,128)(2,1)S(1)}, bf16[80,2048]{1,0:T(8,128)(2,1)S(1)}, u32[]{:S(2)}, u32[]{:S(2)}) collective-permute-start(bf16[80,2048]{1,0:T(8,128)(2,1)S(1)} %slice.67), channel_id=1, source_target_pairs={{0,2},{1,3},{2,0},{3,1},{4,6},{5,7},{6,4},{7,5},{8,10},{9,11},{10,... | collective-permute-start | bytes 983048 | tf_op jit(solution)/shard_map/ppermute | solution.py:336
  204.2 26.7 %collective-permute-start.39 = (bf16[80,2048]{1,0:T(8,128)(2,1)S(1)}, bf16[80,2048]{1,0:T(8,128)(2,1)S(1)}, u32[]{:S(2)}, u32[]{:S(2)}) collective-permute-start(bf16[80,2048]{1,0:T(8,128)(2,1)S(1)} %slice.66), channel_id=1, source_target_pairs={{0,2},{1,3},{2,0},{3,1},{4,6},{5,7},{6,4},{7,5},{8,10},{9,11},{10,... | collective-permute-start | bytes 983048 | tf_op jit(solution)/shard_map/ppermute | solution.py:336
  217.4 20.7 %collective-permute-start.26 = (bf16[80,2048]{1,0:T(8,128)(2,1)S(1)}, bf16[80,2048]{1,0:T(8,128)(2,1)S(1)}, u32[]{:S(2)}, u32[]{:S(2)}) collective-permute-start(bf16[80,2048]{1,0:T(8,128)(2,1)S(1)} %fusion.2), channel_id=1, source_target_pairs={{0,12},{1,13},{2,14},{3,15},{4,0},{5,1},{6,2},{7,3},{8,4},{9,5},{1... | collective-permute-start | bytes 983048 | tf_op jit(solution)/shard_map/ppermute | solution.py:353
  224.4 29.4 %collective-permute-start.33 = (bf16[80,2048]{1,0:T(8,128)(2,1)S(1)}, bf16[80,2048]{1,0:T(8,128)(2,1)S(1)}, u32[]{:S(2)}, u32[]{:S(2)}) collective-permute-start(bf16[80,2048]{1,0:T(8,128)(2,1)S(1)} %fusion.1), channel_id=1, source_target_pairs={{0,8},{1,9},{2,10},{3,11},{4,12},{5,13},{6,14},{7,15},{8,0},{9,1},... | collective-permute-start | bytes 983048 | tf_op jit(solution)/shard_map/ppermute | solution.py:353
  231.0 22.8 %collective-permute-start.40 = (bf16[80,2048]{1,0:T(8,128)(2,1)S(1)}, bf16[80,2048]{1,0:T(8,128)(2,1)S(1)}, u32[]{:S(2)}, u32[]{:S(2)}) collective-permute-start(bf16[80,2048]{1,0:T(8,128)(2,1)S(1)} %fusion), channel_id=1, source_target_pairs={{0,4},{1,5},{2,6},{3,7},{4,8},{5,9},{6,10},{7,11},{8,12},{9,13},{1... | collective-permute-start | bytes 983048 | tf_op jit(solution)/shard_map/ppermute | solution.py:353
  (9 other events, 6.6 us)

commit v2 on v0

v2 whole, which is shorter than its diff:
```python
import functools
import math

import jax
import jax.numpy as jnp
from jax import lax
from jax.experimental import pallas as pl
from jax.experimental.pallas import tpu as pltpu
from jax.sharding import PartitionSpec as P

OUTERS = 4
HEAD_SIZE = 128
LANES = 128
EPSILON = 1e-06
MIB = 1 << 20
BF16, F32 = jnp.bfloat16, jnp.float32
NT = (((1,), (1,)), ((), ()))
ANY = pl.BlockSpec(memory_space=pl.ANY)
VMEM = pl.BlockSpec(memory_space=pltpu.VMEM)
SMEM = pl.BlockSpec(memory_space=pltpu.SMEM)


def swap(array, n, offset):
    return lax.ppermute(array, "ctx", [(i, i ^ offset) for i in range(n)])


def gather_inner(array, n, *tokens):
    pieces = {0: array}
    bit = n // OUTERS // 2
    while bit:
        for j in list(pieces):
            ready = lax.optimization_barrier((pieces[j], *tokens))[0] if j and tokens else pieces[j]
            pieces[j | bit] = swap(ready, n, bit)
        bit //= 2
    return [pieces[j] for j in range(n // OUTERS)]


def halves(inner):
    order, bit = [0], inner // 2
    while bit:
        order = order + [j | bit for j in order]
        bit //= 2
    return order


def call(kernel, outs, operands, specs, name, tokens=(), limit=16, scratch=(), out_specs=None, grid=None, cost=True):
    count = len(operands)

    def body(*refs):
        kernel(*refs[:count], *refs[count + len(tokens) :])

    more = {} if grid is None else {"grid": grid}
    return pl.pallas_call(
        body,
        out_shape=outs,
        in_specs=list(specs) + [ANY] * len(tokens),
        out_specs=out_specs,
        scratch_shapes=list(scratch),
        compiler_params=pltpu.CompilerParams(vmem_limit_bytes=limit * MIB),
        cost_estimate=pl.CostEstimate(flops=1, bytes_accessed=1, transcendentals=0),
        name=name,
        **more,
    )(*operands, *tokens)


def whole(shape):
    return pl.BlockSpec(shape, lambda *_: (0,) * len(shape))


def start_all(pairs, sems):
    copies = [
        pltpu.make_async_copy(src, dst, sems.at[at]) for at, (src, dst) in enumerate(pairs)
    ]
    for copy in copies:
        copy.start()
    return copies


def wait_all(copies):
    for copy in copies:
        copy.wait()


def pack_kernel(inner, spot, *refs):
    sources, refs = refs[:6], refs[6:]
    outs, made = refs[:OUTERS], refs[OUTERS : 2 * OUTERS]
    queries, fresh, cache, ids, weights, placement, sems, last = refs[2 * OUTERS :]
    landed = (queries, fresh, cache, ids, weights, placement)
    copies = start_all(list(zip(sources, landed))[::-1], sems)[::-1]
    wait_all(copies[2:])
    outer, place = spot[0], spot[1]
    rows = queries.shape[0]
    keys = cache.shape[1]
    group = queries.shape[1] // (OUTERS * HEAD_SIZE)
    per_device = group // inner
    experts = placement.shape[1]
    part = experts // OUTERS
    share = weights[...] / jnp.sum(weights[...], axis=0, keepdims=True)
    expert = lax.broadcasted_iota(jnp.int32, (experts, rows), 0)
    gates = jnp.zeros((experts, rows), F32)
    for k in range(ids.shape[0]):
        gates += jnp.where(ids[k : k + 1, :] == expert, share[k : k + 1, :], 0.0)
    gates = gates.T
    high = gates.astype(BF16)
    low = (gates - high.astype(F32)).astype(BF16)
    lane = lax.broadcasted_iota(jnp.int32, (LANES, experts), 0)
    slot = jnp.broadcast_to(placement[...], (LANES, experts))
    half = LANES // 2
    sent = []
    wait_all(copies[:2])
    for k in [1, 2, 3, 0]:
        to = outer ^ k
        block = made[k]
        column = pl.ds(pl.multiple_of(to * HEAD_SIZE, HEAD_SIZE), HEAD_SIZE)
        block[0:keys, :] = cache[0, :, column]
        block[keys : 2 * keys, :] = cache[1, :, column]
        first = to * part
        pick_high = jnp.where((slot == first + lane) & (lane < part), 1.0, 0.0)
        pick_low = jnp.where(
            (slot == first + lane - half) & (lane >= half) & (lane < half + part), 1.0, 0.0
        )
        wanted = lax.dot_general(
            high, pick_high.astype(BF16), NT, preferred_element_type=F32
        ) + lax.dot_general(low, pick_low.astype(BF16), NT, preferred_element_type=F32)
        at = 2 * keys + rows
        block[2 * keys : at, :] = wanted.astype(BF16)
        for h in range(group):
            head = to * group + (place ^ (h // per_device)) * per_device + h % per_device
            block[at : at + rows, :] = queries[
                :, pl.ds(pl.multiple_of(head * HEAD_SIZE, HEAD_SIZE), HEAD_SIZE)
            ]
            at += rows
        block[at : at + rows, :] = fresh[0, :, column]
        block[at + rows :, :] = fresh[1, :, column]
        copy = pltpu.make_async_copy(block, outs[k], last.at[k])
        copy.start()
        sent.append(copy)
    wait_all(sent)


def merge_kernel(keys, rows, *refs):
    blocks, out, sems = refs[:-2], refs[-2], refs[-1]
    count = len(blocks)
    start = count * rows
    pairs = []
    for k in range(count):
        for at, size, to in (
            (2 * keys, rows, k * rows),
            (0, keys, start + k * keys),
            (keys, keys, start + (count + k) * keys),
        ):
            pairs.append((blocks[k].at[pl.ds(at, size)], out.at[pl.ds(to, size)]))
    wait_all(start_all(pairs, sems))


def attention_kernel(inner, group, rows, packed, *refs):
    caches, projections = refs[: 2 * inner], refs[2 * inner : 3 * inner]
    out, keys, values, attention = refs[3 * inner :]
    block = keys.shape[0] // (2 * inner)
    start = caches[0].shape[0] - 2 * block
    for j in range(2 * inner):
        keys[j * block : (j + 1) * block, :] = caches[j][start : start + block, :]
        values[j * block : (j + 1) * block, :] = caches[j][start + block :, :]
    factor = HEAD_SIZE ** (-0.5) * math.log2(math.e)
    qf = packed.at[pl.ds(packed.shape[0] - (group + 2) * rows, (group + 2) * rows)]
    own_key = qf[group * rows : (group + 1) * rows, :].astype(F32)
    own_value = qf[(group + 1) * rows :, :].astype(F32)
    step = max(1, group // 2)
    for h0 in range(0, group, step):
        query = qf[h0 * rows : (h0 + step) * rows, :]
        own = jnp.sum(
            query.astype(F32) * jnp.concatenate([own_key] * step, axis=0), axis=-1, keepdims=True
        )
        scores = lax.dot_general(query, keys[...], NT, preferred_element_type=F32)
        peak = jnp.maximum(own, jnp.max(scores, axis=-1, keepdims=True)) * factor
        weights = jnp.exp2(scores * factor - peak)
        own = jnp.exp2(own * factor - peak)
        totals = jnp.sum(weights, axis=-1, keepdims=True) + own
        weighted = jnp.dot(weights.astype(BF16), values[...], preferred_element_type=F32)
        weighted = weighted + own * jnp.concatenate([own_value] * step, axis=0)
        block_out = (weighted / totals).astype(BF16)
        for h in range(step):
            attention[:, (h0 + h) * HEAD_SIZE : (h0 + h + 1) * HEAD_SIZE] = block_out[
                h * rows : (h + 1) * rows, :
            ]
    depth = projections[0].shape[0]
    wide = math.gcd(out.shape[1], 512)
    for c in range(0, out.shape[1], wide):
        total = jnp.dot(
            attention[:, :depth], projections[0][:, c : c + wide], preferred_element_type=F32
        )
        for j in range(1, inner):
            total += jnp.dot(
                attention[:, j * depth : (j + 1) * depth],
                projections[j][:, c : c + wide],
                preferred_element_type=F32,
            )
        out[:, c : c + wide] = total.astype(out.dtype)


def select_kernel(inner, local, capacity, spot, *refs):
    gates, (sel, selt, share) = refs[: 2 * inner], refs[2 * inner :]
    early = pl.program_id(0) < OUTERS // 2
    table = jnp.concatenate(
        [jnp.where(early, gates[j][...], gates[inner + j][...]) for j in halves(inner)], axis=0
    )
    rows = table.shape[0]
    first = spot[1] * local
    lane = lax.broadcasted_iota(jnp.int32, (LANES, LANES), 1)
    sub = lax.broadcasted_iota(jnp.int32, (LANES, LANES), 0)
    pick = jnp.where((lane == first + sub) & (sub < local), 1.0, 0.0).astype(BF16)
    across = lax.dot_general(pick[:16], table, NT, preferred_element_type=F32)
    down = lax.dot_general(table, pick, NT, preferred_element_type=F32)
    r = lax.broadcasted_iota(jnp.int32, (rows, rows), 0)
    c = lax.broadcasted_iota(jnp.int32, (rows, rows), 1)
    upper = jnp.where(r <= c, 1.0, 0.0).astype(BF16)
    lower = jnp.where(c <= r, 1.0, 0.0).astype(BF16)
    across_rank = jnp.dot(
        jnp.where(across > 0, 1.0, 0.0).astype(BF16), upper, preferred_element_type=F32
    )
    across_rank = jnp.where(across > 0, across_rank, 0.0)
    down_rank = jnp.dot(
        lower, jnp.where(down > 0, 1.0, 0.0).astype(BF16), preferred_element_type=F32
    )
    down_rank = jnp.where(down > 0, down_rank, 0.0)
    place = lax.broadcasted_iota(jnp.int32, (capacity, rows), 0).astype(F32) + 1.0
    place_t = lax.broadcasted_iota(jnp.int32, (rows, capacity), 1).astype(F32) + 1.0
    spread = lax.broadcasted_iota(jnp.int32, (capacity, LANES), 1)
    for e in range(local):
        chosen = jnp.where(across_rank[e : e + 1, :] == place, 1.0, 0.0).astype(BF16)
        sel[0, e * capacity : (e + 1) * capacity, :] = chosen
        selt[0, :, e * capacity : (e + 1) * capacity] = jnp.where(
            down_rank[:, e : e + 1] == place_t, 1.0, 0.0
        ).astype(BF16)
        mine = (spread == first + e) | (spread == first + e + LANES // 2)
        found = jnp.dot(chosen, table, preferred_element_type=F32)
        value = jnp.sum(jnp.where(mine, found, 0.0), axis=-1, keepdims=True)
        share[0, e * capacity : (e + 1) * capacity, :] = jnp.broadcast_to(value, (capacity, LANES))


def norm_kernel(residual, gain, own, *refs):
    arrived, (hidden, normed) = refs[:-2], refs[-2:]
    total = own[...]
    for ref in arrived:
        total = total + ref[...].astype(F32)
    rounded = (residual[...].astype(F32) + total).astype(BF16)
    hidden[...] = rounded
    wide = rounded.astype(F32)
    scale = lax.rsqrt(jnp.mean(wide * wide, axis=-1, keepdims=True) + EPSILON)
    normed[...] = (wide * scale * gain[...]).astype(BF16)


def expert_kernel(inner, chunk, *refs):
    pieces = refs[:inner]
    sel, selt, share, gate_up, down = refs[inner : inner + 5]
    sel, selt, share = sel.at[chunk], selt.at[chunk], share.at[chunk]
    outs = refs[inner + 5 : 2 * inner + 5]
    stacked, packed, active, made = refs[2 * inner + 5 :]
    local, width, both = gate_up.shape
    ff = both // 2
    rows = pieces[0].shape[0]
    capacity = sel.shape[0] // local
    for at, j in enumerate(halves(inner)):
        stacked[at * rows : (at + 1) * rows, :] = pieces[j][...]
    wide = math.gcd(width, 512)
    tile = math.gcd(ff, 256)
    for c in range(0, width, wide):
        packed[:, c : c + wide] = jnp.dot(
            sel[...], stacked[:, c : c + wide], preferred_element_type=F32
        ).astype(BF16)
    for e in range(local):
        at = slice(e * capacity, (e + 1) * capacity)
        for f in range(0, ff, tile):
            left = jnp.dot(packed[at, :], gate_up[e, :, f : f + tile], preferred_element_type=F32)
            right = jnp.dot(
                packed[at, :], gate_up[e, :, ff + f : ff + f + tile], preferred_element_type=F32
            )
            active[at, f : f + tile] = (left / (1.0 + jnp.exp(-left)) * right).astype(BF16)
        for c in range(0, width, wide):
            produced = jnp.dot(active[at, :], down[e, :, c : c + wide], preferred_element_type=F32)
            made[at, c : c + wide] = (produced * share[at, 0:1]).astype(BF16)
    for c in range(0, width, wide):
        total = jnp.dot(selt[...], made[:, c : c + wide], preferred_element_type=F32).astype(BF16)
        for at, out in enumerate(outs):
            out[:, c : c + wide] = total[at * rows : (at + 1) * rows, :]


def add_kernel(*refs):
    total = refs[0][...].astype(F32)
    for ref in refs[1:-1]:
        total = total + ref[...].astype(F32)
    refs[-1][...] = total.astype(refs[-1].dtype)


def local_program(
    n,
    queries,
    fresh,
    cache,
    residual,
    gain,
    out_proj,
    w_gate_up,
    w_down,
    route_ids,
    route_weights,
    placement,
):
    inner = n // OUTERS
    rows, width = residual.shape
    keys = cache.shape[1]
    group = queries.shape[1] // (OUTERS * HEAD_SIZE)
    local, _, both = w_gate_up.shape
    ff = both // 2
    experts_all = placement.shape[0]
    top = route_ids.shape[1]
    most = max(2, 3 * rows * top // (2 * experts_all))
    capacity = -(-most * inner // 16) * 16
    chunk_rows = rows * inner
    me = lax.axis_index("ctx")
    spot = jnp.stack([me // inner, me % inner]).astype(jnp.int32)
    dma = pltpu.SemaphoreType.DMA

    packed_rows = 2 * keys + rows + (group + 2) * rows
    ids_t, weights_t, slots = route_ids.T, route_weights.T, placement.reshape(1, -1)
    operands = (queries, fresh, cache, ids_t, weights_t, slots)
    packed = call(
        functools.partial(pack_kernel, inner),
        [jax.ShapeDtypeStruct((packed_rows, HEAD_SIZE), BF16)] * OUTERS,
        (spot, *operands),
        [SMEM] + [ANY] * 6,
        "pack",
        limit=60,
        out_specs=[ANY] * OUTERS,
        scratch=[
            *[pltpu.VMEM((packed_rows, HEAD_SIZE), BF16)] * OUTERS,
            *[pltpu.VMEM(a.shape, a.dtype) for a in operands],
            dma((6,)),
            dma((OUTERS,)),
        ],
    )
    blocks = [packed[0]] + [swap(packed[k], n, k * inner) for k in range(1, OUTERS)]
    half_outers = OUTERS // 2
    caches, tokens = [], ()
    for at in (0, half_outers):
        merged = call(
            functools.partial(merge_kernel, keys, rows),
            jax.ShapeDtypeStruct((half_outers * (2 * keys + rows), HEAD_SIZE), BF16),
            blocks[at : at + half_outers],
            [ANY] * half_outers,
            "merge",
            tokens,
            out_specs=ANY,
            scratch=[dma((3 * half_outers,))],
        )
        caches += gather_inner(merged, n)
        tokens = (caches[inner // 2],)
    projections = gather_inner(out_proj, n, merged)

    def add(terms, tokens=()):
        return call(
            add_kernel,
            jax.ShapeDtypeStruct((rows, width), BF16),
            terms,
            [VMEM] * len(terms),
            "add",
            tokens,
            out_specs=VMEM,
        )

    def attend(k, tokens, kind):
        return call(
            functools.partial(attention_kernel, inner, group, rows),
            jax.ShapeDtypeStruct((rows, width), kind),
            (blocks[k], *caches, *projections),
            [VMEM] * (1 + 3 * inner),
            "attention",
            tokens,
            limit=18,
            out_specs=VMEM,
            scratch=[
                pltpu.VMEM((n * keys, HEAD_SIZE), BF16),
                pltpu.VMEM((n * keys, HEAD_SIZE), BF16),
                pltpu.VMEM((rows, group * HEAD_SIZE), BF16),
            ],
        )

    selected = [
        (local * capacity, chunk_rows),
        (chunk_rows, local * capacity),
        (local * capacity, LANES),
    ]
    kinds = [BF16, BF16, F32]
    last_half = half_outers - 1
    far = attend(3, (), BF16)
    across = attend(2, (far,), F32)
    near = attend(1, (across,), BF16)
    sent = add([across, swap(far, n, inner)], (near,))
    own = attend(0, (sent,), F32)
    home = [swap(near, n, inner), swap(sent, n, 2 * inner)]
    selection = call(
        functools.partial(select_kernel, inner, local, capacity),
        [jax.ShapeDtypeStruct((OUTERS, *s), d) for s, d in zip(selected, kinds)],
        (spot, *caches),
        [SMEM]
        + [pl.BlockSpec((rows, LANES), lambda k: (jnp.minimum(k, last_half), 0))] * inner
        + [pl.BlockSpec((rows, LANES), lambda k: (jnp.maximum(k - half_outers, 0), 0))] * inner,
        "select",
        (own,),
        out_specs=[pl.BlockSpec((1, *s), lambda k: (k, 0, 0)) for s in selected],
        grid=(OUTERS,),
    )
    block = whole((rows, width))
    hidden, normed = call(
        norm_kernel,
        [jax.ShapeDtypeStruct((rows, width), BF16)] * 2,
        (residual, gain.reshape(1, -1), own, *home),
        [block, whole((1, width)), block, block, block],
        "norm",
        (selection[0],),
        out_specs=[block, block],
        grid=(1,),
    )

    def experts(k, pieces, tokens):
        return call(
            functools.partial(expert_kernel, inner, k),
            [jax.ShapeDtypeStruct((rows, width), BF16)] * inner,
            (*pieces, *selection, w_gate_up, w_down),
            [VMEM] * (inner + 5),
            "experts",
            tokens,
            limit=14,
            out_specs=[VMEM] * inner,
            scratch=[
                pltpu.VMEM((chunk_rows, width), BF16),
                pltpu.VMEM((local * capacity, width), BF16),
                pltpu.VMEM((local * capacity, ff), BF16),
                pltpu.VMEM((local * capacity, width), BF16),
            ],
        )

    bits = [1 << b for b in range(inner.bit_length() - 1)]
    first, second = swap(normed, n, inner), swap(normed, n, 2 * inner)
    around = gather_inner(normed, n)
    third = swap(second, n, inner)
    slots = [None] * OUTERS

    def fold(k):
        middle = len(slots[k]) // 2
        arrived = [swap(a, n, bits[0]) for a in slots[k][:middle - 1:-1]][::-1]
        slots[k] = [[a, b] for a, b in zip(slots[k][:middle], arrived)]

    def finish(k, tokens):
        terms = slots[k]
        for bit in bits[1:]:
            middle = len(terms) // 2
            sent = [add(t, tokens) for t in terms[middle:]]
            terms = [t + [swap(a, n, bit)] for t, a in zip(terms[:middle], sent)]
        return terms[0], sent[0]

    slots[0] = experts(0, around, ())
    fold(0)
    done = slots[0][0][0]
    slots[1] = experts(1, gather_inner(first, n, done), (done, second))
    fold(1)
    done = slots[1][0][0]
    slots[3] = experts(3, gather_inner(third, n, done), (done,))
    fold(3)
    done = slots[3][0][0]
    terms, sent = finish(3, (done,))
    slots[2] = experts(2, gather_inner(second, n, done), (sent,))
    fold(2)
    far = swap(add(terms, (slots[2][0][0],)), n, inner)
    terms, sent = finish(2, (slots[2][0][0],))
    total = add(terms + [far], (sent,))
    across = swap(total, n, 2 * inner)
    terms, sent = finish(1, (total,))
    total = add(terms, (sent,))
    near = swap(total, n, inner)
    terms, sent = finish(0, (total,))
    return hidden, add(terms + [near, across])


def solution(mesh):
    rows = P(("groups", "ctx"), None)
    middle = P(None, ("groups", "ctx"), None)
    in_specs = (
        rows,
        middle,
        middle,
        rows,
        P(),
        P("ctx", None),
        P("ctx", None, None),
        P("ctx", None, None),
        rows,
        rows,
        P(),
    )
    return jax.shard_map(
        functools.partial(local_program, mesh.shape["ctx"]),
        mesh=mesh,
        in_specs=in_specs,
        out_specs=(rows, rows),
        check_vma=False,
    )
```

time: 446 us -> 166 us (0.37)
  the two profiles are of different devices: /device:TPU:13 before, /device:TPU:0 now
where the time goes in v2:
time: 166 us; the launch traced here: 165 us
  waiting for transfers between devices  82.8 us (50%)
  starting transfers between devices  41.1 us (25%)
  Pallas kernels  37.7 us (23%)
  local copies, waits for them, and re-layouts  2.24 us (1%)
    ppermute x45, waiting for transfers between devices, swap(): return lax.ppermute(array, 'ctx', [(i, i ^ offset) for i in range(n)])  82.8 us
    ppermute x45, starting transfers between devices, swap(): return lax.ppermute(array, 'ctx', [(i, i ^ offset) for i in range(n)])  41.1 us
    pallas_call x22, Pallas kernels, call(): pl.pallas_call(body, out_shape=outs, in_specs=list(specs) + [ANY] * len(t...  37.7 us
  transfers between devices with their start and end apart: 45, of which 22 were waited for; matrix products, arithmetic and copies ran while one was open for 0% of the time, Pallas kernels for 17%

profile of v2, /device:TPU:0, one launch (start us, length us, event | category | flops | bytes accessed | tf_op | source)
XLA Modules:
  0.0 165.5 jit_solution(18115133459942493834)
XLA Ops:
  0.6 3.0 %collective-permute-start.10 = (bf16[256,2048]{1,0:T(8,128)(2,1)}, bf16[256,2048]{1,0:T(8,128)(2,1)S(1)}, u32[]{:S(2)}, u32[]{:S(2)}) collective-permute-start(bf16[256,2048]{1,0:T(8,128)(2,1)} %refs_9_.7), channel_id=1, source_target_pairs={{0,2},{1,3},{2,0},{3,1},{4,6},{5,7},{6,4},{7,5},{8,10},{9,11},{10,... | collective-permute-start | bytes 3145736 | tf_op jit(solution)/shard_map/ppermute | solution.py:24
  4.3 3.2 %pack.1 = (bf16[1136,128]{1,0:T(8,128)(2,1)}, bf16[1136,128]{1,0:T(8,128)(2,1)}, bf16[1136,128]{1,0:T(8,128)(2,1)}, bf16[1136,128]{1,0:T(8,128)(2,1)}) custom-call(s32[2]{0:T(128)} %pad_add_fusion.refs_0_, bf16[80,4096]{1,0:T(8,128)(2,1)} %refs_1_.1, bf16[2,80,512]{2,1,0:T(8,128)(2,1)} %refs_2_.1, bf16[2,128,512]{2,1,0:T(8,128)(2,1)} %refs_3_.1, ...), custom_call_target="tpu_custom_call" | custom-call | flops 1 | bytes 1 | tf_op jit(solution)/shard_map/pack/pallas_call | solution.py:53
  7.5 1.6 collective-permute-start
  9.2 2.6 %collective-permute-start.4 = (bf16[1136,128]{1,0:T(8,128)(2,1)}, bf16[1136,128]{1,0:T(8,128)(2,1)S(1)}, u32[]{:S(2)}, u32[]{:S(2)}) collective-permute-start(bf16[1136,128]{1,0:T(8,128)(2,1)} %get-tuple-element.33), channel_id=1, source_target_pairs={{0,8},{1,9},{2,10},{3,11},{4,12},{5,13},{6,14},{7,15},{8,0},{9,1},... | collective-permute-start | bytes 872456 | tf_op jit(solution)/shard_map/ppermute | solution.py:24
  12.0 9.5 %collective-permute-done.refs_1_.refs_0_ = bf16[1136,128]{1,0:T(8,128)(2,1)S(1)} collective-permute-done((bf16[1136,128]{1,0:T(8,128)(2,1)}, bf16[1136,128]{1,0:T(8,128)(2,1)S(1)}, u32[]{:S(2)}, u32[]{:S(2)}) %collective-permute-start) | collective-permute-done | bytes 290848 | tf_op jit(solution)/shard_map/ppermute | solution.py:24
  21.5 1.0 copy-done.1
  23.1 9.5 %collective-permute-done.4.refs_0_ = bf16[1136,128]{1,0:T(8,128)(2,1)S(1)} collective-permute-done((bf16[1136,128]{1,0:T(8,128)(2,1)}, bf16[1136,128]{1,0:T(8,128)(2,1)S(1)}, u32[]{:S(2)}, u32[]{:S(2)}) %collective-permute-start.4) | collective-permute-done | bytes 290848 | tf_op jit(solution)/shard_map/ppermute | solution.py:24
  34.0 1.9 %collective-permute-done.1.refs_2_ = bf16[672,128]{1,0:T(8,128)(2,1)S(1)} collective-permute-done((bf16[672,128]{1,0:T(8,128)(2,1)S(1)}, bf16[672,128]{1,0:T(8,128)(2,1)S(1)}, u32[]{:S(2)}, u32[]{:S(2)}) %collective-permute-start.1) | collective-permute-done | bytes 172064 | tf_op jit(solution)/shard_map/ppermute | solution.py:24
  36.0 3.8 %collective-permute-done.7.refs_7_ = bf16[672,128]{1,0:T(8,128)(2,1)S(1)} collective-permute-done((bf16[672,128]{1,0:T(8,128)(2,1)S(1)}, bf16[672,128]{1,0:T(8,128)(2,1)S(1)}, u32[]{:S(2)}, u32[]{:S(2)}) %collective-permute-start.7) | collective-permute-done | bytes 172064 | tf_op jit(solution)/shard_map/ppermute | solution.py:24
  39.8 1.4 collective-permute-done.8.refs_8_
  41.3 1.2 copy-done
  42.5 3.3 %attention.4.refs_13_ = bf16[80,2048]{1,0:T(8,128)(2,1)S(1)} custom-call(bf16[1136,128]{1,0:T(8,128)(2,1)S(1)} %collective-permute-done.5.refs_1_.refs_0_, bf16[672,128]{1,0:T(8,128)(2,1)S(1)} %merge.2.refs_1_, bf16[672,128]{1,0:T(8,128)(2,1)S(1)} %collective-permute-done.1.refs_2_, bf16[672,128]{1,0:T(8,128)(2,1)S(1)} %collective-permute-done.2.refs_2_.refs_3_, ...), custom_call_target="tpu_custom_call" | custom-call | flops 1 | bytes 1 | tf_op jit(solution)/shard_map/attention/pallas_call | solution.py:53
  45.8 5.1 %collective-permute-start.12 = (bf16[80,2048]{1,0:T(8,128)(2,1)S(1)}, bf16[80,2048]{1,0:T(8,128)(2,1)S(1)}, u32[]{:S(2)}, u32[]{:S(2)}) collective-permute-start(bf16[80,2048]{1,0:T(8,128)(2,1)S(1)} %attention.4.refs_13_), channel_id=1, source_target_pairs={{0,4},{1,5},{2,6},{3,7},{4,0},{5,1},{6,2},{7,3},{8,12},{9,13},{10,... | collective-permute-start | bytes 983048 | tf_op jit(solution)/shard_map/ppermute | solution.py:24
  51.0 3.3 %attention.5.refs_13_.refs_0_ = f32[80,2048]{1,0:T(8,128)S(1)} custom-call(bf16[1136,128]{1,0:T(8,128)(2,1)S(1)} %collective-permute-done.4.refs_0_, bf16[672,128]{1,0:T(8,128)(2,1)S(1)} %merge.2.refs_1_, bf16[672,128]{1,0:T(8,128)(2,1)S(1)} %collective-permute-done.1.refs_2_, bf16[672,128]{1,0:T(8,128)(2,1)S(1)} %collective-permute-done.2.refs_2_.refs_3_, ...), custom_call_target="tpu_custom_call" | custom-call | flops 1 | bytes 1 | tf_op jit(solution)/shard_map/attention/pallas_call | solution.py:53
  54.3 3.3 %attention.6.refs_2_ = bf16[80,2048]{1,0:T(8,128)(2,1)S(1)} custom-call(bf16[1136,128]{1,0:T(8,128)(2,1)S(1)} %collective-permute-done.refs_1_.refs_0_, bf16[672,128]{1,0:T(8,128)(2,1)S(1)} %merge.2.refs_1_, bf16[672,128]{1,0:T(8,128)(2,1)S(1)} %collective-permute-done.1.refs_2_, bf16[672,128]{1,0:T(8,128)(2,1)S(1)} %collective-permute-done.2.refs_2_.refs_3_, ...), custom_call_target="tpu_custom_call" | custom-call | flops 1 | bytes 1 | tf_op jit(solution)/shard_map/attention/pallas_call | solution.py:53
  57.7 1.3 collective-permute-done.12.refs_1_
  59.1 3.0 %collective-permute-start.14 = (bf16[80,2048]{1,0:T(8,128)(2,1)S(1)}, bf16[80,2048]{1,0:T(8,128)(2,1)S(1)}, u32[]{:S(2)}, u32[]{:S(2)}) collective-permute-start(bf16[80,2048]{1,0:T(8,128)(2,1)S(1)} %add.17.refs_13_), channel_id=1, source_target_pairs={{0,8},{1,9},{2,10},{3,11},{4,12},{5,13},{6,14},{7,15},{8,0},{9,1},... | collective-permute-start | bytes 983048 | tf_op jit(solution)/shard_map/ppermute | solution.py:24
  62.1 3.3 %attention.7.refs_9_.refs_2_ = f32[80,2048]{1,0:T(8,128)S(1)} custom-call(bf16[1136,128]{1,0:T(8,128)(2,1)S(1)} %copy-done.2, bf16[672,128]{1,0:T(8,128)(2,1)S(1)} %merge.2.refs_1_, bf16[672,128]{1,0:T(8,128)(2,1)S(1)} %collective-permute-done.1.refs_2_, bf16[672,128]{1,0:T(8,128)(2,1)S(1)} %collective-permute-done.2.refs_2_.refs_3_, ...), custom_call_target="tpu_custom_call" | custom-call | flops 1 | bytes 1 | tf_op jit(solution)/shard_map/attention/pallas_call | solution.py:53
  65.5 3.1 %select.7 = (bf16[4,256,320]{2,1,0:T(8,128)(2,1)S(1)}, bf16[4,320,256]{2,1,0:T(8,128)(2,1)S(1)}, f32[4,256,128]{2,1,0:T(8,128)S(1)}) custom-call(s32[2]{0:T(128)S(1)} %copy-done.5, bf16[672,128]{1,0:T(8,128)(2,1)S(1)} %merge.2.refs_1_, bf16[672,128]{1,0:T(8,128)(2,1)S(1)} %collective-permute-done.1.refs_2_, ...), custom_call_target="tpu_custom_call" | custom-call | flops 1 | bytes 1 | tf_op jit(solution)/shard_map/select/pallas_call | solution.py:53
  68.6 4.5 %collective-permute-done.13.refs_3_ = bf16[80,2048]{1,0:T(8,128)(2,1)S(1)} collective-permute-done((bf16[80,2048]{1,0:T(8,128)(2,1)S(1)}, bf16[80,2048]{1,0:T(8,128)(2,1)S(1)}, u32[]{:S(2)}, u32[]{:S(2)}) %collective-permute-start.13) | collective-permute-done | bytes 327712 | tf_op jit(solution)/shard_map/ppermute | solution.py:24
  73.1 3.2 %collective-permute-done.14.refs_4_ = bf16[80,2048]{1,0:T(8,128)(2,1)S(1)} collective-permute-done((bf16[80,2048]{1,0:T(8,128)(2,1)S(1)}, bf16[80,2048]{1,0:T(8,128)(2,1)S(1)}, u32[]{:S(2)}, u32[]{:S(2)}) %collective-permute-start.14) | collective-permute-done | bytes 327712 | tf_op jit(solution)/shard_map/ppermute | solution.py:24
  77.8 3.0 %collective-permute-start.24 = (bf16[80,2048]{1,0:T(8,128)(2,1)S(1)}, bf16[80,2048]{1,0:T(8,128)(2,1)S(1)}, u32[]{:S(2)}, u32[]{:S(2)}) collective-permute-start(bf16[80,2048]{1,0:T(8,128)(2,1)S(1)} %get-tuple-element.38.refs_0_), channel_id=1, source_target_pairs={{0,8},{1,9},{2,10},{3,11},{4,12},{5,13},{6,14},{7,15},{8,0},{9,1},... | collective-permute-start | bytes 983048 | tf_op jit(solution)/shard_map/ppermute | solution.py:24
  80.8 3.5 %collective-permute-done.16.refs_2_ = bf16[80,2048]{1,0:T(8,128)(2,1)S(1)} collective-permute-done((bf16[80,2048]{1,0:T(8,128)(2,1)S(1)}, bf16[80,2048]{1,0:T(8,128)(2,1)S(1)}, u32[]{:S(2)}, u32[]{:S(2)}) %collective-permute-start.16) | collective-permute-done | bytes 327712 | tf_op jit(solution)/shard_map/ppermute | solution.py:24
  84.4 6.9 %collective-permute-done.20.refs_0_ = bf16[80,2048]{1,0:T(8,128)(2,1)S(1)} collective-permute-done((bf16[80,2048]{1,0:T(8,128)(2,1)S(1)}, bf16[80,2048]{1,0:T(8,128)(2,1)S(1)}, u32[]{:S(2)}, u32[]{:S(2)}) %collective-permute-start.20) | collective-permute-done | bytes 327712 | tf_op jit(solution)/shard_map/ppermute | solution.py:24
  91.2 1.5 collective-permute-start.22
  92.7 1.3 collective-permute-done.24.refs_10_.refs_0_
  94.4 3.7 %experts.4 = (bf16[80,2048]{1,0:T(8,128)(2,1)S(1)}, bf16[80,2048]{1,0:T(8,128)(2,1)S(1)}, bf16[80,2048]{1,0:T(8,128)(2,1)S(1)}, bf16[80,2048]{1,0:T(8,128)(2,1)S(1)}) custom-call(bf16[80,2048]{1,0:T(8,128)(2,1)S(1)} %get-tuple-element.38.refs_0_, bf16[80,2048]{1,0:T(8,128)(2,1)S(1)} %collective-permute-done.15.refs_1_, ...), custom_call_target="tpu_custom_call" | custom-call | flops 1 | bytes 1 | tf_op jit(solution)/shard_map/experts/pallas_call | solution.py:53
  98.7 2.5 %collective-permute-done.29.refs_0_ = bf16[80,2048]{1,0:T(8,128)(2,1)S(1)} collective-permute-done((bf16[80,2048]{1,0:T(8,128)(2,1)S(1)}, bf16[80,2048]{1,0:T(8,128)(2,1)S(1)}, u32[]{:S(2)}, u32[]{:S(2)}) %collective-permute-start.29) | collective-permute-done | bytes 327712 | tf_op jit(solution)/shard_map/ppermute | solution.py:24
  101.1 1.5 collective-permute-start.31
  102.7 3.7 %experts.5 = (bf16[80,2048]{1,0:T(8,128)(2,1)S(1)}, bf16[80,2048]{1,0:T(8,128)(2,1)S(1)}, bf16[80,2048]{1,0:T(8,128)(2,1)S(1)}, bf16[80,2048]{1,0:T(8,128)(2,1)S(1)}) custom-call(bf16[80,2048]{1,0:T(8,128)(2,1)S(1)} %collective-permute-done.20.refs_0_, bf16[80,2048]{1,0:T(8,128)(2,1)S(1)} %collective-permute-done.21.refs_1_, ...), custom_call_target="tpu_custom_call" | custom-call | flops 1 | bytes 1 | tf_op jit(solution)/shard_map/experts/pallas_call | solution.py:53
  106.4 2.1 %collective-permute-done.31.refs_2_ = bf16[80,2048]{1,0:T(8,128)(2,1)S(1)} collective-permute-done((bf16[80,2048]{1,0:T(8,128)(2,1)S(1)}, bf16[80,2048]{1,0:T(8,128)(2,1)S(1)}, u32[]{:S(2)}, u32[]{:S(2)}) %collective-permute-start.31) | collective-permute-done | bytes 327712 | tf_op jit(solution)/shard_map/ppermute | solution.py:24
  108.4 1.5 collective-permute-start.28
  110.2 3.7 %experts.6 = (bf16[80,2048]{1,0:T(8,128)(2,1)S(1)}, bf16[80,2048]{1,0:T(8,128)(2,1)S(1)}, bf16[80,2048]{1,0:T(8,128)(2,1)S(1)}, bf16[80,2048]{1,0:T(8,128)(2,1)S(1)}) custom-call(bf16[80,2048]{1,0:T(8,128)(2,1)S(1)} %collective-permute-done.29.refs_0_, bf16[80,2048]{1,0:T(8,128)(2,1)S(1)} %collective-permute-done.30.refs_1_, ...), custom_call_target="tpu_custom_call" | custom-call | flops 1 | bytes 1 | tf_op jit(solution)/shard_map/experts/pallas_call | solution.py:53
  114.2 4.3 %collective-permute-done.28.refs_2_ = bf16[80,2048]{1,0:T(8,128)(2,1)S(1)} collective-permute-done((bf16[80,2048]{1,0:T(8,128)(2,1)S(1)}, bf16[80,2048]{1,0:T(8,128)(2,1)S(1)}, u32[]{:S(2)}, u32[]{:S(2)}) %collective-permute-start.28) | collective-permute-done | bytes 327712 | tf_op jit(solution)/shard_map/ppermute | solution.py:24
  118.7 1.5 collective-permute-done.33.refs_3_
  120.2 3.9 %experts.7 = (bf16[80,2048]{1,0:T(8,128)(2,1)S(1)}, bf16[80,2048]{1,0:T(8,128)(2,1)S(1)}, bf16[80,2048]{1,0:T(8,128)(2,1)S(1)}, bf16[80,2048]{1,0:T(8,128)(2,1)S(1)}) custom-call(bf16[80,2048]{1,0:T(8,128)(2,1)S(1)} %collective-permute-done.24.refs_10_.refs_0_, bf16[80,2048]{1,0:T(8,128)(2,1)S(1)} %collective-permute-done.27.refs_1_, ...), custom_call_target="tpu_custom_call" | custom-call | flops 1 | bytes 1 | tf_op jit(solution)/shard_map/experts/pallas_call | solution.py:53
  124.7 1.5 collective-permute-start.39
  126.3 1.2 collective-permute-start.37
  127.5 7.8 %collective-permute-done.39.refs_2_ = bf16[80,2048]{1,0:T(8,128)(2,1)S(1)} collective-permute-done((bf16[80,2048]{1,0:T(8,128)(2,1)S(1)}, bf16[80,2048]{1,0:T(8,128)(2,1)S(1)}, u32[]{:S(2)}, u32[]{:S(2)}) %collective-permute-start.39) | collective-permute-done | bytes 327712 | tf_op jit(solution)/shard_map/ppermute | solution.py:24
  135.4 1.8 %collective-permute-start.40 = (bf16[80,2048]{1,0:T(8,128)(2,1)S(1)}, bf16[80,2048]{1,0:T(8,128)(2,1)S(1)}, u32[]{:S(2)}, u32[]{:S(2)}) collective-permute-start(bf16[80,2048]{1,0:T(8,128)(2,1)S(1)} %add.20), channel_id=1, source_target_pairs={{0,4},{1,5},{2,6},{3,7},{4,0},{5,1},{6,2},{7,3},{8,12},{9,13},{10,... | collective-permute-start | bytes 983048 | tf_op jit(solution)/shard_map/ppermute | solution.py:24
  137.7 3.8 %collective-permute-done.37.refs_2_ = bf16[80,2048]{1,0:T(8,128)(2,1)S(1)} collective-permute-done((bf16[80,2048]{1,0:T(8,128)(2,1)S(1)}, bf16[80,2048]{1,0:T(8,128)(2,1)S(1)}, u32[]{:S(2)}, u32[]{:S(2)}) %collective-permute-start.37) | collective-permute-done | bytes 327712 | tf_op jit(solution)/shard_map/ppermute | solution.py:24
  141.5 2.1 %collective-permute-done.40.refs_3_ = bf16[80,2048]{1,0:T(8,128)(2,1)S(1)} collective-permute-done((bf16[80,2048]{1,0:T(8,128)(2,1)S(1)}, bf16[80,2048]{1,0:T(8,128)(2,1)S(1)}, u32[]{:S(2)}, u32[]{:S(2)}) %collective-permute-start.40) | collective-permute-done | bytes 327712 | tf_op jit(solution)/shard_map/ppermute | solution.py:24
  143.8 1.6 collective-permute-start.41
  145.9 3.3 %collective-permute-start.44 = (bf16[80,2048]{1,0:T(8,128)(2,1)S(1)}, bf16[80,2048]{1,0:T(8,128)(2,1)S(1)}, u32[]{:S(2)}, u32[]{:S(2)}) collective-permute-start(bf16[80,2048]{1,0:T(8,128)(2,1)S(1)} %add.21.refs_2_), channel_id=1, source_target_pairs={{0,8},{1,9},{2,10},{3,11},{4,12},{5,13},{6,14},{7,15},{8,0},{9,1},... | collective-permute-start | bytes 983048 | tf_op jit(solution)/shard_map/ppermute | solution.py:24
  149.3 1.8 %collective-permute-done.41.refs_2_ = bf16[80,2048]{1,0:T(8,128)(2,1)S(1)} collective-permute-done((bf16[80,2048]{1,0:T(8,128)(2,1)S(1)}, bf16[80,2048]{1,0:T(8,128)(2,1)S(1)}, u32[]{:S(2)}, u32[]{:S(2)}) %collective-permute-start.41) | collective-permute-done | bytes 327712 | tf_op jit(solution)/shard_map/ppermute | solution.py:24
  151.2 1.8 %collective-permute-start.43 = (bf16[80,2048]{1,0:T(8,128)(2,1)S(1)}, bf16[80,2048]{1,0:T(8,128)(2,1)S(1)}, u32[]{:S(2)}, u32[]{:S(2)}) collective-permute-start(bf16[80,2048]{1,0:T(8,128)(2,1)S(1)} %add.23.refs_2_), channel_id=1, source_target_pairs={{0,4},{1,5},{2,6},{3,7},{4,0},{5,1},{6,2},{7,3},{8,12},{9,13},{10,... | collective-permute-start | bytes 983048 | tf_op jit(solution)/shard_map/ppermute | solution.py:24
  153.1 1.7 %collective-permute-start.42 = (bf16[80,2048]{1,0:T(8,128)(2,1)S(1)}, bf16[80,2048]{1,0:T(8,128)(2,1)S(1)}, u32[]{:S(2)}, u32[]{:S(2)}) collective-permute-start(bf16[80,2048]{1,0:T(8,128)(2,1)S(1)} %add.24), channel_id=1, source_target_pairs={{0,2},{1,3},{2,0},{3,1},{4,6},{5,7},{6,4},{7,5},{8,10},{9,11},{10,... | collective-permute-start | bytes 983048 | tf_op jit(solution)/shard_map/ppermute | solution.py:24
  154.8 9.4 %collective-permute-done.44.refs_4_ = bf16[80,2048]{1,0:T(8,128)(2,1)S(1)} collective-permute-done((bf16[80,2048]{1,0:T(8,128)(2,1)S(1)}, bf16[80,2048]{1,0:T(8,128)(2,1)S(1)}, u32[]{:S(2)}, u32[]{:S(2)}) %collective-permute-start.44) | collective-permute-done | bytes 327712 | tf_op jit(solution)/shard_map/ppermute | solution.py:24
  (89 shorter events, 9.6 us)
Async XLA Ops:
  0.6 32.3 %collective-permute-start.10 = (bf16[256,2048]{1,0:T(8,128)(2,1)}, bf16[256,2048]{1,0:T(8,128)(2,1)S(1)}, u32[]{:S(2)}, u32[]{:S(2)}) collective-permute-start(bf16[256,2048]{1,0:T(8,128)(2,1)} %refs_9_.7), channel_id=1, source_target_pairs={{0,2},{1,3},{2,0},{3,1},{4,6},{5,7},{6,4},{7,5},{8,10},{9,11},{10,... | collective-permute-start | bytes 3145736 | tf_op jit(solution)/shard_map/ppermute | solution.py:24
  7.5 14.0 %collective-permute-start = (bf16[1136,128]{1,0:T(8,128)(2,1)}, bf16[1136,128]{1,0:T(8,128)(2,1)S(1)}, u32[]{:S(2)}, u32[]{:S(2)}) collective-permute-start(bf16[1136,128]{1,0:T(8,128)(2,1)} %get-tuple-element.32), channel_id=1, source_target_pairs={{0,4},{1,5},{2,6},{3,7},{4,0},{5,1},{6,2},{7,3},{8,12},{9,13},{10,... | collective-permute-start | bytes 872456 | tf_op jit(solution)/shard_map/ppermute | solution.py:24
  9.2 23.4 %collective-permute-start.4 = (bf16[1136,128]{1,0:T(8,128)(2,1)}, bf16[1136,128]{1,0:T(8,128)(2,1)S(1)}, u32[]{:S(2)}, u32[]{:S(2)}) collective-permute-start(bf16[1136,128]{1,0:T(8,128)(2,1)} %get-tuple-element.33), channel_id=1, source_target_pairs={{0,8},{1,9},{2,10},{3,11},{4,12},{5,13},{6,14},{7,15},{8,0},{9,1},... | collective-permute-start | bytes 872456 | tf_op jit(solution)/shard_map/ppermute | solution.py:24
  11.8 20.8 %collective-permute-start.5 = (bf16[1136,128]{1,0:T(8,128)(2,1)}, bf16[1136,128]{1,0:T(8,128)(2,1)S(1)}, u32[]{:S(2)}, u32[]{:S(2)}) collective-permute-start(bf16[1136,128]{1,0:T(8,128)(2,1)} %get-tuple-element.34), channel_id=1, source_target_pairs={{0,12},{1,13},{2,14},{3,15},{4,8},{5,9},{6,10},{7,11},{8,4},{9,5},... | collective-permute-start | bytes 872456 | tf_op jit(solution)/shard_map/ppermute | solution.py:24
  22.7 9.9 %collective-permute-start.2 = (bf16[672,128]{1,0:T(8,128)(2,1)S(1)}, bf16[672,128]{1,0:T(8,128)(2,1)S(1)}, u32[]{:S(2)}, u32[]{:S(2)}) collective-permute-start(bf16[672,128]{1,0:T(8,128)(2,1)S(1)} %merge.2.refs_1_), channel_id=1, source_target_pairs={{0,2},{1,3},{2,0},{3,1},{4,6},{5,7},{6,4},{7,5},{8,10},{9,11},{10,... | collective-permute-start | bytes 516104 | tf_op jit(solution)/shard_map/ppermute | solution.py:24
  23.1 18.1 %collective-permute-start.9 = (bf16[256,2048]{1,0:T(8,128)(2,1)}, bf16[256,2048]{1,0:T(8,128)(2,1)S(1)}, u32[]{:S(2)}, u32[]{:S(2)}) collective-permute-start(bf16[256,2048]{1,0:T(8,128)(2,1)} %refs_9_.7), channel_id=1, source_target_pairs={{0,1},{1,0},{2,3},{3,2},{4,5},{5,4},{6,7},{7,6},{8,9},{9,8},{10,11... | collective-permute-start | bytes 3145736 | tf_op jit(solution)/shard_map/ppermute | solution.py:24
  32.9 8.3 %collective-permute-start.11 = (bf16[256,2048]{1,0:T(8,128)(2,1)S(1)}, bf16[256,2048]{1,0:T(8,128)(2,1)S(1)}, u32[]{:S(2)}, u32[]{:S(2)}) collective-permute-start(bf16[256,2048]{1,0:T(8,128)(2,1)S(1)} %collective-permute-done.10.refs_11_), channel_id=1, source_target_pairs={{0,1},{1,0},{2,3},{3,2},{4,5},{5,4},{6,7},{7,6},{8,9},{9,8},{10,11... | collective-permute-start | bytes 3145736 | tf_op jit(solution)/shard_map/ppermute | solution.py:24
  33.0 2.9 %collective-permute-start.1 = (bf16[672,128]{1,0:T(8,128)(2,1)S(1)}, bf16[672,128]{1,0:T(8,128)(2,1)S(1)}, u32[]{:S(2)}, u32[]{:S(2)}) collective-permute-start(bf16[672,128]{1,0:T(8,128)(2,1)S(1)} %merge.2.refs_1_), channel_id=1, source_target_pairs={{0,1},{1,0},{2,3},{3,2},{4,5},{5,4},{6,7},{7,6},{8,9},{9,8},{10,11... | collective-permute-start | bytes 516104 | tf_op jit(solution)/shard_map/ppermute | solution.py:24
  33.5 6.4 %collective-permute-start.7 = (bf16[672,128]{1,0:T(8,128)(2,1)S(1)}, bf16[672,128]{1,0:T(8,128)(2,1)S(1)}, u32[]{:S(2)}, u32[]{:S(2)}) collective-permute-start(bf16[672,128]{1,0:T(8,128)(2,1)S(1)} %merge.3.refs_5_), channel_id=1, source_target_pairs={{0,2},{1,3},{2,0},{3,1},{4,6},{5,7},{6,4},{7,5},{8,10},{9,11},{10,... | collective-permute-start | bytes 516104 | tf_op jit(solution)/shard_map/ppermute | solution.py:24
  34.0 5.9 %collective-permute-start.6 = (bf16[672,128]{1,0:T(8,128)(2,1)S(1)}, bf16[672,128]{1,0:T(8,128)(2,1)S(1)}, u32[]{:S(2)}, u32[]{:S(2)}) collective-permute-start(bf16[672,128]{1,0:T(8,128)(2,1)S(1)} %merge.3.refs_5_), channel_id=1, source_target_pairs={{0,1},{1,0},{2,3},{3,2},{4,5},{5,4},{6,7},{7,6},{8,9},{9,8},{10,11... | collective-permute-start | bytes 516104 | tf_op jit(solution)/shard_map/ppermute | solution.py:24
  35.9 4.0 %collective-permute-start.3 = (bf16[672,128]{1,0:T(8,128)(2,1)S(1)}, bf16[672,128]{1,0:T(8,128)(2,1)S(1)}, u32[]{:S(2)}, u32[]{:S(2)}) collective-permute-start(bf16[672,128]{1,0:T(8,128)(2,1)S(1)} %collective-permute-done.2.refs_2_.refs_3_), channel_id=1, source_target_pairs={{0,1},{1,0},{2,3},{3,2},{4,5},{5,4},{6,7},{7,6},{8,9},{9,8},{10,11... | collective-permute-start | bytes 516104 | tf_op jit(solution)/shard_map/ppermute | solution.py:24
  39.8 1.4 collective-permute-start.8
  45.8 48.5 %slice-start = ((s8[12582912]{0:T(1024)(128)(4,1)}), s8[4194304]{0:T(1024)(128)(4,1)S(1)}, s32[]{:S(2)}) async-start(s8[12582912]{0:T(1024)(128)(4,1)} %bitcast.6), calls=%async_computation | async-start | bytes 8388608
  45.8 48.5 %slice-start.3 = ((s8[6291456]{0:T(1024)(128)(4,1)}), s8[4194304]{0:T(1024)(128)(4,1)S(1)}, s32[]{:S(2)}) async-start(s8[6291456]{0:T(1024)(128)(4,1)} %bitcast.8), calls=%async_computation.3 | async-start | bytes 8388608
  45.8 13.1 %collective-permute-start.12 = (bf16[80,2048]{1,0:T(8,128)(2,1)S(1)}, bf16[80,2048]{1,0:T(8,128)(2,1)S(1)}, u32[]{:S(2)}, u32[]{:S(2)}) collective-permute-start(bf16[80,2048]{1,0:T(8,128)(2,1)S(1)} %attention.4.refs_13_), channel_id=1, source_target_pairs={{0,4},{1,5},{2,6},{3,7},{4,0},{5,1},{6,2},{7,3},{8,12},{9,13},{10,... | collective-permute-start | bytes 983048 | tf_op jit(solution)/shard_map/ppermute | solution.py:24
  54.3 40.1 %slice-start.1 = ((s8[12582912]{0:T(1024)(128)(4,1)}), s8[4194304]{0:T(1024)(128)(4,1)S(1)}, s32[]{:S(2)}) async-start(s8[12582912]{0:T(1024)(128)(4,1)} %bitcast.6), calls=%async_computation.1 | async-start | bytes 8388608
  57.6 15.5 %collective-permute-start.13 = (bf16[80,2048]{1,0:T(8,128)(2,1)S(1)}, bf16[80,2048]{1,0:T(8,128)(2,1)S(1)}, u32[]{:S(2)}, u32[]{:S(2)}) collective-permute-start(bf16[80,2048]{1,0:T(8,128)(2,1)S(1)} %attention.6.refs_2_), channel_id=1, source_target_pairs={{0,4},{1,5},{2,6},{3,7},{4,0},{5,1},{6,2},{7,3},{8,12},{9,13},{10,... | collective-permute-start | bytes 983048 | tf_op jit(solution)/shard_map/ppermute | solution.py:24
  59.1 17.3 %collective-permute-start.14 = (bf16[80,2048]{1,0:T(8,128)(2,1)S(1)}, bf16[80,2048]{1,0:T(8,128)(2,1)S(1)}, u32[]{:S(2)}, u32[]{:S(2)}) collective-permute-start(bf16[80,2048]{1,0:T(8,128)(2,1)S(1)} %add.17.refs_13_), channel_id=1, source_target_pairs={{0,8},{1,9},{2,10},{3,11},{4,12},{5,13},{6,14},{7,15},{8,0},{9,1},... | collective-permute-start | bytes 983048 | tf_op jit(solution)/shard_map/ppermute | solution.py:24
  77.3 7.1 %collective-permute-start.16 = (bf16[80,2048]{1,0:T(8,128)(2,1)S(1)}, bf16[80,2048]{1,0:T(8,128)(2,1)S(1)}, u32[]{:S(2)}, u32[]{:S(2)}) collective-permute-start(bf16[80,2048]{1,0:T(8,128)(2,1)S(1)} %get-tuple-element.38.refs_0_), channel_id=1, source_target_pairs={{0,2},{1,3},{2,0},{3,1},{4,6},{5,7},{6,4},{7,5},{8,10},{9,11},{10,... | collective-permute-start | bytes 983048 | tf_op jit(solution)/shard_map/ppermute | solution.py:24
  77.8 13.4 %collective-permute-start.20 = (bf16[80,2048]{1,0:T(8,128)(2,1)S(1)}, bf16[80,2048]{1,0:T(8,128)(2,1)S(1)}, u32[]{:S(2)}, u32[]{:S(2)}) collective-permute-start(bf16[80,2048]{1,0:T(8,128)(2,1)S(1)} %get-tuple-element.38.refs_0_), channel_id=1, source_target_pairs={{0,4},{1,5},{2,6},{3,7},{4,0},{5,1},{6,2},{7,3},{8,12},{9,13},{10,... | collective-permute-start | bytes 983048 | tf_op jit(solution)/shard_map/ppermute | solution.py:24
  77.8 16.3 %collective-permute-start.24 = (bf16[80,2048]{1,0:T(8,128)(2,1)S(1)}, bf16[80,2048]{1,0:T(8,128)(2,1)S(1)}, u32[]{:S(2)}, u32[]{:S(2)}) collective-permute-start(bf16[80,2048]{1,0:T(8,128)(2,1)S(1)} %get-tuple-element.38.refs_0_), channel_id=1, source_target_pairs={{0,8},{1,9},{2,10},{3,11},{4,12},{5,13},{6,14},{7,15},{8,0},{9,1},... | collective-permute-start | bytes 983048 | tf_op jit(solution)/shard_map/ppermute | solution.py:24
  80.8 13.5 %collective-permute-start.15 = (bf16[80,2048]{1,0:T(8,128)(2,1)S(1)}, bf16[80,2048]{1,0:T(8,128)(2,1)S(1)}, u32[]{:S(2)}, u32[]{:S(2)}) collective-permute-start(bf16[80,2048]{1,0:T(8,128)(2,1)S(1)} %get-tuple-element.38.refs_0_), channel_id=1, source_target_pairs={{0,1},{1,0},{2,3},{3,2},{4,5},{5,4},{6,7},{7,6},{8,9},{9,8},{10,11... | collective-permute-start | bytes 983048 | tf_op jit(solution)/shard_map/ppermute | solution.py:24
  84.4 9.9 %collective-permute-start.17 = (bf16[80,2048]{1,0:T(8,128)(2,1)S(1)}, bf16[80,2048]{1,0:T(8,128)(2,1)S(1)}, u32[]{:S(2)}, u32[]{:S(2)}) collective-permute-start(bf16[80,2048]{1,0:T(8,128)(2,1)S(1)} %collective-permute-done.16.refs_2_), channel_id=1, source_target_pairs={{0,1},{1,0},{2,3},{3,2},{4,5},{5,4},{6,7},{7,6},{8,9},{9,8},{10,11... | collective-permute-start | bytes 983048 | tf_op jit(solution)/shard_map/ppermute | solution.py:24
  91.2 7.1 %collective-permute-start.22 = (bf16[80,2048]{1,0:T(8,128)(2,1)S(1)}, bf16[80,2048]{1,0:T(8,128)(2,1)S(1)}, u32[]{:S(2)}, u32[]{:S(2)}) collective-permute-start(bf16[80,2048]{1,0:T(8,128)(2,1)S(1)} %collective-permute-done.20.refs_0_), channel_id=1, source_target_pairs={{0,2},{1,3},{2,0},{3,1},{4,6},{5,7},{6,4},{7,5},{8,10},{9,11},{10,... | collective-permute-start | bytes 983048 | tf_op jit(solution)/shard_map/ppermute | solution.py:24
  94.1 7.1 %collective-permute-start.29 = (bf16[80,2048]{1,0:T(8,128)(2,1)S(1)}, bf16[80,2048]{1,0:T(8,128)(2,1)S(1)}, u32[]{:S(2)}, u32[]{:S(2)}) collective-permute-start(bf16[80,2048]{1,0:T(8,128)(2,1)S(1)} %collective-permute-done.24.refs_10_.refs_0_), channel_id=1, source_target_pairs={{0,4},{1,5},{2,6},{3,7},{4,0},{5,1},{6,2},{7,3},{8,12},{9,13},{10,... | collective-permute-start | bytes 983048 | tf_op jit(solution)/shard_map/ppermute | solution.py:24
  94.3 8.4 %collective-permute-start.21 = (bf16[80,2048]{1,0:T(8,128)(2,1)S(1)}, bf16[80,2048]{1,0:T(8,128)(2,1)S(1)}, u32[]{:S(2)}, u32[]{:S(2)}) collective-permute-start(bf16[80,2048]{1,0:T(8,128)(2,1)S(1)} %collective-permute-done.20.refs_0_), channel_id=1, source_target_pairs={{0,1},{1,0},{2,3},{3,2},{4,5},{5,4},{6,7},{7,6},{8,9},{9,8},{10,11... | collective-permute-start | bytes 983048 | tf_op jit(solution)/shard_map/ppermute | solution.py:24
  98.3 4.4 %collective-permute-start.23 = (bf16[80,2048]{1,0:T(8,128)(2,1)S(1)}, bf16[80,2048]{1,0:T(8,128)(2,1)S(1)}, u32[]{:S(2)}, u32[]{:S(2)}) collective-permute-start(bf16[80,2048]{1,0:T(8,128)(2,1)S(1)} %collective-permute-done.22.refs_2_), channel_id=1, source_target_pairs={{0,1},{1,0},{2,3},{3,2},{4,5},{5,4},{6,7},{7,6},{8,9},{9,8},{10,11... | collective-permute-start | bytes 983048 | tf_op jit(solution)/shard_map/ppermute | solution.py:24
  101.1 7.3 %collective-permute-start.31 = (bf16[80,2048]{1,0:T(8,128)(2,1)S(1)}, bf16[80,2048]{1,0:T(8,128)(2,1)S(1)}, u32[]{:S(2)}, u32[]{:S(2)}) collective-permute-start(bf16[80,2048]{1,0:T(8,128)(2,1)S(1)} %collective-permute-done.29.refs_0_), channel_id=1, source_target_pairs={{0,2},{1,3},{2,0},{3,1},{4,6},{5,7},{6,4},{7,5},{8,10},{9,11},{10,... | collective-permute-start | bytes 983048 | tf_op jit(solution)/shard_map/ppermute | solution.py:24
  102.7 7.5 %collective-permute-start.30 = (bf16[80,2048]{1,0:T(8,128)(2,1)S(1)}, bf16[80,2048]{1,0:T(8,128)(2,1)S(1)}, u32[]{:S(2)}, u32[]{:S(2)}) collective-permute-start(bf16[80,2048]{1,0:T(8,128)(2,1)S(1)} %collective-permute-done.29.refs_0_), channel_id=1, source_target_pairs={{0,1},{1,0},{2,3},{3,2},{4,5},{5,4},{6,7},{7,6},{8,9},{9,8},{10,11... | collective-permute-start | bytes 983048 | tf_op jit(solution)/shard_map/ppermute | solution.py:24
  108.4 1.8 %collective-permute-start.32 = (bf16[80,2048]{1,0:T(8,128)(2,1)S(1)}, bf16[80,2048]{1,0:T(8,128)(2,1)S(1)}, u32[]{:S(2)}, u32[]{:S(2)}) collective-permute-start(bf16[80,2048]{1,0:T(8,128)(2,1)S(1)} %collective-permute-done.31.refs_2_), channel_id=1, source_target_pairs={{0,1},{1,0},{2,3},{3,2},{4,5},{5,4},{6,7},{7,6},{8,9},{9,8},{10,11... | collective-permute-start | bytes 983048 | tf_op jit(solution)/shard_map/ppermute | solution.py:24
  108.4 10.1 %collective-permute-start.28 = (bf16[80,2048]{1,0:T(8,128)(2,1)S(1)}, bf16[80,2048]{1,0:T(8,128)(2,1)S(1)}, u32[]{:S(2)}, u32[]{:S(2)}) collective-permute-start(bf16[80,2048]{1,0:T(8,128)(2,1)S(1)} %collective-permute-done.24.refs_10_.refs_0_), channel_id=1, source_target_pairs={{0,2},{1,3},{2,0},{3,1},{4,6},{5,7},{6,4},{7,5},{8,10},{9,11},{10,... | collective-permute-start | bytes 983048 | tf_op jit(solution)/shard_map/ppermute | solution.py:24
  110.0 8.7 %collective-permute-start.27 = (bf16[80,2048]{1,0:T(8,128)(2,1)S(1)}, bf16[80,2048]{1,0:T(8,128)(2,1)S(1)}, u32[]{:S(2)}, u32[]{:S(2)}) collective-permute-start(bf16[80,2048]{1,0:T(8,128)(2,1)S(1)} %collective-permute-done.24.refs_10_.refs_0_), channel_id=1, source_target_pairs={{0,1},{1,0},{2,3},{3,2},{4,5},{5,4},{6,7},{7,6},{8,9},{9,8},{10,11... | collective-permute-start | bytes 983048 | tf_op jit(solution)/shard_map/ppermute | solution.py:24
  113.9 4.7 %collective-permute-start.34 = (bf16[80,2048]{1,0:T(8,128)(2,1)S(1)}, bf16[80,2048]{1,0:T(8,128)(2,1)S(1)}, u32[]{:S(2)}, u32[]{:S(2)}) collective-permute-start(bf16[80,2048]{1,0:T(8,128)(2,1)S(1)} %get-tuple-element.54), channel_id=1, source_target_pairs={{0,1},{1,0},{2,3},{3,2},{4,5},{5,4},{6,7},{7,6},{8,9},{9,8},{10,11... | collective-permute-start | bytes 983048 | tf_op jit(solution)/shard_map/ppermute | solution.py:24
  118.6 1.6 collective-permute-start.33
  124.1 2.1 %collective-permute-start.36 = (bf16[80,2048]{1,0:T(8,128)(2,1)S(1)}, bf16[80,2048]{1,0:T(8,128)(2,1)S(1)}, u32[]{:S(2)}, u32[]{:S(2)}) collective-permute-start(bf16[80,2048]{1,0:T(8,128)(2,1)S(1)} %get-tuple-element.58), channel_id=1, source_target_pairs={{0,1},{1,0},{2,3},{3,2},{4,5},{5,4},{6,7},{7,6},{8,9},{9,8},{10,11... | collective-permute-start | bytes 983048 | tf_op jit(solution)/shard_map/ppermute | solution.py:24
  124.3 3.2 %collective-permute-start.38 = (bf16[80,2048]{1,0:T(8,128)(2,1)S(1)}, bf16[80,2048]{1,0:T(8,128)(2,1)S(1)}, u32[]{:S(2)}, u32[]{:S(2)}) collective-permute-start(bf16[80,2048]{1,0:T(8,128)(2,1)S(1)} %get-tuple-element.59), channel_id=1, source_target_pairs={{0,1},{1,0},{2,3},{3,2},{4,5},{5,4},{6,7},{7,6},{8,9},{9,8},{10,11... | collective-permute-start | bytes 983048 | tf_op jit(solution)/shard_map/ppermute | solution.py:24
  124.7 10.6 %collective-permute-start.39 = (bf16[80,2048]{1,0:T(8,128)(2,1)S(1)}, bf16[80,2048]{1,0:T(8,128)(2,1)S(1)}, u32[]{:S(2)}, u32[]{:S(2)}) collective-permute-start(bf16[80,2048]{1,0:T(8,128)(2,1)S(1)} %add.18.refs_9_), channel_id=1, source_target_pairs={{0,2},{1,3},{2,0},{3,1},{4,6},{5,7},{6,4},{7,5},{8,10},{9,11},{10,... | collective-permute-start | bytes 983048 | tf_op jit(solution)/shard_map/ppermute | solution.py:24
  126.2 11.5 %collective-permute-start.35 = (bf16[80,2048]{1,0:T(8,128)(2,1)S(1)}, bf16[80,2048]{1,0:T(8,128)(2,1)S(1)}, u32[]{:S(2)}, u32[]{:S(2)}) collective-permute-start(bf16[80,2048]{1,0:T(8,128)(2,1)S(1)} %get-tuple-element.56), channel_id=1, source_target_pairs={{0,1},{1,0},{2,3},{3,2},{4,5},{5,4},{6,7},{7,6},{8,9},{9,8},{10,11... | collective-permute-start | bytes 983048 | tf_op jit(solution)/shard_map/ppermute | solution.py:24
  126.3 15.2 %collective-permute-start.37 = (bf16[80,2048]{1,0:T(8,128)(2,1)S(1)}, bf16[80,2048]{1,0:T(8,128)(2,1)S(1)}, u32[]{:S(2)}, u32[]{:S(2)}) collective-permute-start(bf16[80,2048]{1,0:T(8,128)(2,1)S(1)} %add.19.refs_4_), channel_id=1, source_target_pairs={{0,2},{1,3},{2,0},{3,1},{4,6},{5,7},{6,4},{7,5},{8,10},{9,11},{10,... | collective-permute-start | bytes 983048 | tf_op jit(solution)/shard_map/ppermute | solution.py:24
  135.4 8.2 %collective-permute-start.40 = (bf16[80,2048]{1,0:T(8,128)(2,1)S(1)}, bf16[80,2048]{1,0:T(8,128)(2,1)S(1)}, u32[]{:S(2)}, u32[]{:S(2)}) collective-permute-start(bf16[80,2048]{1,0:T(8,128)(2,1)S(1)} %add.20), channel_id=1, source_target_pairs={{0,4},{1,5},{2,6},{3,7},{4,0},{5,1},{6,2},{7,3},{8,12},{9,13},{10,... | collective-permute-start | bytes 983048 | tf_op jit(solution)/shard_map/ppermute | solution.py:24
  137.1 6.6 %collective-permute-start.26 = (bf16[80,2048]{1,0:T(8,128)(2,1)S(1)}, bf16[80,2048]{1,0:T(8,128)(2,1)S(1)}, u32[]{:S(2)}, u32[]{:S(2)}) collective-permute-start(bf16[80,2048]{1,0:T(8,128)(2,1)S(1)} %get-tuple-element.49), channel_id=1, source_target_pairs={{0,1},{1,0},{2,3},{3,2},{4,5},{5,4},{6,7},{7,6},{8,9},{9,8},{10,11... | collective-permute-start | bytes 983048 | tf_op jit(solution)/shard_map/ppermute | solution.py:24
  137.2 12.1 %collective-permute-start.25 = (bf16[80,2048]{1,0:T(8,128)(2,1)S(1)}, bf16[80,2048]{1,0:T(8,128)(2,1)S(1)}, u32[]{:S(2)}, u32[]{:S(2)}) collective-permute-start(bf16[80,2048]{1,0:T(8,128)(2,1)S(1)} %get-tuple-element.47), channel_id=1, source_target_pairs={{0,1},{1,0},{2,3},{3,2},{4,5},{5,4},{6,7},{7,6},{8,9},{9,8},{10,11... | collective-permute-start | bytes 983048 | tf_op jit(solution)/shard_map/ppermute | solution.py:24
  143.8 7.3 %collective-permute-start.41 = (bf16[80,2048]{1,0:T(8,128)(2,1)S(1)}, bf16[80,2048]{1,0:T(8,128)(2,1)S(1)}, u32[]{:S(2)}, u32[]{:S(2)}) collective-permute-start(bf16[80,2048]{1,0:T(8,128)(2,1)S(1)} %add.22.refs_3_), channel_id=1, source_target_pairs={{0,2},{1,3},{2,0},{3,1},{4,6},{5,7},{6,4},{7,5},{8,10},{9,11},{10,... | collective-permute-start | bytes 983048 | tf_op jit(solution)/shard_map/ppermute | solution.py:24
  145.4 7.6 %collective-permute-start.19 = (bf16[80,2048]{1,0:T(8,128)(2,1)S(1)}, bf16[80,2048]{1,0:T(8,128)(2,1)S(1)}, u32[]{:S(2)}, u32[]{:S(2)}) collective-permute-start(bf16[80,2048]{1,0:T(8,128)(2,1)S(1)} %get-tuple-element.44), channel_id=1, source_target_pairs={{0,1},{1,0},{2,3},{3,2},{4,5},{5,4},{6,7},{7,6},{8,9},{9,8},{10,11... | collective-permute-start | bytes 983048 | tf_op jit(solution)/shard_map/ppermute | solution.py:24
  145.4 9.4 %collective-permute-start.18 = (bf16[80,2048]{1,0:T(8,128)(2,1)S(1)}, bf16[80,2048]{1,0:T(8,128)(2,1)S(1)}, u32[]{:S(2)}, u32[]{:S(2)}) collective-permute-start(bf16[80,2048]{1,0:T(8,128)(2,1)S(1)} %get-tuple-element.42), channel_id=1, source_target_pairs={{0,1},{1,0},{2,3},{3,2},{4,5},{5,4},{6,7},{7,6},{8,9},{9,8},{10,11... | collective-permute-start | bytes 983048 | tf_op jit(solution)/shard_map/ppermute | solution.py:24
  145.9 18.3 %collective-permute-start.44 = (bf16[80,2048]{1,0:T(8,128)(2,1)S(1)}, bf16[80,2048]{1,0:T(8,128)(2,1)S(1)}, u32[]{:S(2)}, u32[]{:S(2)}) collective-permute-start(bf16[80,2048]{1,0:T(8,128)(2,1)S(1)} %add.21.refs_2_), channel_id=1, source_target_pairs={{0,8},{1,9},{2,10},{3,11},{4,12},{5,13},{6,14},{7,15},{8,0},{9,1},... | collective-permute-start | bytes 983048 | tf_op jit(solution)/shard_map/ppermute | solution.py:24
  151.2 13.3 %collective-permute-start.43 = (bf16[80,2048]{1,0:T(8,128)(2,1)S(1)}, bf16[80,2048]{1,0:T(8,128)(2,1)S(1)}, u32[]{:S(2)}, u32[]{:S(2)}) collective-permute-start(bf16[80,2048]{1,0:T(8,128)(2,1)S(1)} %add.23.refs_2_), channel_id=1, source_target_pairs={{0,4},{1,5},{2,6},{3,7},{4,0},{5,1},{6,2},{7,3},{8,12},{9,13},{10,... | collective-permute-start | bytes 983048 | tf_op jit(solution)/shard_map/ppermute | solution.py:24
  153.1 11.4 %collective-permute-start.42 = (bf16[80,2048]{1,0:T(8,128)(2,1)S(1)}, bf16[80,2048]{1,0:T(8,128)(2,1)S(1)}, u32[]{:S(2)}, u32[]{:S(2)}) collective-permute-start(bf16[80,2048]{1,0:T(8,128)(2,1)S(1)} %add.24), channel_id=1, source_target_pairs={{0,2},{1,3},{2,0},{3,1},{4,6},{5,7},{6,4},{7,5},{8,10},{9,11},{10,... | collective-permute-start | bytes 983048 | tf_op jit(solution)/shard_map/ppermute | solution.py:24
  (8 other events, 198.0 us)

commit v3 on v2

--- a/solution.py
+++ b/solution.py
@@ -17,20 +17,26 @@
 NT = (((1,), (1,)), ((), ()))
 ANY = pl.BlockSpec(memory_space=pl.ANY)
 VMEM = pl.BlockSpec(memory_space=pltpu.VMEM)
-SMEM = pl.BlockSpec(memory_space=pltpu.SMEM)
 
 
 def swap(array, n, offset):
     return lax.ppermute(array, "ctx", [(i, i ^ offset) for i in range(n)])
 
 
-def gather_inner(array, n, *tokens):
+def after(array, *tokens):
+    return lax.optimization_barrier((array, *tokens))[0]
+
+
+def gather_inner(array, n, *tokens, far=None):
     pieces = {0: array}
     bit = n // OUTERS // 2
+    if far is not None:
+        pieces[bit] = far
     while bit:
         for j in list(pieces):
-            ready = lax.optimization_barrier((pieces[j], *tokens))[0] if j and tokens else pieces[j]
-            pieces[j | bit] = swap(ready, n, bit)
+            if j | bit not in pieces:
+                ready = after(pieces[j], *tokens) if j and tokens else pieces[j]
+                pieces[j | bit] = swap(ready, n, bit)
         bit //= 2
     return [pieces[j] for j in range(n // OUTERS)]
 
@@ -81,18 +87,19 @@
         copy.wait()
 
 
-def pack_kernel(inner, spot, *refs):
-    sources, refs = refs[:6], refs[6:]
-    outs, made = refs[:OUTERS], refs[OUTERS : 2 * OUTERS]
-    queries, fresh, cache, ids, weights, placement, sems, last = refs[2 * OUTERS :]
-    landed = (queries, fresh, cache, ids, weights, placement)
-    copies = start_all(list(zip(sources, landed))[::-1], sems)[::-1]
-    wait_all(copies[2:])
-    outer, place = spot[0], spot[1]
-    rows = queries.shape[0]
+def place_of(inner):
+    me = lax.axis_index("ctx")
+    return lax.div(me, inner), lax.rem(me, inner)
+
+
+def pack_cache_kernel(inner, *refs):
+    sources, outs, made = refs[:4], refs[4 : 4 + OUTERS], refs[4 + OUTERS : 4 + 2 * OUTERS]
+    cache, ids, weights, placement, sems, last = refs[4 + 2 * OUTERS :]
+    copies = start_all(list(zip(sources, (cache, ids, weights, placement))), sems)
+    outer, _ = place_of(inner)
+    wait_all(copies[1:])
     keys = cache.shape[1]
-    group = queries.shape[1] // (OUTERS * HEAD_SIZE)
-    per_device = group // inner
+    rows = ids.shape[1]
     experts = placement.shape[1]
     part = experts // OUTERS
     share = weights[...] / jnp.sum(weights[...], axis=0, keepdims=True)
@@ -100,14 +107,12 @@
     gates = jnp.zeros((experts, rows), F32)
     for k in range(ids.shape[0]):
         gates += jnp.where(ids[k : k + 1, :] == expert, share[k : k + 1, :], 0.0)
-    gates = gates.T
     high = gates.astype(BF16)
     low = (gates - high.astype(F32)).astype(BF16)
-    lane = lax.broadcasted_iota(jnp.int32, (LANES, experts), 0)
-    slot = jnp.broadcast_to(placement[...], (LANES, experts))
-    half = LANES // 2
+    place = lax.broadcasted_iota(jnp.int32, (2 * part, experts), 0)
+    slot = jnp.broadcast_to(placement[...], (2 * part, experts))
+    wait_all(copies[:1])
     sent = []
-    wait_all(copies[:2])
     for k in [1, 2, 3, 0]:
         to = outer ^ k
         block = made[k]
@@ -115,21 +120,40 @@
         block[0:keys, :] = cache[0, :, column]
         block[keys : 2 * keys, :] = cache[1, :, column]
         first = to * part
-        pick_high = jnp.where((slot == first + lane) & (lane < part), 1.0, 0.0)
-        pick_low = jnp.where(
-            (slot == first + lane - half) & (lane >= half) & (lane < half + part), 1.0, 0.0
-        )
-        wanted = lax.dot_general(
-            high, pick_high.astype(BF16), NT, preferred_element_type=F32
-        ) + lax.dot_general(low, pick_low.astype(BF16), NT, preferred_element_type=F32)
-        at = 2 * keys + rows
-        block[2 * keys : at, :] = wanted.astype(BF16)
+        pick_high = jnp.where((slot == first + place) & (place < part), 1.0, 0.0).astype(BF16)
+        pick_low = jnp.where((slot == first + place - part) & (place >= part), 1.0, 0.0)
+        wanted = jnp.dot(pick_high, high, preferred_element_type=F32) + jnp.dot(
+            pick_low.astype(BF16), low, preferred_element_type=F32
+        )
+        block[2 * keys :, :rows] = wanted.astype(BF16)
+        block[2 * keys :, rows:] = jnp.zeros((2 * part, LANES - rows), BF16)
+        copy = pltpu.make_async_copy(block, outs[k], last.at[k])
+        copy.start()
+        sent.append(copy)
+    wait_all(sent)
+
+
+def pack_queries_kernel(inner, *refs):
+    sources, outs, made = refs[:2], refs[2 : 2 + OUTERS], refs[2 + OUTERS : 2 + 2 * OUTERS]
+    queries, fresh, sems, last = refs[2 + 2 * OUTERS :]
+    copies = start_all(list(zip(sources, (queries, fresh))), sems)
+    outer, place = place_of(inner)
+    rows = queries.shape[0]
+    group = queries.shape[1] // (OUTERS * HEAD_SIZE)
+    per_device = group // inner
+    wait_all(copies)
+    sent = []
+    for k in [3, 2, 1, 0]:
+        to = outer ^ k
+        block = made[k]
+        at = 0
         for h in range(group):
             head = to * group + (place ^ (h // per_device)) * per_device + h % per_device
             block[at : at + rows, :] = queries[
                 :, pl.ds(pl.multiple_of(head * HEAD_SIZE, HEAD_SIZE), HEAD_SIZE)
             ]
             at += rows
+        column = pl.ds(pl.multiple_of(to * HEAD_SIZE, HEAD_SIZE), HEAD_SIZE)
         block[at : at + rows, :] = fresh[0, :, column]
         block[at + rows :, :] = fresh[1, :, column]
         copy = pltpu.make_async_copy(block, outs[k], last.at[k])
@@ -138,14 +162,15 @@
     wait_all(sent)
 
 
-def merge_kernel(keys, rows, *refs):
+def merge_kernel(keys, *refs):
     blocks, out, sems = refs[:-2], refs[-2], refs[-1]
+    gates = blocks[0].shape[0] - 2 * keys
     count = len(blocks)
-    start = count * rows
+    start = count * gates
     pairs = []
     for k in range(count):
         for at, size, to in (
-            (2 * keys, rows, k * rows),
+            (2 * keys, gates, k * gates),
             (0, keys, start + k * keys),
             (keys, keys, start + (count + k) * keys),
         ):
@@ -153,7 +178,7 @@
     wait_all(start_all(pairs, sems))
 
 
-def attention_kernel(inner, group, rows, packed, *refs):
+def attention_kernel(inner, group, rows, qf, *refs):
     caches, projections = refs[: 2 * inner], refs[2 * inner : 3 * inner]
     out, keys, values, attention = refs[3 * inner :]
     block = keys.shape[0] // (2 * inner)
@@ -162,7 +187,6 @@
         keys[j * block : (j + 1) * block, :] = caches[j][start : start + block, :]
         values[j * block : (j + 1) * block, :] = caches[j][start + block :, :]
     factor = HEAD_SIZE ** (-0.5) * math.log2(math.e)
-    qf = packed.at[pl.ds(packed.shape[0] - (group + 2) * rows, (group + 2) * rows)]
     own_key = qf[group * rows : (group + 1) * rows, :].astype(F32)
     own_value = qf[(group + 1) * rows :, :].astype(F32)
     step = max(1, group // 2)
@@ -198,14 +222,23 @@
         out[:, c : c + wide] = total.astype(out.dtype)
 
 
-def select_kernel(inner, local, capacity, spot, *refs):
+def select_kernel(inner, local, capacity, count, *refs):
     gates, (sel, selt, share) = refs[: 2 * inner], refs[2 * inner :]
     early = pl.program_id(0) < OUTERS // 2
-    table = jnp.concatenate(
-        [jnp.where(early, gates[j][...], gates[inner + j][...]) for j in halves(inner)], axis=0
-    )
+    part = gates[0].shape[0] // 2
+    spread = (
+        lax.broadcasted_iota(jnp.int32, (2 * part, LANES), 0)
+        == lax.broadcasted_iota(jnp.int32, (2 * part, LANES), 1)
+    ).astype(F32)
+    turn = (((0,), (0,)), ((), ()))
+    pieces = []
+    for j in halves(inner):
+        block = jnp.where(early, gates[j][...], gates[inner + j][...])
+        turned = lax.dot_general(block, spread.astype(BF16), turn, preferred_element_type=F32)
+        pieces.append(turned.astype(BF16)[:count, :])
+    table = jnp.concatenate(pieces, axis=0)
     rows = table.shape[0]
-    first = spot[1] * local
+    first = place_of(inner)[1] * local
     lane = lax.broadcasted_iota(jnp.int32, (LANES, LANES), 1)
     sub = lax.broadcasted_iota(jnp.int32, (LANES, LANES), 0)
     pick = jnp.where((lane == first + sub) & (sub < local), 1.0, 0.0).astype(BF16)
@@ -225,14 +258,14 @@
     down_rank = jnp.where(down > 0, down_rank, 0.0)
     place = lax.broadcasted_iota(jnp.int32, (capacity, rows), 0).astype(F32) + 1.0
     place_t = lax.broadcasted_iota(jnp.int32, (rows, capacity), 1).astype(F32) + 1.0
-    spread = lax.broadcasted_iota(jnp.int32, (capacity, LANES), 1)
+    column = lax.broadcasted_iota(jnp.int32, (capacity, LANES), 1)
     for e in range(local):
         chosen = jnp.where(across_rank[e : e + 1, :] == place, 1.0, 0.0).astype(BF16)
         sel[0, e * capacity : (e + 1) * capacity, :] = chosen
         selt[0, :, e * capacity : (e + 1) * capacity] = jnp.where(
             down_rank[:, e : e + 1] == place_t, 1.0, 0.0
         ).astype(BF16)
-        mine = (spread == first + e) | (spread == first + e + LANES // 2)
+        mine = (column == first + e) | (column == first + e + part)
         found = jnp.dot(chosen, table, preferred_element_type=F32)
         value = jnp.sum(jnp.where(mine, found, 0.0), axis=-1, keepdims=True)
         share[0, e * capacity : (e + 1) * capacity, :] = jnp.broadcast_to(value, (capacity, LANES))
@@ -285,6 +318,12 @@
             out[:, c : c + wide] = total[at * rows : (at + 1) * rows, :]
 
 
+def hold_kernel(source, out, sem):
+    copy = pltpu.make_async_copy(source, out, sem)
+    copy.start()
+    copy.wait()
+
+
 def add_kernel(*refs):
     total = refs[0][...].astype(F32)
     for ref in refs[1:-1]:
@@ -317,35 +356,43 @@
     most = max(2, 3 * rows * top // (2 * experts_all))
     capacity = -(-most * inner // 16) * 16
     chunk_rows = rows * inner
-    me = lax.axis_index("ctx")
-    spot = jnp.stack([me // inner, me % inner]).astype(jnp.int32)
     dma = pltpu.SemaphoreType.DMA
-
-    packed_rows = 2 * keys + rows + (group + 2) * rows
     ids_t, weights_t, slots = route_ids.T, route_weights.T, placement.reshape(1, -1)
-    operands = (queries, fresh, cache, ids_t, weights_t, slots)
-    packed = call(
-        functools.partial(pack_kernel, inner),
-        [jax.ShapeDtypeStruct((packed_rows, HEAD_SIZE), BF16)] * OUTERS,
-        (spot, *operands),
-        [SMEM] + [ANY] * 6,
-        "pack",
-        limit=60,
-        out_specs=[ANY] * OUTERS,
-        scratch=[
-            *[pltpu.VMEM((packed_rows, HEAD_SIZE), BF16)] * OUTERS,
-            *[pltpu.VMEM(a.shape, a.dtype) for a in operands],
-            dma((6,)),
-            dma((OUTERS,)),
-        ],
+
+    def pack(kernel, size, operands, name, tokens=()):
+        return call(
+            functools.partial(kernel, inner),
+            [jax.ShapeDtypeStruct((size, HEAD_SIZE), BF16)] * OUTERS,
+            operands,
+            [ANY] * len(operands),
+            name,
+            tokens,
+            limit=60,
+            out_specs=[ANY] * OUTERS,
+            scratch=[
+                *[pltpu.VMEM((size, HEAD_SIZE), BF16)] * OUTERS,
+                *[pltpu.VMEM(a.shape, a.dtype) for a in operands],
+                dma((len(operands),)),
+                dma((OUTERS,)),
+            ],
+        )
+
+    gate_rows = 2 * experts_all // OUTERS
+    cache_rows = 2 * keys + gate_rows
+    packed = pack(
+        pack_cache_kernel, cache_rows, (cache, ids_t, weights_t, slots), "pack_cache"
     )
     blocks = [packed[0]] + [swap(packed[k], n, k * inner) for k in range(1, OUTERS)]
+    packed = pack(
+        pack_queries_kernel, (group + 2) * rows, (queries, fresh), "pack_queries", (packed[0],)
+    )
+    asked = [packed[0]] + [swap(packed[k], n, k * inner) for k in range(1, OUTERS)]
     half_outers = OUTERS // 2
-    caches, tokens = [], ()
+    caches, tokens = [], (packed[0],)
     for at in (0, half_outers):
         merged = call(
-            functools.partial(merge_kernel, keys, rows),
-            jax.ShapeDtypeStruct((half_outers * (2 * keys + rows), HEAD_SIZE), BF16),
+            functools.partial(merge_kernel, keys),
+            jax.ShapeDtypeStruct((half_outers * cache_rows, HEAD_SIZE), BF16),
             blocks[at : at + half_outers],
             [ANY] * half_outers,
             "merge",
@@ -353,9 +400,19 @@
             out_specs=ANY,
             scratch=[dma((3 * half_outers,))],
         )
-        caches += gather_inner(merged, n)
-        tokens = (caches[inner // 2],)
-    projections = gather_inner(out_proj, n, merged)
+        caches += gather_inner(merged, n, *asked[1:])
+        tokens = (merged,)
+    projections = gather_inner(out_proj, n, caches[inner - 1], caches[-1])
+    projections[0] = call(
+        hold_kernel,
+        jax.ShapeDtypeStruct(out_proj.shape, BF16),
+        (out_proj,),
+        [ANY],
+        "hold",
+        (merged,),
+        out_specs=VMEM,
+        scratch=[dma],
+    )
 
     def add(terms, tokens=()):
         return call(
@@ -372,7 +429,7 @@
         return call(
             functools.partial(attention_kernel, inner, group, rows),
             jax.ShapeDtypeStruct((rows, width), kind),
-            (blocks[k], *caches, *projections),
+            (asked[k], *caches, *projections),
             [VMEM] * (1 + 3 * inner),
             "attention",
             tokens,
@@ -392,19 +449,19 @@
     ]
     kinds = [BF16, BF16, F32]
     last_half = half_outers - 1
-    far = attend(3, (), BF16)
+    far = attend(3, (asked[1], asked[2]), BF16)
     across = attend(2, (far,), F32)
     near = attend(1, (across,), BF16)
     sent = add([across, swap(far, n, inner)], (near,))
     own = attend(0, (sent,), F32)
     home = [swap(near, n, inner), swap(sent, n, 2 * inner)]
     selection = call(
-        functools.partial(select_kernel, inner, local, capacity),
+        functools.partial(select_kernel, inner, local, capacity, rows),
         [jax.ShapeDtypeStruct((OUTERS, *s), d) for s, d in zip(selected, kinds)],
-        (spot, *caches),
-        [SMEM]
-        + [pl.BlockSpec((rows, LANES), lambda k: (jnp.minimum(k, last_half), 0))] * inner
-        + [pl.BlockSpec((rows, LANES), lambda k: (jnp.maximum(k - half_outers, 0), 0))] * inner,
+        caches,
+        [pl.BlockSpec((gate_rows, LANES), lambda k: (jnp.minimum(k, last_half), 0))] * inner
+        + [pl.BlockSpec((gate_rows, LANES), lambda k: (jnp.maximum(k - half_outers, 0), 0))]
+        * inner,
         "select",
         (own,),
         out_specs=[pl.BlockSpec((1, *s), lambda k: (k, 0, 0)) for s in selected],
@@ -443,7 +500,6 @@
     bits = [1 << b for b in range(inner.bit_length() - 1)]
     first, second = swap(normed, n, inner), swap(normed, n, 2 * inner)
     around = gather_inner(normed, n)
-    third = swap(second, n, inner)
     slots = [None] * OUTERS
 
     def fold(k):
@@ -459,6 +515,7 @@
             terms = [t + [swap(a, n, bit)] for t, a in zip(terms[:middle], sent)]
         return terms[0], sent[0]
 
+    third = swap(second, n, inner)
     slots[0] = experts(0, around, ())
     fold(0)
     done = slots[0][0][0]
@@ -471,8 +528,9 @@
     terms, sent = finish(3, (done,))
     slots[2] = experts(2, gather_inner(second, n, done), (sent,))
     fold(2)
-    far = swap(add(terms, (slots[2][0][0],)), n, inner)
-    terms, sent = finish(2, (slots[2][0][0],))
+    total = add(terms, (slots[2][0][0],))
+    far = swap(total, n, inner)
+    terms, sent = finish(2, (total,))
     total = add(terms + [far], (sent,))
     across = swap(total, n, 2 * inner)
     terms, sent = finish(1, (total,))

time: 166 us -> 161 us (0.970)
  waiting for transfers between devices: 82.8 us -> 79.1 us
  starting transfers between devices: 41.1 us -> 38.7 us
    ppermute x45 -> x48, waiting for transfers between devices: 82.8 us -> 79.1 us  [swap(): return lax.ppermute(array, 'ctx', [(i, i ^ offset) for i in range(n)])]
    ppermute x45 -> x48, starting transfers between devices: 41.1 us -> 38.7 us  [swap(): return lax.ppermute(array, 'ctx', [(i, i ^ offset) for i in range(n)])]
    pallas_call x22 -> x24, Pallas kernels: 37.7 us -> 38.6 us  [call(): pl.pallas_call(body, out_shape=outs, in_specs=list(specs) + [ANY] * len(t...]
  transfers between devices with their start and end apart: 45 -> 48, of which waited for: 22 -> 22; matrix products, arithmetic and copies ran while one was open for 0% -> 0% of each run, Pallas kernels for 17% -> 21%
where the time goes in v3:
time: 161 us
  waiting for transfers between devices  79.1 us (49%)
  starting transfers between devices  38.7 us (24%)
  Pallas kernels  38.6 us (24%)
  local copies, waits for them, and re-layouts  3.09 us (2%)
    ppermute x48, waiting for transfers between devices, swap(): return lax.ppermute(array, 'ctx', [(i, i ^ offset) for i in range(n)])  79.1 us
    ppermute x48, starting transfers between devices, swap(): return lax.ppermute(array, 'ctx', [(i, i ^ offset) for i in range(n)])  38.7 us
    pallas_call x24, Pallas kernels, call(): pl.pallas_call(body, out_shape=outs, in_specs=list(specs) + [ANY] * len(t...  38.6 us
  transfers between devices with their start and end apart: 48, of which 22 were waited for; matrix products, arithmetic and copies ran while one was open for 0% of the time, Pallas kernels for 21%

profile of v3, /device:TPU:0, one launch (start us, length us, event | category | flops | bytes accessed | tf_op | source)
XLA Modules:
  0.0 160.5 jit_solution(2367132355480347282)
XLA Ops:
  0.6 3.0 %collective-permute-start.13 = (bf16[256,2048]{1,0:T(8,128)(2,1)}, bf16[256,2048]{1,0:T(8,128)(2,1)S(1)}, u32[]{:S(2)}, u32[]{:S(2)}) collective-permute-start(bf16[256,2048]{1,0:T(8,128)(2,1)} %refs_0_.6), channel_id=1, source_target_pairs={{0,2},{1,3},{2,0},{3,1},{4,6},{5,7},{6,4},{7,5},{8,10},{9,11},{10,... | collective-permute-start | bytes 3145736 | tf_op jit(solution)/shard_map/ppermute | solution.py:23
  3.7 1.9 %pack_cache.1 = (bf16[272,128]{1,0:T(8,128)(2,1)}, bf16[272,128]{1,0:T(8,128)(2,1)}, bf16[272,128]{1,0:T(8,128)(2,1)}, bf16[272,128]{1,0:T(8,128)(2,1)}) custom-call(bf16[2,128,512]{2,1,0:T(8,128)(2,1)} %refs_0_.4, s32[8,80]{1,0:T(8,128)} %bitcast.9, f32[8,80]{1,0:T(8,128)} %bitcast.10, s32[1,32]{1,0:T(1,128)} %bitcast.11), custom_call_target="tpu_custom_call" | custom-call | flops 1 | bytes 1 | tf_op jit(solution)/shard_map/pack_cache/pallas_call | solution.py:59
  5.5 2.1 %pack_queries.1 = (bf16[800,128]{1,0:T(8,128)(2,1)}, bf16[800,128]{1,0:T(8,128)(2,1)}, bf16[800,128]{1,0:T(8,128)(2,1)}, bf16[800,128]{1,0:T(8,128)(2,1)}) custom-call(bf16[80,4096]{1,0:T(8,128)(2,1)} %refs_0_.5, bf16[2,80,512]{2,1,0:T(8,128)(2,1)} %refs_1_.1, bf16[272,128]{1,0:T(8,128)(2,1)} %get-tuple-element.37.refs_2_.refs_0_), custom_call_target="tpu_custom_call" | custom-call | flops 1 | bytes 1 | tf_op jit(solution)/shard_map/pack_queries/pallas_call | solution.py:59
  7.6 1.6 %collective-permute-start.3 = (bf16[800,128]{1,0:T(8,128)(2,1)}, bf16[800,128]{1,0:T(8,128)(2,1)S(1)}, u32[]{:S(2)}, u32[]{:S(2)}) collective-permute-start(bf16[800,128]{1,0:T(8,128)(2,1)} %get-tuple-element.40), channel_id=1, source_target_pairs={{0,4},{1,5},{2,6},{3,7},{4,0},{5,1},{6,2},{7,3},{8,12},{9,13},{10,... | collective-permute-start | bytes 614408 | tf_op jit(solution)/shard_map/ppermute | solution.py:23
  9.7 2.6 %collective-permute-start.7 = (bf16[272,128]{1,0:T(8,128)(2,1)}, bf16[272,128]{1,0:T(8,128)(2,1)S(1)}, u32[]{:S(2)}, u32[]{:S(2)}) collective-permute-start(bf16[272,128]{1,0:T(8,128)(2,1)} %get-tuple-element.44), channel_id=1, source_target_pairs={{0,8},{1,9},{2,10},{3,11},{4,12},{5,13},{6,14},{7,15},{8,0},{9,1},... | collective-permute-start | bytes 208904 | tf_op jit(solution)/shard_map/ppermute | solution.py:23
  12.3 1.3 collective-permute-start.8
  13.7 3.8 %collective-permute-done.refs_1_ = bf16[272,128]{1,0:T(8,128)(2,1)S(1)} collective-permute-done((bf16[272,128]{1,0:T(8,128)(2,1)}, bf16[272,128]{1,0:T(8,128)(2,1)S(1)}, u32[]{:S(2)}, u32[]{:S(2)}) %collective-permute-start) | collective-permute-done | bytes 69664 | tf_op jit(solution)/shard_map/ppermute | solution.py:23
  17.4 2.6 %collective-permute-start.4 = (bf16[800,128]{1,0:T(8,128)(2,1)}, bf16[800,128]{1,0:T(8,128)(2,1)S(1)}, u32[]{:S(2)}, u32[]{:S(2)}) collective-permute-start(bf16[800,128]{1,0:T(8,128)(2,1)} %get-tuple-element.41), channel_id=1, source_target_pairs={{0,8},{1,9},{2,10},{3,11},{4,12},{5,13},{6,14},{7,15},{8,0},{9,1},... | collective-permute-start | bytes 614408 | tf_op jit(solution)/shard_map/ppermute | solution.py:23
  20.1 2.3 %collective-permute-start.5 = (bf16[800,128]{1,0:T(8,128)(2,1)}, bf16[800,128]{1,0:T(8,128)(2,1)S(1)}, u32[]{:S(2)}, u32[]{:S(2)}) collective-permute-start(bf16[800,128]{1,0:T(8,128)(2,1)} %get-tuple-element.42), channel_id=1, source_target_pairs={{0,12},{1,13},{2,14},{3,15},{4,8},{5,9},{6,10},{7,11},{8,4},{9,5},... | collective-permute-start | bytes 614408 | tf_op jit(solution)/shard_map/ppermute | solution.py:23
  22.4 0.9 copy-done.1
  25.3 1.5 collective-permute-start.2
  26.8 7.4 %collective-permute-done.4.refs_14_.refs_0_ = bf16[800,128]{1,0:T(8,128)(2,1)S(1)} collective-permute-done((bf16[800,128]{1,0:T(8,128)(2,1)}, bf16[800,128]{1,0:T(8,128)(2,1)S(1)}, u32[]{:S(2)}, u32[]{:S(2)}) %collective-permute-start.4) | collective-permute-done | bytes 204832 | tf_op jit(solution)/shard_map/ppermute | solution.py:23
  36.7 1.2 copy-done
  38.0 1.2 collective-permute-done.9.refs_6_.refs_5_
  39.4 3.3 %attention.4.refs_13_ = bf16[80,2048]{1,0:T(8,128)(2,1)S(1)} custom-call(bf16[800,128]{1,0:T(8,128)(2,1)S(1)} %collective-permute-done.5.refs_0_, bf16[544,128]{1,0:T(8,128)(2,1)S(1)} %merge.2.refs_2_.refs_1_.refs_0_, bf16[544,128]{1,0:T(8,128)(2,1)S(1)} %collective-permute-done.1.refs_2_.refs_1_, ...), custom_call_target="tpu_custom_call" | custom-call | flops 1 | bytes 1 | tf_op jit(solution)/shard_map/attention/pallas_call | solution.py:59
  42.7 4.9 %collective-permute-start.15 = (bf16[80,2048]{1,0:T(8,128)(2,1)S(1)}, bf16[80,2048]{1,0:T(8,128)(2,1)S(1)}, u32[]{:S(2)}, u32[]{:S(2)}) collective-permute-start(bf16[80,2048]{1,0:T(8,128)(2,1)S(1)} %attention.4.refs_13_), channel_id=1, source_target_pairs={{0,4},{1,5},{2,6},{3,7},{4,0},{5,1},{6,2},{7,3},{8,12},{9,13},{10,... | collective-permute-start | bytes 983048 | tf_op jit(solution)/shard_map/ppermute | solution.py:23
  47.6 3.3 %attention.5.refs_13_.refs_0_ = f32[80,2048]{1,0:T(8,128)S(1)} custom-call(bf16[800,128]{1,0:T(8,128)(2,1)S(1)} %collective-permute-done.4.refs_14_.refs_0_, bf16[544,128]{1,0:T(8,128)(2,1)S(1)} %merge.2.refs_2_.refs_1_.refs_0_, bf16[544,128]{1,0:T(8,128)(2,1)S(1)} %collective-permute-done.1.refs_2_.refs_1_, ...), custom_call_target="tpu_custom_call" | custom-call | flops 1 | bytes 1 | tf_op jit(solution)/shard_map/attention/pallas_call | solution.py:59
  50.9 3.3 %attention.6.refs_2_ = bf16[80,2048]{1,0:T(8,128)(2,1)S(1)} custom-call(bf16[800,128]{1,0:T(8,128)(2,1)S(1)} %collective-permute-done.3.refs_13_.refs_0_, bf16[544,128]{1,0:T(8,128)(2,1)S(1)} %merge.2.refs_2_.refs_1_.refs_0_, bf16[544,128]{1,0:T(8,128)(2,1)S(1)} %collective-permute-done.1.refs_2_.refs_1_, ...), custom_call_target="tpu_custom_call" | custom-call | flops 1 | bytes 1 | tf_op jit(solution)/shard_map/attention/pallas_call | solution.py:59
  54.3 1.4 collective-permute-done.15.refs_1_
  55.7 2.1 %collective-permute-start.17 = (bf16[80,2048]{1,0:T(8,128)(2,1)S(1)}, bf16[80,2048]{1,0:T(8,128)(2,1)S(1)}, u32[]{:S(2)}, u32[]{:S(2)}) collective-permute-start(bf16[80,2048]{1,0:T(8,128)(2,1)S(1)} %add.9.refs_13_), channel_id=1, source_target_pairs={{0,8},{1,9},{2,10},{3,11},{4,12},{5,13},{6,14},{7,15},{8,0},{9,1},... | collective-permute-start | bytes 983048 | tf_op jit(solution)/shard_map/ppermute | solution.py:23
  57.8 3.3 %attention.7.refs_8_.refs_2_ = f32[80,2048]{1,0:T(8,128)S(1)} custom-call(bf16[800,128]{1,0:T(8,128)(2,1)S(1)} %copy-done.2, bf16[544,128]{1,0:T(8,128)(2,1)S(1)} %merge.2.refs_2_.refs_1_.refs_0_, bf16[544,128]{1,0:T(8,128)(2,1)S(1)} %collective-permute-done.1.refs_2_.refs_1_, bf16[544,128]{1,0:T(8,128)(2,1)S(1)} %collective-permute-done.2.refs_3_.refs_2_, ...), custom_call_target="tpu_custom_call" | custom-call | flops 1 | bytes 1 | tf_op jit(solution)/shard_map/attention/pallas_call | solution.py:59
  61.1 3.4 %select.1 = (bf16[4,256,320]{2,1,0:T(8,128)(2,1)S(1)}, bf16[4,320,256]{2,1,0:T(8,128)(2,1)S(1)}, f32[4,256,128]{2,1,0:T(8,128)S(1)}) custom-call(bf16[544,128]{1,0:T(8,128)(2,1)S(1)} %merge.2.refs_2_.refs_1_.refs_0_, bf16[544,128]{1,0:T(8,128)(2,1)S(1)} %collective-permute-done.1.refs_2_.refs_1_, ...), custom_call_target="tpu_custom_call" | custom-call | flops 1 | bytes 1 | tf_op jit(solution)/shard_map/select/pallas_call | solution.py:59
  64.5 4.2 %collective-permute-done.16.refs_3_ = bf16[80,2048]{1,0:T(8,128)(2,1)S(1)} collective-permute-done((bf16[80,2048]{1,0:T(8,128)(2,1)S(1)}, bf16[80,2048]{1,0:T(8,128)(2,1)S(1)}, u32[]{:S(2)}, u32[]{:S(2)}) %collective-permute-start.16) | collective-permute-done | bytes 327712 | tf_op jit(solution)/shard_map/ppermute | solution.py:23
  68.7 4.4 %collective-permute-done.17.refs_4_ = bf16[80,2048]{1,0:T(8,128)(2,1)S(1)} collective-permute-done((bf16[80,2048]{1,0:T(8,128)(2,1)S(1)}, bf16[80,2048]{1,0:T(8,128)(2,1)S(1)}, u32[]{:S(2)}, u32[]{:S(2)}) %collective-permute-start.17) | collective-permute-done | bytes 327712 | tf_op jit(solution)/shard_map/ppermute | solution.py:23
  73.1 0.9 norm.1
  74.5 2.0 %collective-permute-start.27 = (bf16[80,2048]{1,0:T(8,128)(2,1)S(1)}, bf16[80,2048]{1,0:T(8,128)(2,1)S(1)}, u32[]{:S(2)}, u32[]{:S(2)}) collective-permute-start(bf16[80,2048]{1,0:T(8,128)(2,1)S(1)} %get-tuple-element.50.refs_0_), channel_id=1, source_target_pairs={{0,8},{1,9},{2,10},{3,11},{4,12},{5,13},{6,14},{7,15},{8,0},{9,1},... | collective-permute-start | bytes 983048 | tf_op jit(solution)/shard_map/ppermute | solution.py:23
  76.5 5.9 %collective-permute-done.19.refs_2_ = bf16[80,2048]{1,0:T(8,128)(2,1)S(1)} collective-permute-done((bf16[80,2048]{1,0:T(8,128)(2,1)S(1)}, bf16[80,2048]{1,0:T(8,128)(2,1)S(1)}, u32[]{:S(2)}, u32[]{:S(2)}) %collective-permute-start.19) | collective-permute-done | bytes 327712 | tf_op jit(solution)/shard_map/ppermute | solution.py:23
  82.4 6.0 %collective-permute-done.23.refs_0_ = bf16[80,2048]{1,0:T(8,128)(2,1)S(1)} collective-permute-done((bf16[80,2048]{1,0:T(8,128)(2,1)S(1)}, bf16[80,2048]{1,0:T(8,128)(2,1)S(1)}, u32[]{:S(2)}, u32[]{:S(2)}) %collective-permute-start.23) | collective-permute-done | bytes 327712 | tf_op jit(solution)/shard_map/ppermute | solution.py:23
  88.4 1.5 collective-permute-start.25
  90.7 3.7 %experts.4 = (bf16[80,2048]{1,0:T(8,128)(2,1)S(1)}, bf16[80,2048]{1,0:T(8,128)(2,1)S(1)}, bf16[80,2048]{1,0:T(8,128)(2,1)S(1)}, bf16[80,2048]{1,0:T(8,128)(2,1)S(1)}) custom-call(bf16[80,2048]{1,0:T(8,128)(2,1)S(1)} %get-tuple-element.50.refs_0_, bf16[80,2048]{1,0:T(8,128)(2,1)S(1)} %collective-permute-done.18.refs_1_, ...), custom_call_target="tpu_custom_call" | custom-call | flops 1 | bytes 1 | tf_op jit(solution)/shard_map/experts/pallas_call | solution.py:59
  94.4 2.7 %collective-permute-done.25.refs_2_ = bf16[80,2048]{1,0:T(8,128)(2,1)S(1)} collective-permute-done((bf16[80,2048]{1,0:T(8,128)(2,1)S(1)}, bf16[80,2048]{1,0:T(8,128)(2,1)S(1)}, u32[]{:S(2)}, u32[]{:S(2)}) %collective-permute-start.25) | collective-permute-done | bytes 327712 | tf_op jit(solution)/shard_map/ppermute | solution.py:23
  97.1 1.2 collective-permute-done.32.refs_0_
  98.3 0.9 collective-permute-start.34
  99.3 3.7 %experts.5 = (bf16[80,2048]{1,0:T(8,128)(2,1)S(1)}, bf16[80,2048]{1,0:T(8,128)(2,1)S(1)}, bf16[80,2048]{1,0:T(8,128)(2,1)S(1)}, bf16[80,2048]{1,0:T(8,128)(2,1)S(1)}) custom-call(bf16[80,2048]{1,0:T(8,128)(2,1)S(1)} %collective-permute-done.23.refs_0_, bf16[80,2048]{1,0:T(8,128)(2,1)S(1)} %collective-permute-done.24.refs_1_, ...), custom_call_target="tpu_custom_call" | custom-call | flops 1 | bytes 1 | tf_op jit(solution)/shard_map/experts/pallas_call | solution.py:59
  103.0 4.3 %collective-permute-done.34.refs_2_ = bf16[80,2048]{1,0:T(8,128)(2,1)S(1)} collective-permute-done((bf16[80,2048]{1,0:T(8,128)(2,1)S(1)}, bf16[80,2048]{1,0:T(8,128)(2,1)S(1)}, u32[]{:S(2)}, u32[]{:S(2)}) %collective-permute-start.34) | collective-permute-done | bytes 327712 | tf_op jit(solution)/shard_map/ppermute | solution.py:23
  107.2 1.5 collective-permute-start.31
  109.0 3.7 %experts.6 = (bf16[80,2048]{1,0:T(8,128)(2,1)S(1)}, bf16[80,2048]{1,0:T(8,128)(2,1)S(1)}, bf16[80,2048]{1,0:T(8,128)(2,1)S(1)}, bf16[80,2048]{1,0:T(8,128)(2,1)S(1)}) custom-call(bf16[80,2048]{1,0:T(8,128)(2,1)S(1)} %collective-permute-done.32.refs_0_, bf16[80,2048]{1,0:T(8,128)(2,1)S(1)} %collective-permute-done.33.refs_1_, ...), custom_call_target="tpu_custom_call" | custom-call | flops 1 | bytes 1 | tf_op jit(solution)/shard_map/experts/pallas_call | solution.py:59
  113.0 4.3 %collective-permute-done.31.refs_2_ = bf16[80,2048]{1,0:T(8,128)(2,1)S(1)} collective-permute-done((bf16[80,2048]{1,0:T(8,128)(2,1)S(1)}, bf16[80,2048]{1,0:T(8,128)(2,1)S(1)}, u32[]{:S(2)}, u32[]{:S(2)}) %collective-permute-start.31) | collective-permute-done | bytes 327712 | tf_op jit(solution)/shard_map/ppermute | solution.py:23
  117.9 1.6 collective-permute-start.41
  119.5 3.9 %experts.7 = (bf16[80,2048]{1,0:T(8,128)(2,1)S(1)}, bf16[80,2048]{1,0:T(8,128)(2,1)S(1)}, bf16[80,2048]{1,0:T(8,128)(2,1)S(1)}, bf16[80,2048]{1,0:T(8,128)(2,1)S(1)}) custom-call(bf16[80,2048]{1,0:T(8,128)(2,1)S(1)} %collective-permute-done.27.refs_10_.refs_0_, bf16[80,2048]{1,0:T(8,128)(2,1)S(1)} %collective-permute-done.30.refs_1_, ...), custom_call_target="tpu_custom_call" | custom-call | flops 1 | bytes 1 | tf_op jit(solution)/shard_map/experts/pallas_call | solution.py:59
  124.0 3.6 %collective-permute-done.41.refs_2_ = bf16[80,2048]{1,0:T(8,128)(2,1)S(1)} collective-permute-done((bf16[80,2048]{1,0:T(8,128)(2,1)S(1)}, bf16[80,2048]{1,0:T(8,128)(2,1)S(1)}, u32[]{:S(2)}, u32[]{:S(2)}) %collective-permute-start.41) | collective-permute-done | bytes 327712 | tf_op jit(solution)/shard_map/ppermute | solution.py:23
  127.9 1.6 collective-permute-start.42
  130.0 6.7 %collective-permute-done.42.refs_2_ = bf16[80,2048]{1,0:T(8,128)(2,1)S(1)} collective-permute-done((bf16[80,2048]{1,0:T(8,128)(2,1)S(1)}, bf16[80,2048]{1,0:T(8,128)(2,1)S(1)}, u32[]{:S(2)}, u32[]{:S(2)}) %collective-permute-start.42) | collective-permute-done | bytes 327712 | tf_op jit(solution)/shard_map/ppermute | solution.py:23
  136.7 1.2 collective-permute-done.43.refs_3_
  139.3 6.5 %collective-permute-done.44.refs_2_ = bf16[80,2048]{1,0:T(8,128)(2,1)S(1)} collective-permute-done((bf16[80,2048]{1,0:T(8,128)(2,1)S(1)}, bf16[80,2048]{1,0:T(8,128)(2,1)S(1)}, u32[]{:S(2)}, u32[]{:S(2)}) %collective-permute-start.44) | collective-permute-done | bytes 327712 | tf_op jit(solution)/shard_map/ppermute | solution.py:23
  147.2 9.4 %collective-permute-done.47.refs_4_ = bf16[80,2048]{1,0:T(8,128)(2,1)S(1)} collective-permute-done((bf16[80,2048]{1,0:T(8,128)(2,1)S(1)}, bf16[80,2048]{1,0:T(8,128)(2,1)S(1)}, u32[]{:S(2)}, u32[]{:S(2)}) %collective-permute-start.47) | collective-permute-done | bytes 327712 | tf_op jit(solution)/shard_map/ppermute | solution.py:23
  156.6 2.9 %collective-permute-done.46.refs_3_ = bf16[80,2048]{1,0:T(8,128)(2,1)S(1)} collective-permute-done((bf16[80,2048]{1,0:T(8,128)(2,1)S(1)}, bf16[80,2048]{1,0:T(8,128)(2,1)S(1)}, u32[]{:S(2)}, u32[]{:S(2)}) %collective-permute-start.46) | collective-permute-done | bytes 327712 | tf_op jit(solution)/shard_map/ppermute | solution.py:23
  159.6 0.9 add.17
  (96 shorter events, 11.8 us)
Async XLA Ops:
  0.6 35.2 %collective-permute-start.13 = (bf16[256,2048]{1,0:T(8,128)(2,1)}, bf16[256,2048]{1,0:T(8,128)(2,1)S(1)}, u32[]{:S(2)}, u32[]{:S(2)}) collective-permute-start(bf16[256,2048]{1,0:T(8,128)(2,1)} %refs_0_.6), channel_id=1, source_target_pairs={{0,2},{1,3},{2,0},{3,1},{4,6},{5,7},{6,4},{7,5},{8,10},{9,11},{10,... | collective-permute-start | bytes 3145736 | tf_op jit(solution)/shard_map/ppermute | solution.py:23
  7.6 17.7 %collective-permute-start.3 = (bf16[800,128]{1,0:T(8,128)(2,1)}, bf16[800,128]{1,0:T(8,128)(2,1)S(1)}, u32[]{:S(2)}, u32[]{:S(2)}) collective-permute-start(bf16[800,128]{1,0:T(8,128)(2,1)} %get-tuple-element.40), channel_id=1, source_target_pairs={{0,4},{1,5},{2,6},{3,7},{4,0},{5,1},{6,2},{7,3},{8,12},{9,13},{10,... | collective-permute-start | bytes 614408 | tf_op jit(solution)/shard_map/ppermute | solution.py:23
  9.3 8.2 %collective-permute-start = (bf16[272,128]{1,0:T(8,128)(2,1)}, bf16[272,128]{1,0:T(8,128)(2,1)S(1)}, u32[]{:S(2)}, u32[]{:S(2)}) collective-permute-start(bf16[272,128]{1,0:T(8,128)(2,1)} %get-tuple-element.39), channel_id=1, source_target_pairs={{0,4},{1,5},{2,6},{3,7},{4,0},{5,1},{6,2},{7,3},{8,12},{9,13},{10,... | collective-permute-start | bytes 208904 | tf_op jit(solution)/shard_map/ppermute | solution.py:23
  9.7 10.3 %collective-permute-start.7 = (bf16[272,128]{1,0:T(8,128)(2,1)}, bf16[272,128]{1,0:T(8,128)(2,1)S(1)}, u32[]{:S(2)}, u32[]{:S(2)}) collective-permute-start(bf16[272,128]{1,0:T(8,128)(2,1)} %get-tuple-element.44), channel_id=1, source_target_pairs={{0,8},{1,9},{2,10},{3,11},{4,12},{5,13},{6,14},{7,15},{8,0},{9,1},... | collective-permute-start | bytes 208904 | tf_op jit(solution)/shard_map/ppermute | solution.py:23
  12.3 12.1 %collective-permute-start.8 = (bf16[272,128]{1,0:T(8,128)(2,1)}, bf16[272,128]{1,0:T(8,128)(2,1)S(1)}, u32[]{:S(2)}, u32[]{:S(2)}) collective-permute-start(bf16[272,128]{1,0:T(8,128)(2,1)} %get-tuple-element.45), channel_id=1, source_target_pairs={{0,12},{1,13},{2,14},{3,15},{4,8},{5,9},{6,10},{7,11},{8,4},{9,5},... | collective-permute-start | bytes 208904 | tf_op jit(solution)/shard_map/ppermute | solution.py:23
  17.4 16.8 %collective-permute-start.4 = (bf16[800,128]{1,0:T(8,128)(2,1)}, bf16[800,128]{1,0:T(8,128)(2,1)S(1)}, u32[]{:S(2)}, u32[]{:S(2)}) collective-permute-start(bf16[800,128]{1,0:T(8,128)(2,1)} %get-tuple-element.41), channel_id=1, source_target_pairs={{0,8},{1,9},{2,10},{3,11},{4,12},{5,13},{6,14},{7,15},{8,0},{9,1},... | collective-permute-start | bytes 614408 | tf_op jit(solution)/shard_map/ppermute | solution.py:23
  20.1 14.2 %collective-permute-start.5 = (bf16[800,128]{1,0:T(8,128)(2,1)}, bf16[800,128]{1,0:T(8,128)(2,1)S(1)}, u32[]{:S(2)}, u32[]{:S(2)}) collective-permute-start(bf16[800,128]{1,0:T(8,128)(2,1)} %get-tuple-element.42), channel_id=1, source_target_pairs={{0,12},{1,13},{2,14},{3,15},{4,8},{5,9},{6,10},{7,11},{8,4},{9,5},... | collective-permute-start | bytes 614408 | tf_op jit(solution)/shard_map/ppermute | solution.py:23
  24.7 9.5 %collective-permute-start.10 = (bf16[544,128]{1,0:T(8,128)(2,1)S(1)}, bf16[544,128]{1,0:T(8,128)(2,1)S(1)}, u32[]{:S(2)}, u32[]{:S(2)}) collective-permute-start(bf16[544,128]{1,0:T(8,128)(2,1)S(1)} %merge.3.refs_1_.refs_5_.refs_4_), channel_id=1, source_target_pairs={{0,2},{1,3},{2,0},{3,1},{4,6},{5,7},{6,4},{7,5},{8,10},{9,11},{10,... | collective-permute-start | bytes 417800 | tf_op jit(solution)/shard_map/ppermute | solution.py:23
  25.3 8.9 %collective-permute-start.2 = (bf16[544,128]{1,0:T(8,128)(2,1)S(1)}, bf16[544,128]{1,0:T(8,128)(2,1)S(1)}, u32[]{:S(2)}, u32[]{:S(2)}) collective-permute-start(bf16[544,128]{1,0:T(8,128)(2,1)S(1)} %merge.2.refs_2_.refs_1_.refs_0_), channel_id=1, source_target_pairs={{0,2},{1,3},{2,0},{3,1},{4,6},{5,7},{6,4},{7,5},{8,10},{9,11},{10,... | collective-permute-start | bytes 417800 | tf_op jit(solution)/shard_map/ppermute | solution.py:23
  34.2 1.4 collective-permute-start.6
  34.3 1.5 collective-permute-start.11
  34.8 4.6 %collective-permute-start.12 = (bf16[256,2048]{1,0:T(8,128)(2,1)}, bf16[256,2048]{1,0:T(8,128)(2,1)S(1)}, u32[]{:S(2)}, u32[]{:S(2)}) collective-permute-start(bf16[256,2048]{1,0:T(8,128)(2,1)} %refs_0_.6), channel_id=1, source_target_pairs={{0,1},{1,0},{2,3},{3,2},{4,5},{5,4},{6,7},{7,6},{8,9},{9,8},{10,11... | collective-permute-start | bytes 3145736 | tf_op jit(solution)/shard_map/ppermute | solution.py:23
  35.8 3.5 %collective-permute-start.14 = (bf16[256,2048]{1,0:T(8,128)(2,1)S(1)}, bf16[256,2048]{1,0:T(8,128)(2,1)S(1)}, u32[]{:S(2)}, u32[]{:S(2)}) collective-permute-start(bf16[256,2048]{1,0:T(8,128)(2,1)S(1)} %collective-permute-done.13.refs_11_), channel_id=1, source_target_pairs={{0,1},{1,0},{2,3},{3,2},{4,5},{5,4},{6,7},{7,6},{8,9},{9,8},{10,11... | collective-permute-start | bytes 3145736 | tf_op jit(solution)/shard_map/ppermute | solution.py:23
  36.2 3.0 %collective-permute-start.9 = (bf16[544,128]{1,0:T(8,128)(2,1)S(1)}, bf16[544,128]{1,0:T(8,128)(2,1)S(1)}, u32[]{:S(2)}, u32[]{:S(2)}) collective-permute-start(bf16[544,128]{1,0:T(8,128)(2,1)S(1)} %merge.3.refs_1_.refs_5_.refs_4_), channel_id=1, source_target_pairs={{0,1},{1,0},{2,3},{3,2},{4,5},{5,4},{6,7},{7,6},{8,9},{9,8},{10,11... | collective-permute-start | bytes 417800 | tf_op jit(solution)/shard_map/ppermute | solution.py:23
  36.4 3.0 %collective-permute-start.1 = (bf16[544,128]{1,0:T(8,128)(2,1)S(1)}, bf16[544,128]{1,0:T(8,128)(2,1)S(1)}, u32[]{:S(2)}, u32[]{:S(2)}) collective-permute-start(bf16[544,128]{1,0:T(8,128)(2,1)S(1)} %merge.2.refs_2_.refs_1_.refs_0_), channel_id=1, source_target_pairs={{0,1},{1,0},{2,3},{3,2},{4,5},{5,4},{6,7},{7,6},{8,9},{9,8},{10,11... | collective-permute-start | bytes 417800 | tf_op jit(solution)/shard_map/ppermute | solution.py:23
  42.7 12.9 %collective-permute-start.15 = (bf16[80,2048]{1,0:T(8,128)(2,1)S(1)}, bf16[80,2048]{1,0:T(8,128)(2,1)S(1)}, u32[]{:S(2)}, u32[]{:S(2)}) collective-permute-start(bf16[80,2048]{1,0:T(8,128)(2,1)S(1)} %attention.4.refs_13_), channel_id=1, source_target_pairs={{0,4},{1,5},{2,6},{3,7},{4,0},{5,1},{6,2},{7,3},{8,12},{9,13},{10,... | collective-permute-start | bytes 983048 | tf_op jit(solution)/shard_map/ppermute | solution.py:23
  54.2 14.5 %collective-permute-start.16 = (bf16[80,2048]{1,0:T(8,128)(2,1)S(1)}, bf16[80,2048]{1,0:T(8,128)(2,1)S(1)}, u32[]{:S(2)}, u32[]{:S(2)}) collective-permute-start(bf16[80,2048]{1,0:T(8,128)(2,1)S(1)} %attention.6.refs_2_), channel_id=1, source_target_pairs={{0,4},{1,5},{2,6},{3,7},{4,0},{5,1},{6,2},{7,3},{8,12},{9,13},{10,... | collective-permute-start | bytes 983048 | tf_op jit(solution)/shard_map/ppermute | solution.py:23
  55.7 17.3 %collective-permute-start.17 = (bf16[80,2048]{1,0:T(8,128)(2,1)S(1)}, bf16[80,2048]{1,0:T(8,128)(2,1)S(1)}, u32[]{:S(2)}, u32[]{:S(2)}) collective-permute-start(bf16[80,2048]{1,0:T(8,128)(2,1)S(1)} %add.9.refs_13_), channel_id=1, source_target_pairs={{0,8},{1,9},{2,10},{3,11},{4,12},{5,13},{6,14},{7,15},{8,0},{9,1},... | collective-permute-start | bytes 983048 | tf_op jit(solution)/shard_map/ppermute | solution.py:23
  74.0 8.5 %collective-permute-start.19 = (bf16[80,2048]{1,0:T(8,128)(2,1)S(1)}, bf16[80,2048]{1,0:T(8,128)(2,1)S(1)}, u32[]{:S(2)}, u32[]{:S(2)}) collective-permute-start(bf16[80,2048]{1,0:T(8,128)(2,1)S(1)} %get-tuple-element.50.refs_0_), channel_id=1, source_target_pairs={{0,2},{1,3},{2,0},{3,1},{4,6},{5,7},{6,4},{7,5},{8,10},{9,11},{10,... | collective-permute-start | bytes 983048 | tf_op jit(solution)/shard_map/ppermute | solution.py:23
  74.5 13.9 %collective-permute-start.23 = (bf16[80,2048]{1,0:T(8,128)(2,1)S(1)}, bf16[80,2048]{1,0:T(8,128)(2,1)S(1)}, u32[]{:S(2)}, u32[]{:S(2)}) collective-permute-start(bf16[80,2048]{1,0:T(8,128)(2,1)S(1)} %get-tuple-element.50.refs_0_), channel_id=1, source_target_pairs={{0,4},{1,5},{2,6},{3,7},{4,0},{5,1},{6,2},{7,3},{8,12},{9,13},{10,... | collective-permute-start | bytes 983048 | tf_op jit(solution)/shard_map/ppermute | solution.py:23
  74.5 16.1 %collective-permute-start.27 = (bf16[80,2048]{1,0:T(8,128)(2,1)S(1)}, bf16[80,2048]{1,0:T(8,128)(2,1)S(1)}, u32[]{:S(2)}, u32[]{:S(2)}) collective-permute-start(bf16[80,2048]{1,0:T(8,128)(2,1)S(1)} %get-tuple-element.50.refs_0_), channel_id=1, source_target_pairs={{0,8},{1,9},{2,10},{3,11},{4,12},{5,13},{6,14},{7,15},{8,0},{9,1},... | collective-permute-start | bytes 983048 | tf_op jit(solution)/shard_map/ppermute | solution.py:23
  76.5 14.1 %collective-permute-start.18 = (bf16[80,2048]{1,0:T(8,128)(2,1)S(1)}, bf16[80,2048]{1,0:T(8,128)(2,1)S(1)}, u32[]{:S(2)}, u32[]{:S(2)}) collective-permute-start(bf16[80,2048]{1,0:T(8,128)(2,1)S(1)} %get-tuple-element.50.refs_0_), channel_id=1, source_target_pairs={{0,1},{1,0},{2,3},{3,2},{4,5},{5,4},{6,7},{7,6},{8,9},{9,8},{10,11... | collective-permute-start | bytes 983048 | tf_op jit(solution)/shard_map/ppermute | solution.py:23
  82.4 8.2 %collective-permute-start.20 = (bf16[80,2048]{1,0:T(8,128)(2,1)S(1)}, bf16[80,2048]{1,0:T(8,128)(2,1)S(1)}, u32[]{:S(2)}, u32[]{:S(2)}) collective-permute-start(bf16[80,2048]{1,0:T(8,128)(2,1)S(1)} %collective-permute-done.19.refs_2_), channel_id=1, source_target_pairs={{0,1},{1,0},{2,3},{3,2},{4,5},{5,4},{6,7},{7,6},{8,9},{9,8},{10,11... | collective-permute-start | bytes 983048 | tf_op jit(solution)/shard_map/ppermute | solution.py:23
  88.4 8.7 %collective-permute-start.25 = (bf16[80,2048]{1,0:T(8,128)(2,1)S(1)}, bf16[80,2048]{1,0:T(8,128)(2,1)S(1)}, u32[]{:S(2)}, u32[]{:S(2)}) collective-permute-start(bf16[80,2048]{1,0:T(8,128)(2,1)S(1)} %collective-permute-done.23.refs_0_), channel_id=1, source_target_pairs={{0,2},{1,3},{2,0},{3,1},{4,6},{5,7},{6,4},{7,5},{8,10},{9,11},{10,... | collective-permute-start | bytes 983048 | tf_op jit(solution)/shard_map/ppermute | solution.py:23
  90.6 7.7 %collective-permute-start.32 = (bf16[80,2048]{1,0:T(8,128)(2,1)S(1)}, bf16[80,2048]{1,0:T(8,128)(2,1)S(1)}, u32[]{:S(2)}, u32[]{:S(2)}) collective-permute-start(bf16[80,2048]{1,0:T(8,128)(2,1)S(1)} %collective-permute-done.27.refs_10_.refs_0_), channel_id=1, source_target_pairs={{0,4},{1,5},{2,6},{3,7},{4,0},{5,1},{6,2},{7,3},{8,12},{9,13},{10,... | collective-permute-start | bytes 983048 | tf_op jit(solution)/shard_map/ppermute | solution.py:23
  90.6 8.6 %collective-permute-start.24 = (bf16[80,2048]{1,0:T(8,128)(2,1)S(1)}, bf16[80,2048]{1,0:T(8,128)(2,1)S(1)}, u32[]{:S(2)}, u32[]{:S(2)}) collective-permute-start(bf16[80,2048]{1,0:T(8,128)(2,1)S(1)} %collective-permute-done.23.refs_0_), channel_id=1, source_target_pairs={{0,1},{1,0},{2,3},{3,2},{4,5},{5,4},{6,7},{7,6},{8,9},{9,8},{10,11... | collective-permute-start | bytes 983048 | tf_op jit(solution)/shard_map/ppermute | solution.py:23
  97.1 2.2 %collective-permute-start.26 = (bf16[80,2048]{1,0:T(8,128)(2,1)S(1)}, bf16[80,2048]{1,0:T(8,128)(2,1)S(1)}, u32[]{:S(2)}, u32[]{:S(2)}) collective-permute-start(bf16[80,2048]{1,0:T(8,128)(2,1)S(1)} %collective-permute-done.25.refs_2_), channel_id=1, source_target_pairs={{0,1},{1,0},{2,3},{3,2},{4,5},{5,4},{6,7},{7,6},{8,9},{9,8},{10,11... | collective-permute-start | bytes 983048 | tf_op jit(solution)/shard_map/ppermute | solution.py:23
  98.3 8.9 %collective-permute-start.34 = (bf16[80,2048]{1,0:T(8,128)(2,1)S(1)}, bf16[80,2048]{1,0:T(8,128)(2,1)S(1)}, u32[]{:S(2)}, u32[]{:S(2)}) collective-permute-start(bf16[80,2048]{1,0:T(8,128)(2,1)S(1)} %collective-permute-done.32.refs_0_), channel_id=1, source_target_pairs={{0,2},{1,3},{2,0},{3,1},{4,6},{5,7},{6,4},{7,5},{8,10},{9,11},{10,... | collective-permute-start | bytes 983048 | tf_op jit(solution)/shard_map/ppermute | solution.py:23
  99.3 9.7 %collective-permute-start.33 = (bf16[80,2048]{1,0:T(8,128)(2,1)S(1)}, bf16[80,2048]{1,0:T(8,128)(2,1)S(1)}, u32[]{:S(2)}, u32[]{:S(2)}) collective-permute-start(bf16[80,2048]{1,0:T(8,128)(2,1)S(1)} %collective-permute-done.32.refs_0_), channel_id=1, source_target_pairs={{0,1},{1,0},{2,3},{3,2},{4,5},{5,4},{6,7},{7,6},{8,9},{9,8},{10,11... | collective-permute-start | bytes 983048 | tf_op jit(solution)/shard_map/ppermute | solution.py:23
  107.2 1.8 %collective-permute-start.35 = (bf16[80,2048]{1,0:T(8,128)(2,1)S(1)}, bf16[80,2048]{1,0:T(8,128)(2,1)S(1)}, u32[]{:S(2)}, u32[]{:S(2)}) collective-permute-start(bf16[80,2048]{1,0:T(8,128)(2,1)S(1)} %collective-permute-done.34.refs_2_), channel_id=1, source_target_pairs={{0,1},{1,0},{2,3},{3,2},{4,5},{5,4},{6,7},{7,6},{8,9},{9,8},{10,11... | collective-permute-start | bytes 983048 | tf_op jit(solution)/shard_map/ppermute | solution.py:23
  107.2 10.1 %collective-permute-start.31 = (bf16[80,2048]{1,0:T(8,128)(2,1)S(1)}, bf16[80,2048]{1,0:T(8,128)(2,1)S(1)}, u32[]{:S(2)}, u32[]{:S(2)}) collective-permute-start(bf16[80,2048]{1,0:T(8,128)(2,1)S(1)} %collective-permute-done.27.refs_10_.refs_0_), channel_id=1, source_target_pairs={{0,2},{1,3},{2,0},{3,1},{4,6},{5,7},{6,4},{7,5},{8,10},{9,11},{10,... | collective-permute-start | bytes 983048 | tf_op jit(solution)/shard_map/ppermute | solution.py:23
  108.7 10.8 %collective-permute-start.30 = (bf16[80,2048]{1,0:T(8,128)(2,1)S(1)}, bf16[80,2048]{1,0:T(8,128)(2,1)S(1)}, u32[]{:S(2)}, u32[]{:S(2)}) collective-permute-start(bf16[80,2048]{1,0:T(8,128)(2,1)S(1)} %collective-permute-done.27.refs_10_.refs_0_), channel_id=1, source_target_pairs={{0,1},{1,0},{2,3},{3,2},{4,5},{5,4},{6,7},{7,6},{8,9},{9,8},{10,11... | collective-permute-start | bytes 983048 | tf_op jit(solution)/shard_map/ppermute | solution.py:23
  112.7 5.2 %collective-permute-start.37 = (bf16[80,2048]{1,0:T(8,128)(2,1)S(1)}, bf16[80,2048]{1,0:T(8,128)(2,1)S(1)}, u32[]{:S(2)}, u32[]{:S(2)}) collective-permute-start(bf16[80,2048]{1,0:T(8,128)(2,1)S(1)} %get-tuple-element.66), channel_id=1, source_target_pairs={{0,1},{1,0},{2,3},{3,2},{4,5},{5,4},{6,7},{7,6},{8,9},{9,8},{10,11... | collective-permute-start | bytes 983048 | tf_op jit(solution)/shard_map/ppermute | solution.py:23
  117.4 2.2 %collective-permute-start.36 = (bf16[80,2048]{1,0:T(8,128)(2,1)S(1)}, bf16[80,2048]{1,0:T(8,128)(2,1)S(1)}, u32[]{:S(2)}, u32[]{:S(2)}) collective-permute-start(bf16[80,2048]{1,0:T(8,128)(2,1)S(1)} %collective-permute-done.31.refs_2_), channel_id=1, source_target_pairs={{0,1},{1,0},{2,3},{3,2},{4,5},{5,4},{6,7},{7,6},{8,9},{9,8},{10,11... | collective-permute-start | bytes 983048 | tf_op jit(solution)/shard_map/ppermute | solution.py:23
  117.4 6.7 %collective-permute-start.40 = (bf16[80,2048]{1,0:T(8,128)(2,1)S(1)}, bf16[80,2048]{1,0:T(8,128)(2,1)S(1)}, u32[]{:S(2)}, u32[]{:S(2)}) collective-permute-start(bf16[80,2048]{1,0:T(8,128)(2,1)S(1)} %get-tuple-element.71), channel_id=1, source_target_pairs={{0,1},{1,0},{2,3},{3,2},{4,5},{5,4},{6,7},{7,6},{8,9},{9,8},{10,11... | collective-permute-start | bytes 983048 | tf_op jit(solution)/shard_map/ppermute | solution.py:23
  117.9 9.7 %collective-permute-start.41 = (bf16[80,2048]{1,0:T(8,128)(2,1)S(1)}, bf16[80,2048]{1,0:T(8,128)(2,1)S(1)}, u32[]{:S(2)}, u32[]{:S(2)}) collective-permute-start(bf16[80,2048]{1,0:T(8,128)(2,1)S(1)} %add.10.refs_9_), channel_id=1, source_target_pairs={{0,2},{1,3},{2,0},{3,1},{4,6},{5,7},{6,4},{7,5},{8,10},{9,11},{10,... | collective-permute-start | bytes 983048 | tf_op jit(solution)/shard_map/ppermute | solution.py:23
  123.4 4.3 %collective-permute-start.39 = (bf16[80,2048]{1,0:T(8,128)(2,1)S(1)}, bf16[80,2048]{1,0:T(8,128)(2,1)S(1)}, u32[]{:S(2)}, u32[]{:S(2)}) collective-permute-start(bf16[80,2048]{1,0:T(8,128)(2,1)S(1)} %get-tuple-element.70), channel_id=1, source_target_pairs={{0,1},{1,0},{2,3},{3,2},{4,5},{5,4},{6,7},{7,6},{8,9},{9,8},{10,11... | collective-permute-start | bytes 983048 | tf_op jit(solution)/shard_map/ppermute | solution.py:23
  123.5 6.4 %collective-permute-start.38 = (bf16[80,2048]{1,0:T(8,128)(2,1)S(1)}, bf16[80,2048]{1,0:T(8,128)(2,1)S(1)}, u32[]{:S(2)}, u32[]{:S(2)}) collective-permute-start(bf16[80,2048]{1,0:T(8,128)(2,1)S(1)} %get-tuple-element.68), channel_id=1, source_target_pairs={{0,1},{1,0},{2,3},{3,2},{4,5},{5,4},{6,7},{7,6},{8,9},{9,8},{10,11... | collective-permute-start | bytes 983048 | tf_op jit(solution)/shard_map/ppermute | solution.py:23
  127.9 8.8 %collective-permute-start.42 = (bf16[80,2048]{1,0:T(8,128)(2,1)S(1)}, bf16[80,2048]{1,0:T(8,128)(2,1)S(1)}, u32[]{:S(2)}, u32[]{:S(2)}) collective-permute-start(bf16[80,2048]{1,0:T(8,128)(2,1)S(1)} %add.12.refs_4_), channel_id=1, source_target_pairs={{0,2},{1,3},{2,0},{3,1},{4,6},{5,7},{6,4},{7,5},{8,10},{9,11},{10,... | collective-permute-start | bytes 983048 | tf_op jit(solution)/shard_map/ppermute | solution.py:23
  129.4 8.5 %collective-permute-start.43 = (bf16[80,2048]{1,0:T(8,128)(2,1)S(1)}, bf16[80,2048]{1,0:T(8,128)(2,1)S(1)}, u32[]{:S(2)}, u32[]{:S(2)}) collective-permute-start(bf16[80,2048]{1,0:T(8,128)(2,1)S(1)} %add.11.refs_2_), channel_id=1, source_target_pairs={{0,4},{1,5},{2,6},{3,7},{4,0},{5,1},{6,2},{7,3},{8,12},{9,13},{10,... | collective-permute-start | bytes 983048 | tf_op jit(solution)/shard_map/ppermute | solution.py:23
  129.4 8.7 %collective-permute-start.29 = (bf16[80,2048]{1,0:T(8,128)(2,1)S(1)}, bf16[80,2048]{1,0:T(8,128)(2,1)S(1)}, u32[]{:S(2)}, u32[]{:S(2)}) collective-permute-start(bf16[80,2048]{1,0:T(8,128)(2,1)S(1)} %get-tuple-element.61), channel_id=1, source_target_pairs={{0,1},{1,0},{2,3},{3,2},{4,5},{5,4},{6,7},{7,6},{8,9},{9,8},{10,11... | collective-permute-start | bytes 983048 | tf_op jit(solution)/shard_map/ppermute | solution.py:23
  129.4 9.8 %collective-permute-start.28 = (bf16[80,2048]{1,0:T(8,128)(2,1)S(1)}, bf16[80,2048]{1,0:T(8,128)(2,1)S(1)}, u32[]{:S(2)}, u32[]{:S(2)}) collective-permute-start(bf16[80,2048]{1,0:T(8,128)(2,1)S(1)} %get-tuple-element.59), channel_id=1, source_target_pairs={{0,1},{1,0},{2,3},{3,2},{4,5},{5,4},{6,7},{7,6},{8,9},{9,8},{10,11... | collective-permute-start | bytes 983048 | tf_op jit(solution)/shard_map/ppermute | solution.py:23
  138.2 7.6 %collective-permute-start.44 = (bf16[80,2048]{1,0:T(8,128)(2,1)S(1)}, bf16[80,2048]{1,0:T(8,128)(2,1)S(1)}, u32[]{:S(2)}, u32[]{:S(2)}) collective-permute-start(bf16[80,2048]{1,0:T(8,128)(2,1)S(1)} %add.14.refs_3_), channel_id=1, source_target_pairs={{0,2},{1,3},{2,0},{3,1},{4,6},{5,7},{6,4},{7,5},{8,10},{9,11},{10,... | collective-permute-start | bytes 983048 | tf_op jit(solution)/shard_map/ppermute | solution.py:23
  138.8 7.8 %collective-permute-start.22 = (bf16[80,2048]{1,0:T(8,128)(2,1)S(1)}, bf16[80,2048]{1,0:T(8,128)(2,1)S(1)}, u32[]{:S(2)}, u32[]{:S(2)}) collective-permute-start(bf16[80,2048]{1,0:T(8,128)(2,1)S(1)} %get-tuple-element.56), channel_id=1, source_target_pairs={{0,1},{1,0},{2,3},{3,2},{4,5},{5,4},{6,7},{7,6},{8,9},{9,8},{10,11... | collective-permute-start | bytes 983048 | tf_op jit(solution)/shard_map/ppermute | solution.py:23
  138.8 8.5 %collective-permute-start.21 = (bf16[80,2048]{1,0:T(8,128)(2,1)S(1)}, bf16[80,2048]{1,0:T(8,128)(2,1)S(1)}, u32[]{:S(2)}, u32[]{:S(2)}) collective-permute-start(bf16[80,2048]{1,0:T(8,128)(2,1)S(1)} %get-tuple-element.54), channel_id=1, source_target_pairs={{0,1},{1,0},{2,3},{3,2},{4,5},{5,4},{6,7},{7,6},{8,9},{9,8},{10,11... | collective-permute-start | bytes 983048 | tf_op jit(solution)/shard_map/ppermute | solution.py:23
  139.3 17.4 %collective-permute-start.47 = (bf16[80,2048]{1,0:T(8,128)(2,1)S(1)}, bf16[80,2048]{1,0:T(8,128)(2,1)S(1)}, u32[]{:S(2)}, u32[]{:S(2)}) collective-permute-start(bf16[80,2048]{1,0:T(8,128)(2,1)S(1)} %add.13.refs_2_), channel_id=1, source_target_pairs={{0,8},{1,9},{2,10},{3,11},{4,12},{5,13},{6,14},{7,15},{8,0},{9,1},... | collective-permute-start | bytes 983048 | tf_op jit(solution)/shard_map/ppermute | solution.py:23
  145.9 13.6 %collective-permute-start.46 = (bf16[80,2048]{1,0:T(8,128)(2,1)S(1)}, bf16[80,2048]{1,0:T(8,128)(2,1)S(1)}, u32[]{:S(2)}, u32[]{:S(2)}) collective-permute-start(bf16[80,2048]{1,0:T(8,128)(2,1)S(1)} %add.15.refs_2_), channel_id=1, source_target_pairs={{0,4},{1,5},{2,6},{3,7},{4,0},{5,1},{6,2},{7,3},{8,12},{9,13},{10,... | collective-permute-start | bytes 983048 | tf_op jit(solution)/shard_map/ppermute | solution.py:23
  146.6 12.9 %collective-permute-start.45 = (bf16[80,2048]{1,0:T(8,128)(2,1)S(1)}, bf16[80,2048]{1,0:T(8,128)(2,1)S(1)}, u32[]{:S(2)}, u32[]{:S(2)}) collective-permute-start(bf16[80,2048]{1,0:T(8,128)(2,1)S(1)} %add.16), channel_id=1, source_target_pairs={{0,2},{1,3},{2,0},{3,1},{4,6},{5,7},{6,4},{7,5},{8,10},{9,11},{10,... | collective-permute-start | bytes 983048 | tf_op jit(solution)/shard_map/ppermute | solution.py:23
  (11 other events, 308.1 us)

commit v4 on v3

--- a/solution.py
+++ b/solution.py
@@ -14,6 +14,19 @@
 EPSILON = 1e-06
 MIB = 1 << 20
 BF16, F32 = jnp.bfloat16, jnp.float32
+PLAN = {
+    "seq": ["E0", "E1", "E3", "f3", "E2", "t3", "f2", "t2", "f1", "t1", "f0"],
+    "tok": {"E1": ["x2"]},
+    "gate": {"c1": ["E0"], "c3": ["E1"], "c2": ["E3"]},
+    "forward": True,
+    "parts": 1,
+    "cost": {"attention": 3000000000, "pack_queries": 6000000000, "norm": 6000000000},
+    "mtok": ["pq"],
+    "cgate": ["q1", "q2", "q3"],
+    "pgate": ["cb"],
+    "att": [3, 2, 1, "add", 0, "sel"],
+    "atok": ["q1", "q2"],
+}
 NT = (((1,), (1,)), ((), ()))
 ANY = pl.BlockSpec(memory_space=pl.ANY)
 VMEM = pl.BlockSpec(memory_space=pltpu.VMEM)
@@ -63,7 +76,7 @@
         out_specs=out_specs,
         scratch_shapes=list(scratch),
         compiler_params=pltpu.CompilerParams(vmem_limit_bytes=limit * MIB),
-        cost_estimate=pl.CostEstimate(flops=1, bytes_accessed=1, transcendentals=0),
+        cost_estimate=pl.CostEstimate(flops=PLAN["cost"].get(name, 1), bytes_accessed=1, transcendentals=0),
         name=name,
         **more,
     )(*operands, *tokens)
@@ -180,7 +193,7 @@
 
 def attention_kernel(inner, group, rows, qf, *refs):
     caches, projections = refs[: 2 * inner], refs[2 * inner : 3 * inner]
-    out, keys, values, attention = refs[3 * inner :]
+    outs, (keys, values, attention) = refs[3 * inner : -3], refs[-3:]
     block = keys.shape[0] // (2 * inner)
     start = caches[0].shape[0] - 2 * block
     for j in range(2 * inner):
@@ -208,8 +221,9 @@
                 h * rows : (h + 1) * rows, :
             ]
     depth = projections[0].shape[0]
-    wide = math.gcd(out.shape[1], 512)
-    for c in range(0, out.shape[1], wide):
+    columns = outs[0].shape[1]
+    wide = math.gcd(columns, 512)
+    for c in range(0, columns * len(outs), wide):
         total = jnp.dot(
             attention[:, :depth], projections[0][:, c : c + wide], preferred_element_type=F32
         )
@@ -219,7 +233,8 @@
                 projections[j][:, c : c + wide],
                 preferred_element_type=F32,
             )
-        out[:, c : c + wide] = total.astype(out.dtype)
+        out = outs[c // columns]
+        out[:, c % columns : c % columns + wide] = total.astype(out.dtype)
 
 
 def select_kernel(inner, local, capacity, count, *refs):
@@ -271,9 +286,9 @@
         share[0, e * capacity : (e + 1) * capacity, :] = jnp.broadcast_to(value, (capacity, LANES))
 
 
-def norm_kernel(residual, gain, own, *refs):
-    arrived, (hidden, normed) = refs[:-2], refs[-2:]
-    total = own[...]
+def norm_kernel(count, residual, gain, *refs):
+    arrived, narrow, (hidden, normed) = refs[: -2 - count], refs[-2 - count : -2], refs[-2:]
+    total = jnp.concatenate([ref[...].astype(F32) for ref in narrow], axis=1)
     for ref in arrived:
         total = total + ref[...].astype(F32)
     rounded = (residual[...].astype(F32) + total).astype(BF16)
@@ -318,17 +333,24 @@
             out[:, c : c + wide] = total[at * rows : (at + 1) * rows, :]
 
 
-def hold_kernel(source, out, sem):
-    copy = pltpu.make_async_copy(source, out, sem)
-    copy.start()
-    copy.wait()
-
-
-def add_kernel(*refs):
-    total = refs[0][...].astype(F32)
-    for ref in refs[1:-1]:
-        total = total + ref[...].astype(F32)
-    refs[-1][...] = total.astype(refs[-1].dtype)
+def add_kernel(at, *refs):
+    out = refs[-1]
+    wide = out.shape[1]
+    total = jnp.zeros(out.shape, F32)
+    for ref in refs[:-1]:
+        total = total + (ref[:, at : at + wide] if ref.shape[1] > wide else ref[...]).astype(F32)
+    out[...] = total.astype(out.dtype)
+
+
+def gather_columns_kernel(count, *refs):
+    out, narrow = refs[-1], refs[-1 - count : -1]
+    wide = narrow[0].shape[1]
+    for p in range(count):
+        at = slice(p * wide, (p + 1) * wide)
+        total = narrow[p][...].astype(F32)
+        for ref in refs[: -1 - count]:
+            total = total + ref[:, at].astype(F32)
+        out[:, at] = total.astype(out.dtype)
 
 
 def local_program(
@@ -387,9 +409,10 @@
         pack_queries_kernel, (group + 2) * rows, (queries, fresh), "pack_queries", (packed[0],)
     )
     asked = [packed[0]] + [swap(packed[k], n, k * inner) for k in range(1, OUTERS)]
-    half_outers = OUTERS // 2
-    caches, tokens = [], (packed[0],)
-    for at in (0, half_outers):
+    half_outers, half = OUTERS // 2, inner // 2
+    front = {"pq": packed[0], "q1": asked[1], "q2": asked[2], "q3": asked[3]}
+    caches, tokens = [], [front[t] for t in PLAN["mtok"]]
+    for at, name in ((0, "a"), (half_outers, "b")):
         merged = call(
             functools.partial(merge_kernel, keys),
             jax.ShapeDtypeStruct((half_outers * cache_rows, HEAD_SIZE), BF16),
@@ -400,24 +423,18 @@
             out_specs=ANY,
             scratch=[dma((3 * half_outers,))],
         )
-        caches += gather_inner(merged, n, *asked[1:])
+        caches += gather_inner(merged, n, *[front[t] for t in PLAN["cgate"]])
         tokens = (merged,)
-    projections = gather_inner(out_proj, n, caches[inner - 1], caches[-1])
-    projections[0] = call(
-        hold_kernel,
-        jax.ShapeDtypeStruct(out_proj.shape, BF16),
-        (out_proj,),
-        [ANY],
-        "hold",
-        (merged,),
-        out_specs=VMEM,
-        scratch=[dma],
-    )
-
-    def add(terms, tokens=()):
+        front["m" + name], front["y" + name], front["c" + name] = merged, caches[half - inner], caches[-1]
+    projections = gather_inner(out_proj, n, *[front[t] for t in PLAN["pgate"]])
+
+    parts = PLAN["parts"]
+    columns = width // parts
+
+    def add(terms, tokens=(), part=None):
         return call(
-            add_kernel,
-            jax.ShapeDtypeStruct((rows, width), BF16),
+            functools.partial(add_kernel, 0 if part is None else part * columns),
+            jax.ShapeDtypeStruct((rows, width if part is None else columns), BF16),
             terms,
             [VMEM] * len(terms),
             "add",
@@ -425,16 +442,23 @@
             out_specs=VMEM,
         )
 
-    def attend(k, tokens, kind):
+    def add_parts(terms, others, tokens):
+        done = []
+        for p in range(parts):
+            done.append(add(terms + [t[p] for t in others], tokens, p))
+            tokens = (done[-1],)
+        return done
+
+    def attend(k, tokens, kind, pieces=1):
         return call(
             functools.partial(attention_kernel, inner, group, rows),
-            jax.ShapeDtypeStruct((rows, width), kind),
+            [jax.ShapeDtypeStruct((rows, width // pieces), kind)] * pieces,
             (asked[k], *caches, *projections),
             [VMEM] * (1 + 3 * inner),
             "attention",
             tokens,
             limit=18,
-            out_specs=VMEM,
+            out_specs=[VMEM] * pieces,
             scratch=[
                 pltpu.VMEM((n * keys, HEAD_SIZE), BF16),
                 pltpu.VMEM((n * keys, HEAD_SIZE), BF16),
@@ -449,32 +473,44 @@
     ]
     kinds = [BF16, BF16, F32]
     last_half = half_outers - 1
-    far = attend(3, (asked[1], asked[2]), BF16)
-    across = attend(2, (far,), F32)
-    near = attend(1, (across,), BF16)
-    sent = add([across, swap(far, n, inner)], (near,))
-    own = attend(0, (sent,), F32)
-    home = [swap(near, n, inner), swap(sent, n, 2 * inner)]
-    selection = call(
-        functools.partial(select_kernel, inner, local, capacity, rows),
-        [jax.ShapeDtypeStruct((OUTERS, *s), d) for s, d in zip(selected, kinds)],
-        caches,
-        [pl.BlockSpec((gate_rows, LANES), lambda k: (jnp.minimum(k, last_half), 0))] * inner
-        + [pl.BlockSpec((gate_rows, LANES), lambda k: (jnp.maximum(k - half_outers, 0), 0))]
-        * inner,
-        "select",
-        (own,),
-        out_specs=[pl.BlockSpec((1, *s), lambda k: (k, 0, 0)) for s in selected],
-        grid=(OUTERS,),
-    )
+    def select(tokens):
+        return call(
+            functools.partial(select_kernel, inner, local, capacity, rows),
+            [jax.ShapeDtypeStruct((OUTERS, *s), d) for s, d in zip(selected, kinds)],
+            caches,
+            [pl.BlockSpec((gate_rows, LANES), lambda k: (jnp.minimum(k, last_half), 0))] * inner
+            + [pl.BlockSpec((gate_rows, LANES), lambda k: (jnp.maximum(k - half_outers, 0), 0))]
+            * inner,
+            "select",
+            tokens,
+            out_specs=[pl.BlockSpec((1, *s), lambda k: (k, 0, 0)) for s in selected],
+            grid=(OUTERS,),
+        )
+
+    parts_done, tokens = {}, [front[t] for t in PLAN["atok"]]
+    for step in PLAN["att"]:
+        if step == "sel":
+            selection = select(tokens)
+            tokens = (selection[0],)
+            continue
+        if step == "add":
+            parts_done[step] = add_parts(parts_done[2], [far], tokens)
+        else:
+            kind, pieces = (F32 if step in (0, 2) else BF16), (parts if step == 3 else 1)
+            parts_done[step] = list(attend(step, tokens, kind, pieces))
+        tokens = (parts_done[step][-1],)
+        if step == 3:
+            far = [swap(a, n, inner) for a in parts_done[3]]
+    own, near = parts_done[0][0], swap(parts_done[1][0], n, inner)
+    home = [swap(a, n, 2 * inner) for a in parts_done["add"]]
     block = whole((rows, width))
     hidden, normed = call(
-        norm_kernel,
+        functools.partial(norm_kernel, parts),
         [jax.ShapeDtypeStruct((rows, width), BF16)] * 2,
-        (residual, gain.reshape(1, -1), own, *home),
-        [block, whole((1, width)), block, block, block],
+        (residual, gain.reshape(1, -1), own, near, *home),
+        [block, whole((1, width)), block, block] + [whole((rows, columns))] * parts,
         "norm",
-        (selection[0],),
+        tokens,
         out_specs=[block, block],
         grid=(1,),
     )
@@ -498,46 +534,70 @@
         )
 
     bits = [1 << b for b in range(inner.bit_length() - 1)]
-    first, second = swap(normed, n, inner), swap(normed, n, 2 * inner)
-    around = gather_inner(normed, n)
-    slots = [None] * OUTERS
-
-    def fold(k):
-        middle = len(slots[k]) // 2
-        arrived = [swap(a, n, bits[0]) for a in slots[k][:middle - 1:-1]][::-1]
-        slots[k] = [[a, b] for a, b in zip(slots[k][:middle], arrived)]
-
-    def finish(k, tokens):
-        terms = slots[k]
-        for bit in bits[1:]:
-            middle = len(terms) // 2
-            sent = [add(t, tokens) for t in terms[middle:]]
-            terms = [t + [swap(a, n, bit)] for t, a in zip(terms[:middle], sent)]
-        return terms[0], sent[0]
-
-    third = swap(second, n, inner)
-    slots[0] = experts(0, around, ())
-    fold(0)
-    done = slots[0][0][0]
-    slots[1] = experts(1, gather_inner(first, n, done), (done, second))
-    fold(1)
-    done = slots[1][0][0]
-    slots[3] = experts(3, gather_inner(third, n, done), (done,))
-    fold(3)
-    done = slots[3][0][0]
-    terms, sent = finish(3, (done,))
-    slots[2] = experts(2, gather_inner(second, n, done), (sent,))
-    fold(2)
-    total = add(terms, (slots[2][0][0],))
-    far = swap(total, n, inner)
-    terms, sent = finish(2, (total,))
-    total = add(terms + [far], (sent,))
-    across = swap(total, n, 2 * inner)
-    terms, sent = finish(1, (total,))
-    total = add(terms, (sent,))
-    near = swap(total, n, inner)
-    terms, sent = finish(0, (total,))
-    return hidden, add(terms + [near, across])
+    made = {"x0": normed, "x1": swap(normed, n, inner), "x2": swap(normed, n, 2 * inner)}
+
+    def waiting(array, name):
+        gates = PLAN["gate"].get(name, ())
+        return after(array, *[get(t) for t in gates]) if gates else array
+
+    def fold(slots):
+        middle = len(slots) // 2
+        arrived = [swap(a, n, bits[0]) for a in slots[: middle - 1 : -1]][::-1]
+        return [[a, b] for a, b in zip(slots[:middle], arrived)]
+
+    def get(name):
+        if name not in made:
+            made[name] = make(name[0], int(name[1]), name)
+        return made[name]
+
+    def make(kind, k, name):
+        if name == "x3":
+            return swap(waiting(get("x2"), name), n, inner)
+        if kind == "y":
+            return swap(waiting(get("x%d" % k), name), n, half)
+        at = PLAN["seq"].index(name)
+        tokens = [get(t) for t in PLAN["seq"][max(at - 1, 0) : at] + PLAN["tok"].get(name, [])]
+        if kind == "E":
+            gates = [get(t) for t in PLAN["gate"].get("c%d" % k, ())]
+            outs = experts(k, gather_inner(get("x%d" % k), n, *gates, far=get("y%d" % k)), tokens)
+            made["slots%d" % k] = fold(outs)
+            return outs[0]
+        if kind == "f":
+            get("E%d" % k)
+            terms = made["slots%d" % k]
+            for bit in bits[1:]:
+                middle = len(terms) // 2
+                sent = [add(t, tokens) for t in terms[middle:]]
+                terms = [t + [swap(a, n, bit)] for t, a in zip(terms[:middle], sent)]
+            made["terms%d" % k] = terms[0]
+            return sent[0]
+        get("f%d" % k)
+        terms = made["terms%d" % k]
+        if not PLAN["forward"] or k == 1:
+            return add(terms, tokens)
+        if k == 2:
+            get("t3")
+        made["sums%d" % k] = add_parts(terms, [made["far"]] if k == 2 else [], tokens)
+        if k == 3:
+            made["far"] = [swap(a, n, inner) for a in made["sums3"]]
+        return made["sums%d" % k][-1]
+
+    for name in PLAN["seq"]:
+        get(name)
+    near = swap(made["t1"], n, inner)
+    if not PLAN["forward"]:
+        arrivals = [near, swap(made["t2"], n, 2 * inner), swap(made["t3"], n, 3 * inner)]
+        return hidden, add(made["terms0"] + arrivals)
+    across = [swap(a, n, 2 * inner) for a in made["sums2"]]
+    total = call(
+        functools.partial(gather_columns_kernel, parts),
+        jax.ShapeDtypeStruct((rows, width), BF16),
+        made["terms0"] + [near] + across,
+        [VMEM] * (len(made["terms0"]) + 1 + parts),
+        "add",
+        out_specs=VMEM,
+    )
+    return hidden, total
 
 
 def solution(mesh):

time: 161 us -> 157 us (0.975)
  waiting for transfers between devices: 79.1 us -> 71.5 us
  starting transfers between devices: 38.7 us -> 44.6 us
  local copies, waits for them, and re-layouts: 3.09 us -> 0.99 us
    ppermute x48, waiting for transfers between devices: 79.1 us -> 71.5 us  [swap(): return lax.ppermute(array, 'ctx', [(i, i ^ offset) for i in range(n)])]
    ppermute x48, starting transfers between devices: 38.7 us -> 44.6 us  [swap(): return lax.ppermute(array, 'ctx', [(i, i ^ offset) for i in range(n)])]
    unnamed x22, local copies, waits for them, and re-layouts: 3.09 us -> 0.99 us
    pallas_call x24 -> x23, Pallas kernels: 38.6 us -> 38.4 us  [call(): pl.pallas_call(body, out_shape=outs, in_specs=list(specs) + [ANY] * len(t...]
  transfers between devices with their start and end apart: 48 -> 48, of which waited for: 22 -> 21; matrix products, arithmetic and copies ran while one was open for 0% -> 0% of each run, Pallas kernels for 21% -> 21%
where the time goes in v4:
time: 157 us
  waiting for transfers between devices  71.5 us (46%)
  starting transfers between devices  44.6 us (28%)
  Pallas kernels  38.4 us (24%)
    ppermute x48, waiting for transfers between devices, swap(): return lax.ppermute(array, 'ctx', [(i, i ^ offset) for i in range(n)])  71.5 us
    ppermute x48, starting transfers between devices, swap(): return lax.ppermute(array, 'ctx', [(i, i ^ offset) for i in range(n)])  44.6 us
    pallas_call x23, Pallas kernels, call(): pl.pallas_call(body, out_shape=outs, in_specs=list(specs) + [ANY] * len(t...  38.4 us
  transfers between devices with their start and end apart: 48, of which 21 were waited for; matrix products, arithmetic and copies ran while one was open for 0% of the time, Pallas kernels for 21%

profile of v4, /device:TPU:0, one launch (start us, length us, event | category | flops | bytes accessed | tf_op | source)
XLA Modules:
  0.0 156.5 jit_solution(14218293342607242756)
XLA Ops:
  0.6 3.0 %collective-permute-start.13 = (bf16[256,2048]{1,0:T(8,128)(2,1)}, bf16[256,2048]{1,0:T(8,128)(2,1)S(1)}, u32[]{:S(2)}, u32[]{:S(2)}) collective-permute-start(bf16[256,2048]{1,0:T(8,128)(2,1)} %refs_9_.7), channel_id=1, source_target_pairs={{0,2},{1,3},{2,0},{3,1},{4,6},{5,7},{6,4},{7,5},{8,10},{9,11},{10,... | collective-permute-start | bytes 3145736 | tf_op jit(solution)/shard_map/ppermute | solution.py:36
  3.7 1.9 %pack_cache.1 = (bf16[272,128]{1,0:T(8,128)(2,1)}, bf16[272,128]{1,0:T(8,128)(2,1)}, bf16[272,128]{1,0:T(8,128)(2,1)}, bf16[272,128]{1,0:T(8,128)(2,1)}) custom-call(bf16[2,128,512]{2,1,0:T(8,128)(2,1)} %refs_0_.3, s32[8,80]{1,0:T(8,128)} %bitcast.9, f32[8,80]{1,0:T(8,128)} %bitcast.10, s32[1,32]{1,0:T(1,128)} %bitcast.11), custom_call_target="tpu_custom_call" | custom-call | flops 1 | bytes 1 | tf_op jit(solution)/shard_map/pack_cache/pallas_call | solution.py:72
  5.5 1.6 %collective-permute-start = (bf16[272,128]{1,0:T(8,128)(2,1)}, bf16[272,128]{1,0:T(8,128)(2,1)S(1)}, u32[]{:S(2)}, u32[]{:S(2)}) collective-permute-start(bf16[272,128]{1,0:T(8,128)(2,1)} %get-tuple-element.39), channel_id=1, source_target_pairs={{0,4},{1,5},{2,6},{3,7},{4,0},{5,1},{6,2},{7,3},{8,12},{9,13},{10,... | collective-permute-start | bytes 208904 | tf_op jit(solution)/shard_map/ppermute | solution.py:36
  7.2 2.6 %collective-permute-start.7 = (bf16[272,128]{1,0:T(8,128)(2,1)}, bf16[272,128]{1,0:T(8,128)(2,1)S(1)}, u32[]{:S(2)}, u32[]{:S(2)}) collective-permute-start(bf16[272,128]{1,0:T(8,128)(2,1)} %get-tuple-element.44), channel_id=1, source_target_pairs={{0,8},{1,9},{2,10},{3,11},{4,12},{5,13},{6,14},{7,15},{8,0},{9,1},... | collective-permute-start | bytes 208904 | tf_op jit(solution)/shard_map/ppermute | solution.py:36
  10.0 2.1 %pack_queries.1 = (bf16[800,128]{1,0:T(8,128)(2,1)}, bf16[800,128]{1,0:T(8,128)(2,1)}, bf16[800,128]{1,0:T(8,128)(2,1)}, bf16[800,128]{1,0:T(8,128)(2,1)}) custom-call(bf16[80,4096]{1,0:T(8,128)(2,1)} %refs_0_.4, bf16[2,80,512]{2,1,0:T(8,128)(2,1)} %refs_1_.1, bf16[272,128]{1,0:T(8,128)(2,1)} %get-tuple-element.37.refs_2_.refs_0_), custom_call_target="tpu_custom_call" | custom-call | flops 6000000000 | bytes 1 | tf_op jit(solution)/shard_map/pack_queries/pallas_call | solution.py:72
  12.8 3.5 %collective-permute-start.4 = (bf16[800,128]{1,0:T(8,128)(2,1)}, bf16[800,128]{1,0:T(8,128)(2,1)S(1)}, u32[]{:S(2)}, u32[]{:S(2)}) collective-permute-start(bf16[800,128]{1,0:T(8,128)(2,1)} %get-tuple-element.41), channel_id=1, source_target_pairs={{0,8},{1,9},{2,10},{3,11},{4,12},{5,13},{6,14},{7,15},{8,0},{9,1},... | collective-permute-start | bytes 614408 | tf_op jit(solution)/shard_map/ppermute | solution.py:36
  16.3 1.6 %collective-permute-start.5 = (bf16[800,128]{1,0:T(8,128)(2,1)}, bf16[800,128]{1,0:T(8,128)(2,1)S(1)}, u32[]{:S(2)}, u32[]{:S(2)}) collective-permute-start(bf16[800,128]{1,0:T(8,128)(2,1)} %get-tuple-element.42), channel_id=1, source_target_pairs={{0,12},{1,13},{2,14},{3,15},{4,8},{5,9},{6,10},{7,11},{8,4},{9,5},... | collective-permute-start | bytes 614408 | tf_op jit(solution)/shard_map/ppermute | solution.py:36
  17.9 0.9 copy-done
  19.9 3.1 %collective-permute-done.3.refs_13_.refs_0_ = bf16[800,128]{1,0:T(8,128)(2,1)S(1)} collective-permute-done((bf16[800,128]{1,0:T(8,128)(2,1)}, bf16[800,128]{1,0:T(8,128)(2,1)S(1)}, u32[]{:S(2)}, u32[]{:S(2)}) %collective-permute-start.3) | collective-permute-done | bytes 204832 | tf_op jit(solution)/shard_map/ppermute | solution.py:36
  23.1 8.3 %collective-permute-done.4.refs_14_.refs_0_ = bf16[800,128]{1,0:T(8,128)(2,1)S(1)} collective-permute-done((bf16[800,128]{1,0:T(8,128)(2,1)}, bf16[800,128]{1,0:T(8,128)(2,1)S(1)}, u32[]{:S(2)}, u32[]{:S(2)}) %collective-permute-start.4) | collective-permute-done | bytes 204832 | tf_op jit(solution)/shard_map/ppermute | solution.py:36
  33.9 4.9 %collective-permute-done.2.refs_3_.refs_2_ = bf16[544,128]{1,0:T(8,128)(2,1)S(1)} collective-permute-done((bf16[544,128]{1,0:T(8,128)(2,1)S(1)}, bf16[544,128]{1,0:T(8,128)(2,1)S(1)}, u32[]{:S(2)}, u32[]{:S(2)}) %collective-permute-start.2) | collective-permute-done | bytes 139296 | tf_op jit(solution)/shard_map/ppermute | solution.py:36
  38.8 1.3 collective-permute-done.6.refs_4_.refs_3_
  40.2 3.3 %attention.4.refs_13_ = bf16[80,2048]{1,0:T(8,128)(2,1)S(1)} custom-call(bf16[800,128]{1,0:T(8,128)(2,1)S(1)} %collective-permute-done.5.refs_0_, bf16[544,128]{1,0:T(8,128)(2,1)S(1)} %merge.2.refs_2_.refs_1_.refs_0_, bf16[544,128]{1,0:T(8,128)(2,1)S(1)} %collective-permute-done.1.refs_2_.refs_1_, ...), custom_call_target="tpu_custom_call" | custom-call | flops 3000000000 | bytes 1 | tf_op jit(solution)/shard_map/attention/pallas_call | solution.py:72
  43.4 3.1 %collective-permute-start.15 = (bf16[80,2048]{1,0:T(8,128)(2,1)S(1)}, bf16[80,2048]{1,0:T(8,128)(2,1)S(1)}, u32[]{:S(2)}, u32[]{:S(2)}) collective-permute-start(bf16[80,2048]{1,0:T(8,128)(2,1)S(1)} %attention.4.refs_13_), channel_id=1, source_target_pairs={{0,4},{1,5},{2,6},{3,7},{4,0},{5,1},{6,2},{7,3},{8,12},{9,13},{10,... | collective-permute-start | bytes 983048 | tf_op jit(solution)/shard_map/ppermute | solution.py:36
  46.5 3.3 %attention.5.refs_13_.refs_0_ = f32[80,2048]{1,0:T(8,128)S(1)} custom-call(bf16[800,128]{1,0:T(8,128)(2,1)S(1)} %collective-permute-done.4.refs_14_.refs_0_, bf16[544,128]{1,0:T(8,128)(2,1)S(1)} %merge.2.refs_2_.refs_1_.refs_0_, bf16[544,128]{1,0:T(8,128)(2,1)S(1)} %collective-permute-done.1.refs_2_.refs_1_, ...), custom_call_target="tpu_custom_call" | custom-call | flops 3000000000 | bytes 1 | tf_op jit(solution)/shard_map/attention/pallas_call | solution.py:72
  49.8 3.3 %attention.6.refs_2_ = bf16[80,2048]{1,0:T(8,128)(2,1)S(1)} custom-call(bf16[800,128]{1,0:T(8,128)(2,1)S(1)} %collective-permute-done.3.refs_13_.refs_0_, bf16[544,128]{1,0:T(8,128)(2,1)S(1)} %merge.2.refs_2_.refs_1_.refs_0_, bf16[544,128]{1,0:T(8,128)(2,1)S(1)} %collective-permute-done.1.refs_2_.refs_1_, ...), custom_call_target="tpu_custom_call" | custom-call | flops 3000000000 | bytes 1 | tf_op jit(solution)/shard_map/attention/pallas_call | solution.py:72
  53.2 1.4 collective-permute-done.15.refs_1_
  54.6 3.0 %collective-permute-start.17 = (bf16[80,2048]{1,0:T(8,128)(2,1)S(1)}, bf16[80,2048]{1,0:T(8,128)(2,1)S(1)}, u32[]{:S(2)}, u32[]{:S(2)}) collective-permute-start(bf16[80,2048]{1,0:T(8,128)(2,1)S(1)} %add.9.refs_13_), channel_id=1, source_target_pairs={{0,8},{1,9},{2,10},{3,11},{4,12},{5,13},{6,14},{7,15},{8,0},{9,1},... | collective-permute-start | bytes 983048 | tf_op jit(solution)/shard_map/ppermute | solution.py:36
  57.6 3.3 %attention.7.refs_8_.refs_2_ = f32[80,2048]{1,0:T(8,128)S(1)} custom-call(bf16[800,128]{1,0:T(8,128)(2,1)S(1)} %copy-done.1, bf16[544,128]{1,0:T(8,128)(2,1)S(1)} %merge.2.refs_2_.refs_1_.refs_0_, bf16[544,128]{1,0:T(8,128)(2,1)S(1)} %collective-permute-done.1.refs_2_.refs_1_, bf16[544,128]{1,0:T(8,128)(2,1)S(1)} %collective-permute-done.2.refs_3_.refs_2_, ...), custom_call_target="tpu_custom_call" | custom-call | flops 3000000000 | bytes 1 | tf_op jit(solution)/shard_map/attention/pallas_call | solution.py:72
  60.9 3.4 %select.1 = (bf16[4,256,320]{2,1,0:T(8,128)(2,1)S(1)}, bf16[4,320,256]{2,1,0:T(8,128)(2,1)S(1)}, f32[4,256,128]{2,1,0:T(8,128)S(1)}) custom-call(bf16[544,128]{1,0:T(8,128)(2,1)S(1)} %merge.2.refs_2_.refs_1_.refs_0_, bf16[544,128]{1,0:T(8,128)(2,1)S(1)} %collective-permute-done.1.refs_2_.refs_1_, ...), custom_call_target="tpu_custom_call" | custom-call | flops 1 | bytes 1 | tf_op jit(solution)/shard_map/select/pallas_call | solution.py:72
  64.3 4.2 %collective-permute-done.16.refs_3_ = bf16[80,2048]{1,0:T(8,128)(2,1)S(1)} collective-permute-done((bf16[80,2048]{1,0:T(8,128)(2,1)S(1)}, bf16[80,2048]{1,0:T(8,128)(2,1)S(1)}, u32[]{:S(2)}, u32[]{:S(2)}) %collective-permute-start.16) | collective-permute-done | bytes 327712 | tf_op jit(solution)/shard_map/ppermute | solution.py:36
  68.6 3.3 %collective-permute-done.17.refs_4_ = bf16[80,2048]{1,0:T(8,128)(2,1)S(1)} collective-permute-done((bf16[80,2048]{1,0:T(8,128)(2,1)S(1)}, bf16[80,2048]{1,0:T(8,128)(2,1)S(1)}, u32[]{:S(2)}, u32[]{:S(2)}) %collective-permute-start.17) | collective-permute-done | bytes 327712 | tf_op jit(solution)/shard_map/ppermute | solution.py:36
  73.3 2.8 %collective-permute-start.27 = (bf16[80,2048]{1,0:T(8,128)(2,1)S(1)}, bf16[80,2048]{1,0:T(8,128)(2,1)S(1)}, u32[]{:S(2)}, u32[]{:S(2)}) collective-permute-start(bf16[80,2048]{1,0:T(8,128)(2,1)S(1)} %get-tuple-element.50.refs_0_), channel_id=1, source_target_pairs={{0,8},{1,9},{2,10},{3,11},{4,12},{5,13},{6,14},{7,15},{8,0},{9,1},... | collective-permute-start | bytes 983048 | tf_op jit(solution)/shard_map/ppermute | solution.py:36
  76.2 3.7 %collective-permute-done.19.refs_2_ = bf16[80,2048]{1,0:T(8,128)(2,1)S(1)} collective-permute-done((bf16[80,2048]{1,0:T(8,128)(2,1)S(1)}, bf16[80,2048]{1,0:T(8,128)(2,1)S(1)}, u32[]{:S(2)}, u32[]{:S(2)}) %collective-permute-start.19) | collective-permute-done | bytes 327712 | tf_op jit(solution)/shard_map/ppermute | solution.py:36
  79.9 6.7 %collective-permute-done.23.refs_0_ = bf16[80,2048]{1,0:T(8,128)(2,1)S(1)} collective-permute-done((bf16[80,2048]{1,0:T(8,128)(2,1)S(1)}, bf16[80,2048]{1,0:T(8,128)(2,1)S(1)}, u32[]{:S(2)}, u32[]{:S(2)}) %collective-permute-start.23) | collective-permute-done | bytes 327712 | tf_op jit(solution)/shard_map/ppermute | solution.py:36
  86.6 1.7 %collective-permute-start.25 = (bf16[80,2048]{1,0:T(8,128)(2,1)S(1)}, bf16[80,2048]{1,0:T(8,128)(2,1)S(1)}, u32[]{:S(2)}, u32[]{:S(2)}) collective-permute-start(bf16[80,2048]{1,0:T(8,128)(2,1)S(1)} %collective-permute-done.23.refs_0_), channel_id=1, source_target_pairs={{0,2},{1,3},{2,0},{3,1},{4,6},{5,7},{6,4},{7,5},{8,10},{9,11},{10,... | collective-permute-start | bytes 983048 | tf_op jit(solution)/shard_map/ppermute | solution.py:36
  88.3 1.1 collective-permute-done.27.refs_10_.refs_0_
  89.6 3.7 %experts.4 = (bf16[80,2048]{1,0:T(8,128)(2,1)S(1)}, bf16[80,2048]{1,0:T(8,128)(2,1)S(1)}, bf16[80,2048]{1,0:T(8,128)(2,1)S(1)}, bf16[80,2048]{1,0:T(8,128)(2,1)S(1)}) custom-call(bf16[80,2048]{1,0:T(8,128)(2,1)S(1)} %get-tuple-element.50.refs_0_, bf16[80,2048]{1,0:T(8,128)(2,1)S(1)} %collective-permute-done.18.refs_1_, ...), custom_call_target="tpu_custom_call" | custom-call | flops 1 | bytes 1 | tf_op jit(solution)/shard_map/experts/pallas_call | solution.py:72
  93.9 2.6 %collective-permute-done.32.refs_0_ = bf16[80,2048]{1,0:T(8,128)(2,1)S(1)} collective-permute-done((bf16[80,2048]{1,0:T(8,128)(2,1)S(1)}, bf16[80,2048]{1,0:T(8,128)(2,1)S(1)}, u32[]{:S(2)}, u32[]{:S(2)}) %collective-permute-start.32) | collective-permute-done | bytes 327712 | tf_op jit(solution)/shard_map/ppermute | solution.py:36
  96.5 1.6 %collective-permute-start.34 = (bf16[80,2048]{1,0:T(8,128)(2,1)S(1)}, bf16[80,2048]{1,0:T(8,128)(2,1)S(1)}, u32[]{:S(2)}, u32[]{:S(2)}) collective-permute-start(bf16[80,2048]{1,0:T(8,128)(2,1)S(1)} %collective-permute-done.32.refs_0_), channel_id=1, source_target_pairs={{0,2},{1,3},{2,0},{3,1},{4,6},{5,7},{6,4},{7,5},{8,10},{9,11},{10,... | collective-permute-start | bytes 983048 | tf_op jit(solution)/shard_map/ppermute | solution.py:36
  98.2 3.7 %experts.5 = (bf16[80,2048]{1,0:T(8,128)(2,1)S(1)}, bf16[80,2048]{1,0:T(8,128)(2,1)S(1)}, bf16[80,2048]{1,0:T(8,128)(2,1)S(1)}, bf16[80,2048]{1,0:T(8,128)(2,1)S(1)}) custom-call(bf16[80,2048]{1,0:T(8,128)(2,1)S(1)} %collective-permute-done.23.refs_0_, bf16[80,2048]{1,0:T(8,128)(2,1)S(1)} %collective-permute-done.24.refs_1_, ...), custom_call_target="tpu_custom_call" | custom-call | flops 1 | bytes 1 | tf_op jit(solution)/shard_map/experts/pallas_call | solution.py:72
  101.8 1.9 %collective-permute-done.34.refs_2_ = bf16[80,2048]{1,0:T(8,128)(2,1)S(1)} collective-permute-done((bf16[80,2048]{1,0:T(8,128)(2,1)S(1)}, bf16[80,2048]{1,0:T(8,128)(2,1)S(1)}, u32[]{:S(2)}, u32[]{:S(2)}) %collective-permute-start.34) | collective-permute-done | bytes 327712 | tf_op jit(solution)/shard_map/ppermute | solution.py:36
  103.8 1.7 %collective-permute-start.31 = (bf16[80,2048]{1,0:T(8,128)(2,1)S(1)}, bf16[80,2048]{1,0:T(8,128)(2,1)S(1)}, u32[]{:S(2)}, u32[]{:S(2)}) collective-permute-start(bf16[80,2048]{1,0:T(8,128)(2,1)S(1)} %collective-permute-done.27.refs_10_.refs_0_), channel_id=1, source_target_pairs={{0,2},{1,3},{2,0},{3,1},{4,6},{5,7},{6,4},{7,5},{8,10},{9,11},{10,... | collective-permute-start | bytes 983048 | tf_op jit(solution)/shard_map/ppermute | solution.py:36
  105.7 3.7 %experts.6 = (bf16[80,2048]{1,0:T(8,128)(2,1)S(1)}, bf16[80,2048]{1,0:T(8,128)(2,1)S(1)}, bf16[80,2048]{1,0:T(8,128)(2,1)S(1)}, bf16[80,2048]{1,0:T(8,128)(2,1)S(1)}) custom-call(bf16[80,2048]{1,0:T(8,128)(2,1)S(1)} %collective-permute-done.32.refs_0_, bf16[80,2048]{1,0:T(8,128)(2,1)S(1)} %collective-permute-done.33.refs_1_, ...), custom_call_target="tpu_custom_call" | custom-call | flops 1 | bytes 1 | tf_op jit(solution)/shard_map/experts/pallas_call | solution.py:72
  109.8 4.1 %collective-permute-done.31.refs_2_ = bf16[80,2048]{1,0:T(8,128)(2,1)S(1)} collective-permute-done((bf16[80,2048]{1,0:T(8,128)(2,1)S(1)}, bf16[80,2048]{1,0:T(8,128)(2,1)S(1)}, u32[]{:S(2)}, u32[]{:S(2)}) %collective-permute-start.31) | collective-permute-done | bytes 327712 | tf_op jit(solution)/shard_map/ppermute | solution.py:36
  114.5 1.8 %collective-permute-start.41 = (bf16[80,2048]{1,0:T(8,128)(2,1)S(1)}, bf16[80,2048]{1,0:T(8,128)(2,1)S(1)}, u32[]{:S(2)}, u32[]{:S(2)}) collective-permute-start(bf16[80,2048]{1,0:T(8,128)(2,1)S(1)} %add.10.refs_9_), channel_id=1, source_target_pairs={{0,2},{1,3},{2,0},{3,1},{4,6},{5,7},{6,4},{7,5},{8,10},{9,11},{10,... | collective-permute-start | bytes 983048 | tf_op jit(solution)/shard_map/ppermute | solution.py:36
  116.3 3.9 %experts.7 = (bf16[80,2048]{1,0:T(8,128)(2,1)S(1)}, bf16[80,2048]{1,0:T(8,128)(2,1)S(1)}, bf16[80,2048]{1,0:T(8,128)(2,1)S(1)}, bf16[80,2048]{1,0:T(8,128)(2,1)S(1)}) custom-call(bf16[80,2048]{1,0:T(8,128)(2,1)S(1)} %collective-permute-done.27.refs_10_.refs_0_, bf16[80,2048]{1,0:T(8,128)(2,1)S(1)} %collective-permute-done.30.refs_1_, ...), custom_call_target="tpu_custom_call" | custom-call | flops 1 | bytes 1 | tf_op jit(solution)/shard_map/experts/pallas_call | solution.py:72
  120.8 3.4 %collective-permute-done.41.refs_2_ = bf16[80,2048]{1,0:T(8,128)(2,1)S(1)} collective-permute-done((bf16[80,2048]{1,0:T(8,128)(2,1)S(1)}, bf16[80,2048]{1,0:T(8,128)(2,1)S(1)}, u32[]{:S(2)}, u32[]{:S(2)}) %collective-permute-start.41) | collective-permute-done | bytes 327712 | tf_op jit(solution)/shard_map/ppermute | solution.py:36
  124.4 1.8 %collective-permute-start.42 = (bf16[80,2048]{1,0:T(8,128)(2,1)S(1)}, bf16[80,2048]{1,0:T(8,128)(2,1)S(1)}, u32[]{:S(2)}, u32[]{:S(2)}) collective-permute-start(bf16[80,2048]{1,0:T(8,128)(2,1)S(1)} %add.12.refs_4_), channel_id=1, source_target_pairs={{0,2},{1,3},{2,0},{3,1},{4,6},{5,7},{6,4},{7,5},{8,10},{9,11},{10,... | collective-permute-start | bytes 983048 | tf_op jit(solution)/shard_map/ppermute | solution.py:36
  126.2 1.6 %collective-permute-start.43 = (bf16[80,2048]{1,0:T(8,128)(2,1)S(1)}, bf16[80,2048]{1,0:T(8,128)(2,1)S(1)}, u32[]{:S(2)}, u32[]{:S(2)}) collective-permute-start(bf16[80,2048]{1,0:T(8,128)(2,1)S(1)} %add.11.refs_2_), channel_id=1, source_target_pairs={{0,4},{1,5},{2,6},{3,7},{4,0},{5,1},{6,2},{7,3},{8,12},{9,13},{10,... | collective-permute-start | bytes 983048 | tf_op jit(solution)/shard_map/ppermute | solution.py:36
  128.4 4.9 %collective-permute-done.42.refs_2_ = bf16[80,2048]{1,0:T(8,128)(2,1)S(1)} collective-permute-done((bf16[80,2048]{1,0:T(8,128)(2,1)S(1)}, bf16[80,2048]{1,0:T(8,128)(2,1)S(1)}, u32[]{:S(2)}, u32[]{:S(2)}) %collective-permute-start.42) | collective-permute-done | bytes 327712 | tf_op jit(solution)/shard_map/ppermute | solution.py:36
  133.2 1.5 collective-permute-done.43.refs_3_
  135.9 3.4 %collective-permute-start.47 = (bf16[80,2048]{1,0:T(8,128)(2,1)S(1)}, bf16[80,2048]{1,0:T(8,128)(2,1)S(1)}, u32[]{:S(2)}, u32[]{:S(2)}) collective-permute-start(bf16[80,2048]{1,0:T(8,128)(2,1)S(1)} %add.13.refs_2_), channel_id=1, source_target_pairs={{0,8},{1,9},{2,10},{3,11},{4,12},{5,13},{6,14},{7,15},{8,0},{9,1},... | collective-permute-start | bytes 983048 | tf_op jit(solution)/shard_map/ppermute | solution.py:36
  139.3 3.3 %collective-permute-done.44.refs_2_ = bf16[80,2048]{1,0:T(8,128)(2,1)S(1)} collective-permute-done((bf16[80,2048]{1,0:T(8,128)(2,1)S(1)}, bf16[80,2048]{1,0:T(8,128)(2,1)S(1)}, u32[]{:S(2)}, u32[]{:S(2)}) %collective-permute-start.44) | collective-permute-done | bytes 327712 | tf_op jit(solution)/shard_map/ppermute | solution.py:36
  142.7 1.7 %collective-permute-start.46 = (bf16[80,2048]{1,0:T(8,128)(2,1)S(1)}, bf16[80,2048]{1,0:T(8,128)(2,1)S(1)}, u32[]{:S(2)}, u32[]{:S(2)}) collective-permute-start(bf16[80,2048]{1,0:T(8,128)(2,1)S(1)} %add.15.refs_2_), channel_id=1, source_target_pairs={{0,4},{1,5},{2,6},{3,7},{4,0},{5,1},{6,2},{7,3},{8,12},{9,13},{10,... | collective-permute-start | bytes 983048 | tf_op jit(solution)/shard_map/ppermute | solution.py:36
  145.1 9.2 %collective-permute-done.47.refs_4_ = bf16[80,2048]{1,0:T(8,128)(2,1)S(1)} collective-permute-done((bf16[80,2048]{1,0:T(8,128)(2,1)S(1)}, bf16[80,2048]{1,0:T(8,128)(2,1)S(1)}, u32[]{:S(2)}, u32[]{:S(2)}) %collective-permute-start.47) | collective-permute-done | bytes 327712 | tf_op jit(solution)/shard_map/ppermute | solution.py:36
  154.3 1.3 collective-permute-done.46.refs_3_
  155.6 0.9 add.17
  (95 shorter events, 11.4 us)
Async XLA Ops:
  0.6 32.1 %collective-permute-start.13 = (bf16[256,2048]{1,0:T(8,128)(2,1)}, bf16[256,2048]{1,0:T(8,128)(2,1)S(1)}, u32[]{:S(2)}, u32[]{:S(2)}) collective-permute-start(bf16[256,2048]{1,0:T(8,128)(2,1)} %refs_9_.7), channel_id=1, source_target_pairs={{0,2},{1,3},{2,0},{3,1},{4,6},{5,7},{6,4},{7,5},{8,10},{9,11},{10,... | collective-permute-start | bytes 3145736 | tf_op jit(solution)/shard_map/ppermute | solution.py:36
  5.5 7.3 %collective-permute-start = (bf16[272,128]{1,0:T(8,128)(2,1)}, bf16[272,128]{1,0:T(8,128)(2,1)S(1)}, u32[]{:S(2)}, u32[]{:S(2)}) collective-permute-start(bf16[272,128]{1,0:T(8,128)(2,1)} %get-tuple-element.39), channel_id=1, source_target_pairs={{0,4},{1,5},{2,6},{3,7},{4,0},{5,1},{6,2},{7,3},{8,12},{9,13},{10,... | collective-permute-start | bytes 208904 | tf_op jit(solution)/shard_map/ppermute | solution.py:36
  7.2 9.2 %collective-permute-start.7 = (bf16[272,128]{1,0:T(8,128)(2,1)}, bf16[272,128]{1,0:T(8,128)(2,1)S(1)}, u32[]{:S(2)}, u32[]{:S(2)}) collective-permute-start(bf16[272,128]{1,0:T(8,128)(2,1)} %get-tuple-element.44), channel_id=1, source_target_pairs={{0,8},{1,9},{2,10},{3,11},{4,12},{5,13},{6,14},{7,15},{8,0},{9,1},... | collective-permute-start | bytes 208904 | tf_op jit(solution)/shard_map/ppermute | solution.py:36
  9.8 9.3 %collective-permute-start.8 = (bf16[272,128]{1,0:T(8,128)(2,1)}, bf16[272,128]{1,0:T(8,128)(2,1)S(1)}, u32[]{:S(2)}, u32[]{:S(2)}) collective-permute-start(bf16[272,128]{1,0:T(8,128)(2,1)} %get-tuple-element.45), channel_id=1, source_target_pairs={{0,12},{1,13},{2,14},{3,15},{4,8},{5,9},{6,10},{7,11},{8,4},{9,5},... | collective-permute-start | bytes 208904 | tf_op jit(solution)/shard_map/ppermute | solution.py:36
  12.1 11.0 %collective-permute-start.3 = (bf16[800,128]{1,0:T(8,128)(2,1)}, bf16[800,128]{1,0:T(8,128)(2,1)S(1)}, u32[]{:S(2)}, u32[]{:S(2)}) collective-permute-start(bf16[800,128]{1,0:T(8,128)(2,1)} %get-tuple-element.40), channel_id=1, source_target_pairs={{0,4},{1,5},{2,6},{3,7},{4,0},{5,1},{6,2},{7,3},{8,12},{9,13},{10,... | collective-permute-start | bytes 614408 | tf_op jit(solution)/shard_map/ppermute | solution.py:36
  12.8 18.5 %collective-permute-start.4 = (bf16[800,128]{1,0:T(8,128)(2,1)}, bf16[800,128]{1,0:T(8,128)(2,1)S(1)}, u32[]{:S(2)}, u32[]{:S(2)}) collective-permute-start(bf16[800,128]{1,0:T(8,128)(2,1)} %get-tuple-element.41), channel_id=1, source_target_pairs={{0,8},{1,9},{2,10},{3,11},{4,12},{5,13},{6,14},{7,15},{8,0},{9,1},... | collective-permute-start | bytes 614408 | tf_op jit(solution)/shard_map/ppermute | solution.py:36
  16.3 15.0 %collective-permute-start.5 = (bf16[800,128]{1,0:T(8,128)(2,1)}, bf16[800,128]{1,0:T(8,128)(2,1)S(1)}, u32[]{:S(2)}, u32[]{:S(2)}) collective-permute-start(bf16[800,128]{1,0:T(8,128)(2,1)} %get-tuple-element.42), channel_id=1, source_target_pairs={{0,12},{1,13},{2,14},{3,15},{4,8},{5,9},{6,10},{7,11},{8,4},{9,5},... | collective-permute-start | bytes 614408 | tf_op jit(solution)/shard_map/ppermute | solution.py:36
  19.3 12.0 %collective-permute-start.10 = (bf16[544,128]{1,0:T(8,128)(2,1)S(1)}, bf16[544,128]{1,0:T(8,128)(2,1)S(1)}, u32[]{:S(2)}, u32[]{:S(2)}) collective-permute-start(bf16[544,128]{1,0:T(8,128)(2,1)S(1)} %merge.3.refs_5_.refs_4_), channel_id=1, source_target_pairs={{0,2},{1,3},{2,0},{3,1},{4,6},{5,7},{6,4},{7,5},{8,10},{9,11},{10,... | collective-permute-start | bytes 417800 | tf_op jit(solution)/shard_map/ppermute | solution.py:36
  31.3 1.4 collective-permute-start.11
  31.3 8.8 %collective-permute-start.12 = (bf16[256,2048]{1,0:T(8,128)(2,1)S(1)}, bf16[256,2048]{1,0:T(8,128)(2,1)S(1)}, u32[]{:S(2)}, u32[]{:S(2)}) collective-permute-start(bf16[256,2048]{1,0:T(8,128)(2,1)S(1)} %copy-done.3), channel_id=1, source_target_pairs={{0,1},{1,0},{2,3},{3,2},{4,5},{5,4},{6,7},{7,6},{8,9},{9,8},{10,11... | collective-permute-start | bytes 3145736 | tf_op jit(solution)/shard_map/ppermute | solution.py:36
  32.7 7.5 %collective-permute-start.14 = (bf16[256,2048]{1,0:T(8,128)(2,1)S(1)}, bf16[256,2048]{1,0:T(8,128)(2,1)S(1)}, u32[]{:S(2)}, u32[]{:S(2)}) collective-permute-start(bf16[256,2048]{1,0:T(8,128)(2,1)S(1)} %collective-permute-done.13.refs_11_), channel_id=1, source_target_pairs={{0,1},{1,0},{2,3},{3,2},{4,5},{5,4},{6,7},{7,6},{8,9},{9,8},{10,11... | collective-permute-start | bytes 3145736 | tf_op jit(solution)/shard_map/ppermute | solution.py:36
  32.8 5.9 %collective-permute-start.2 = (bf16[544,128]{1,0:T(8,128)(2,1)S(1)}, bf16[544,128]{1,0:T(8,128)(2,1)S(1)}, u32[]{:S(2)}, u32[]{:S(2)}) collective-permute-start(bf16[544,128]{1,0:T(8,128)(2,1)S(1)} %merge.2.refs_2_.refs_1_.refs_0_), channel_id=1, source_target_pairs={{0,2},{1,3},{2,0},{3,1},{4,6},{5,7},{6,4},{7,5},{8,10},{9,11},{10,... | collective-permute-start | bytes 417800 | tf_op jit(solution)/shard_map/ppermute | solution.py:36
  33.4 5.4 %collective-permute-start.9 = (bf16[544,128]{1,0:T(8,128)(2,1)S(1)}, bf16[544,128]{1,0:T(8,128)(2,1)S(1)}, u32[]{:S(2)}, u32[]{:S(2)}) collective-permute-start(bf16[544,128]{1,0:T(8,128)(2,1)S(1)} %merge.3.refs_5_.refs_4_), channel_id=1, source_target_pairs={{0,1},{1,0},{2,3},{3,2},{4,5},{5,4},{6,7},{7,6},{8,9},{9,8},{10,11... | collective-permute-start | bytes 417800 | tf_op jit(solution)/shard_map/ppermute | solution.py:36
  33.4 5.4 %collective-permute-start.1 = (bf16[544,128]{1,0:T(8,128)(2,1)S(1)}, bf16[544,128]{1,0:T(8,128)(2,1)S(1)}, u32[]{:S(2)}, u32[]{:S(2)}) collective-permute-start(bf16[544,128]{1,0:T(8,128)(2,1)S(1)} %merge.2.refs_2_.refs_1_.refs_0_), channel_id=1, source_target_pairs={{0,1},{1,0},{2,3},{3,2},{4,5},{5,4},{6,7},{7,6},{8,9},{9,8},{10,11... | collective-permute-start | bytes 417800 | tf_op jit(solution)/shard_map/ppermute | solution.py:36
  38.8 1.4 collective-permute-start.6
  43.4 11.1 %collective-permute-start.15 = (bf16[80,2048]{1,0:T(8,128)(2,1)S(1)}, bf16[80,2048]{1,0:T(8,128)(2,1)S(1)}, u32[]{:S(2)}, u32[]{:S(2)}) collective-permute-start(bf16[80,2048]{1,0:T(8,128)(2,1)S(1)} %attention.4.refs_13_), channel_id=1, source_target_pairs={{0,4},{1,5},{2,6},{3,7},{4,0},{5,1},{6,2},{7,3},{8,12},{9,13},{10,... | collective-permute-start | bytes 983048 | tf_op jit(solution)/shard_map/ppermute | solution.py:36
  53.1 15.5 %collective-permute-start.16 = (bf16[80,2048]{1,0:T(8,128)(2,1)S(1)}, bf16[80,2048]{1,0:T(8,128)(2,1)S(1)}, u32[]{:S(2)}, u32[]{:S(2)}) collective-permute-start(bf16[80,2048]{1,0:T(8,128)(2,1)S(1)} %attention.6.refs_2_), channel_id=1, source_target_pairs={{0,4},{1,5},{2,6},{3,7},{4,0},{5,1},{6,2},{7,3},{8,12},{9,13},{10,... | collective-permute-start | bytes 983048 | tf_op jit(solution)/shard_map/ppermute | solution.py:36
  54.6 17.3 %collective-permute-start.17 = (bf16[80,2048]{1,0:T(8,128)(2,1)S(1)}, bf16[80,2048]{1,0:T(8,128)(2,1)S(1)}, u32[]{:S(2)}, u32[]{:S(2)}) collective-permute-start(bf16[80,2048]{1,0:T(8,128)(2,1)S(1)} %add.9.refs_13_), channel_id=1, source_target_pairs={{0,8},{1,9},{2,10},{3,11},{4,12},{5,13},{6,14},{7,15},{8,0},{9,1},... | collective-permute-start | bytes 983048 | tf_op jit(solution)/shard_map/ppermute | solution.py:36
  72.8 7.1 %collective-permute-start.19 = (bf16[80,2048]{1,0:T(8,128)(2,1)S(1)}, bf16[80,2048]{1,0:T(8,128)(2,1)S(1)}, u32[]{:S(2)}, u32[]{:S(2)}) collective-permute-start(bf16[80,2048]{1,0:T(8,128)(2,1)S(1)} %get-tuple-element.50.refs_0_), channel_id=1, source_target_pairs={{0,2},{1,3},{2,0},{3,1},{4,6},{5,7},{6,4},{7,5},{8,10},{9,11},{10,... | collective-permute-start | bytes 983048 | tf_op jit(solution)/shard_map/ppermute | solution.py:36
  73.3 13.2 %collective-permute-start.23 = (bf16[80,2048]{1,0:T(8,128)(2,1)S(1)}, bf16[80,2048]{1,0:T(8,128)(2,1)S(1)}, u32[]{:S(2)}, u32[]{:S(2)}) collective-permute-start(bf16[80,2048]{1,0:T(8,128)(2,1)S(1)} %get-tuple-element.50.refs_0_), channel_id=1, source_target_pairs={{0,4},{1,5},{2,6},{3,7},{4,0},{5,1},{6,2},{7,3},{8,12},{9,13},{10,... | collective-permute-start | bytes 983048 | tf_op jit(solution)/shard_map/ppermute | solution.py:36
  73.3 16.1 %collective-permute-start.27 = (bf16[80,2048]{1,0:T(8,128)(2,1)S(1)}, bf16[80,2048]{1,0:T(8,128)(2,1)S(1)}, u32[]{:S(2)}, u32[]{:S(2)}) collective-permute-start(bf16[80,2048]{1,0:T(8,128)(2,1)S(1)} %get-tuple-element.50.refs_0_), channel_id=1, source_target_pairs={{0,8},{1,9},{2,10},{3,11},{4,12},{5,13},{6,14},{7,15},{8,0},{9,1},... | collective-permute-start | bytes 983048 | tf_op jit(solution)/shard_map/ppermute | solution.py:36
  76.2 13.4 %collective-permute-start.18 = (bf16[80,2048]{1,0:T(8,128)(2,1)S(1)}, bf16[80,2048]{1,0:T(8,128)(2,1)S(1)}, u32[]{:S(2)}, u32[]{:S(2)}) collective-permute-start(bf16[80,2048]{1,0:T(8,128)(2,1)S(1)} %get-tuple-element.50.refs_0_), channel_id=1, source_target_pairs={{0,1},{1,0},{2,3},{3,2},{4,5},{5,4},{6,7},{7,6},{8,9},{9,8},{10,11... | collective-permute-start | bytes 983048 | tf_op jit(solution)/shard_map/ppermute | solution.py:36
  79.9 9.7 %collective-permute-start.20 = (bf16[80,2048]{1,0:T(8,128)(2,1)S(1)}, bf16[80,2048]{1,0:T(8,128)(2,1)S(1)}, u32[]{:S(2)}, u32[]{:S(2)}) collective-permute-start(bf16[80,2048]{1,0:T(8,128)(2,1)S(1)} %collective-permute-done.19.refs_2_), channel_id=1, source_target_pairs={{0,1},{1,0},{2,3},{3,2},{4,5},{5,4},{6,7},{7,6},{8,9},{9,8},{10,11... | collective-permute-start | bytes 983048 | tf_op jit(solution)/shard_map/ppermute | solution.py:36
  86.6 7.1 %collective-permute-start.25 = (bf16[80,2048]{1,0:T(8,128)(2,1)S(1)}, bf16[80,2048]{1,0:T(8,128)(2,1)S(1)}, u32[]{:S(2)}, u32[]{:S(2)}) collective-permute-start(bf16[80,2048]{1,0:T(8,128)(2,1)S(1)} %collective-permute-done.23.refs_0_), channel_id=1, source_target_pairs={{0,2},{1,3},{2,0},{3,1},{4,6},{5,7},{6,4},{7,5},{8,10},{9,11},{10,... | collective-permute-start | bytes 983048 | tf_op jit(solution)/shard_map/ppermute | solution.py:36
  89.4 7.1 %collective-permute-start.32 = (bf16[80,2048]{1,0:T(8,128)(2,1)S(1)}, bf16[80,2048]{1,0:T(8,128)(2,1)S(1)}, u32[]{:S(2)}, u32[]{:S(2)}) collective-permute-start(bf16[80,2048]{1,0:T(8,128)(2,1)S(1)} %collective-permute-done.27.refs_10_.refs_0_), channel_id=1, source_target_pairs={{0,4},{1,5},{2,6},{3,7},{4,0},{5,1},{6,2},{7,3},{8,12},{9,13},{10,... | collective-permute-start | bytes 983048 | tf_op jit(solution)/shard_map/ppermute | solution.py:36
  89.5 8.6 %collective-permute-start.24 = (bf16[80,2048]{1,0:T(8,128)(2,1)S(1)}, bf16[80,2048]{1,0:T(8,128)(2,1)S(1)}, u32[]{:S(2)}, u32[]{:S(2)}) collective-permute-start(bf16[80,2048]{1,0:T(8,128)(2,1)S(1)} %collective-permute-done.23.refs_0_), channel_id=1, source_target_pairs={{0,1},{1,0},{2,3},{3,2},{4,5},{5,4},{6,7},{7,6},{8,9},{9,8},{10,11... | collective-permute-start | bytes 983048 | tf_op jit(solution)/shard_map/ppermute | solution.py:36
  93.6 4.5 %collective-permute-start.26 = (bf16[80,2048]{1,0:T(8,128)(2,1)S(1)}, bf16[80,2048]{1,0:T(8,128)(2,1)S(1)}, u32[]{:S(2)}, u32[]{:S(2)}) collective-permute-start(bf16[80,2048]{1,0:T(8,128)(2,1)S(1)} %collective-permute-done.25.refs_2_), channel_id=1, source_target_pairs={{0,1},{1,0},{2,3},{3,2},{4,5},{5,4},{6,7},{7,6},{8,9},{9,8},{10,11... | collective-permute-start | bytes 983048 | tf_op jit(solution)/shard_map/ppermute | solution.py:36
  96.5 7.3 %collective-permute-start.34 = (bf16[80,2048]{1,0:T(8,128)(2,1)S(1)}, bf16[80,2048]{1,0:T(8,128)(2,1)S(1)}, u32[]{:S(2)}, u32[]{:S(2)}) collective-permute-start(bf16[80,2048]{1,0:T(8,128)(2,1)S(1)} %collective-permute-done.32.refs_0_), channel_id=1, source_target_pairs={{0,2},{1,3},{2,0},{3,1},{4,6},{5,7},{6,4},{7,5},{8,10},{9,11},{10,... | collective-permute-start | bytes 983048 | tf_op jit(solution)/shard_map/ppermute | solution.py:36
  98.1 7.6 %collective-permute-start.33 = (bf16[80,2048]{1,0:T(8,128)(2,1)S(1)}, bf16[80,2048]{1,0:T(8,128)(2,1)S(1)}, u32[]{:S(2)}, u32[]{:S(2)}) collective-permute-start(bf16[80,2048]{1,0:T(8,128)(2,1)S(1)} %collective-permute-done.32.refs_0_), channel_id=1, source_target_pairs={{0,1},{1,0},{2,3},{3,2},{4,5},{5,4},{6,7},{7,6},{8,9},{9,8},{10,11... | collective-permute-start | bytes 983048 | tf_op jit(solution)/shard_map/ppermute | solution.py:36
  103.8 2.0 %collective-permute-start.35 = (bf16[80,2048]{1,0:T(8,128)(2,1)S(1)}, bf16[80,2048]{1,0:T(8,128)(2,1)S(1)}, u32[]{:S(2)}, u32[]{:S(2)}) collective-permute-start(bf16[80,2048]{1,0:T(8,128)(2,1)S(1)} %collective-permute-done.34.refs_2_), channel_id=1, source_target_pairs={{0,1},{1,0},{2,3},{3,2},{4,5},{5,4},{6,7},{7,6},{8,9},{9,8},{10,11... | collective-permute-start | bytes 983048 | tf_op jit(solution)/shard_map/ppermute | solution.py:36
  103.8 10.1 %collective-permute-start.31 = (bf16[80,2048]{1,0:T(8,128)(2,1)S(1)}, bf16[80,2048]{1,0:T(8,128)(2,1)S(1)}, u32[]{:S(2)}, u32[]{:S(2)}) collective-permute-start(bf16[80,2048]{1,0:T(8,128)(2,1)S(1)} %collective-permute-done.27.refs_10_.refs_0_), channel_id=1, source_target_pairs={{0,2},{1,3},{2,0},{3,1},{4,6},{5,7},{6,4},{7,5},{8,10},{9,11},{10,... | collective-permute-start | bytes 983048 | tf_op jit(solution)/shard_map/ppermute | solution.py:36
  105.5 10.8 %collective-permute-start.30 = (bf16[80,2048]{1,0:T(8,128)(2,1)S(1)}, bf16[80,2048]{1,0:T(8,128)(2,1)S(1)}, u32[]{:S(2)}, u32[]{:S(2)}) collective-permute-start(bf16[80,2048]{1,0:T(8,128)(2,1)S(1)} %collective-permute-done.27.refs_10_.refs_0_), channel_id=1, source_target_pairs={{0,1},{1,0},{2,3},{3,2},{4,5},{5,4},{6,7},{7,6},{8,9},{9,8},{10,11... | collective-permute-start | bytes 983048 | tf_op jit(solution)/shard_map/ppermute | solution.py:36
  109.4 5.0 %collective-permute-start.37 = (bf16[80,2048]{1,0:T(8,128)(2,1)S(1)}, bf16[80,2048]{1,0:T(8,128)(2,1)S(1)}, u32[]{:S(2)}, u32[]{:S(2)}) collective-permute-start(bf16[80,2048]{1,0:T(8,128)(2,1)S(1)} %get-tuple-element.66), channel_id=1, source_target_pairs={{0,1},{1,0},{2,3},{3,2},{4,5},{5,4},{6,7},{7,6},{8,9},{9,8},{10,11... | collective-permute-start | bytes 983048 | tf_op jit(solution)/shard_map/ppermute | solution.py:36
  113.9 2.4 %collective-permute-start.36 = (bf16[80,2048]{1,0:T(8,128)(2,1)S(1)}, bf16[80,2048]{1,0:T(8,128)(2,1)S(1)}, u32[]{:S(2)}, u32[]{:S(2)}) collective-permute-start(bf16[80,2048]{1,0:T(8,128)(2,1)S(1)} %collective-permute-done.31.refs_2_), channel_id=1, source_target_pairs={{0,1},{1,0},{2,3},{3,2},{4,5},{5,4},{6,7},{7,6},{8,9},{9,8},{10,11... | collective-permute-start | bytes 983048 | tf_op jit(solution)/shard_map/ppermute | solution.py:36
  113.9 6.9 %collective-permute-start.40 = (bf16[80,2048]{1,0:T(8,128)(2,1)S(1)}, bf16[80,2048]{1,0:T(8,128)(2,1)S(1)}, u32[]{:S(2)}, u32[]{:S(2)}) collective-permute-start(bf16[80,2048]{1,0:T(8,128)(2,1)S(1)} %get-tuple-element.71), channel_id=1, source_target_pairs={{0,1},{1,0},{2,3},{3,2},{4,5},{5,4},{6,7},{7,6},{8,9},{9,8},{10,11... | collective-permute-start | bytes 983048 | tf_op jit(solution)/shard_map/ppermute | solution.py:36
  114.5 9.7 %collective-permute-start.41 = (bf16[80,2048]{1,0:T(8,128)(2,1)S(1)}, bf16[80,2048]{1,0:T(8,128)(2,1)S(1)}, u32[]{:S(2)}, u32[]{:S(2)}) collective-permute-start(bf16[80,2048]{1,0:T(8,128)(2,1)S(1)} %add.10.refs_9_), channel_id=1, source_target_pairs={{0,2},{1,3},{2,0},{3,1},{4,6},{5,7},{6,4},{7,5},{8,10},{9,11},{10,... | collective-permute-start | bytes 983048 | tf_op jit(solution)/shard_map/ppermute | solution.py:36
  120.2 4.1 %collective-permute-start.39 = (bf16[80,2048]{1,0:T(8,128)(2,1)S(1)}, bf16[80,2048]{1,0:T(8,128)(2,1)S(1)}, u32[]{:S(2)}, u32[]{:S(2)}) collective-permute-start(bf16[80,2048]{1,0:T(8,128)(2,1)S(1)} %get-tuple-element.70), channel_id=1, source_target_pairs={{0,1},{1,0},{2,3},{3,2},{4,5},{5,4},{6,7},{7,6},{8,9},{9,8},{10,11... | collective-permute-start | bytes 983048 | tf_op jit(solution)/shard_map/ppermute | solution.py:36
  120.3 8.1 %collective-permute-start.38 = (bf16[80,2048]{1,0:T(8,128)(2,1)S(1)}, bf16[80,2048]{1,0:T(8,128)(2,1)S(1)}, u32[]{:S(2)}, u32[]{:S(2)}) collective-permute-start(bf16[80,2048]{1,0:T(8,128)(2,1)S(1)} %get-tuple-element.68), channel_id=1, source_target_pairs={{0,1},{1,0},{2,3},{3,2},{4,5},{5,4},{6,7},{7,6},{8,9},{9,8},{10,11... | collective-permute-start | bytes 983048 | tf_op jit(solution)/shard_map/ppermute | solution.py:36
  124.4 8.8 %collective-permute-start.42 = (bf16[80,2048]{1,0:T(8,128)(2,1)S(1)}, bf16[80,2048]{1,0:T(8,128)(2,1)S(1)}, u32[]{:S(2)}, u32[]{:S(2)}) collective-permute-start(bf16[80,2048]{1,0:T(8,128)(2,1)S(1)} %add.12.refs_4_), channel_id=1, source_target_pairs={{0,2},{1,3},{2,0},{3,1},{4,6},{5,7},{6,4},{7,5},{8,10},{9,11},{10,... | collective-permute-start | bytes 983048 | tf_op jit(solution)/shard_map/ppermute | solution.py:36
  126.2 8.5 %collective-permute-start.43 = (bf16[80,2048]{1,0:T(8,128)(2,1)S(1)}, bf16[80,2048]{1,0:T(8,128)(2,1)S(1)}, u32[]{:S(2)}, u32[]{:S(2)}) collective-permute-start(bf16[80,2048]{1,0:T(8,128)(2,1)S(1)} %add.11.refs_2_), channel_id=1, source_target_pairs={{0,4},{1,5},{2,6},{3,7},{4,0},{5,1},{6,2},{7,3},{8,12},{9,13},{10,... | collective-permute-start | bytes 983048 | tf_op jit(solution)/shard_map/ppermute | solution.py:36
  127.8 7.0 %collective-permute-start.29 = (bf16[80,2048]{1,0:T(8,128)(2,1)S(1)}, bf16[80,2048]{1,0:T(8,128)(2,1)S(1)}, u32[]{:S(2)}, u32[]{:S(2)}) collective-permute-start(bf16[80,2048]{1,0:T(8,128)(2,1)S(1)} %get-tuple-element.61), channel_id=1, source_target_pairs={{0,1},{1,0},{2,3},{3,2},{4,5},{5,4},{6,7},{7,6},{8,9},{9,8},{10,11... | collective-permute-start | bytes 983048 | tf_op jit(solution)/shard_map/ppermute | solution.py:36
  127.8 11.4 %collective-permute-start.28 = (bf16[80,2048]{1,0:T(8,128)(2,1)S(1)}, bf16[80,2048]{1,0:T(8,128)(2,1)S(1)}, u32[]{:S(2)}, u32[]{:S(2)}) collective-permute-start(bf16[80,2048]{1,0:T(8,128)(2,1)S(1)} %get-tuple-element.59), channel_id=1, source_target_pairs={{0,1},{1,0},{2,3},{3,2},{4,5},{5,4},{6,7},{7,6},{8,9},{9,8},{10,11... | collective-permute-start | bytes 983048 | tf_op jit(solution)/shard_map/ppermute | solution.py:36
  135.0 7.6 %collective-permute-start.44 = (bf16[80,2048]{1,0:T(8,128)(2,1)S(1)}, bf16[80,2048]{1,0:T(8,128)(2,1)S(1)}, u32[]{:S(2)}, u32[]{:S(2)}) collective-permute-start(bf16[80,2048]{1,0:T(8,128)(2,1)S(1)} %add.14.refs_3_), channel_id=1, source_target_pairs={{0,2},{1,3},{2,0},{3,1},{4,6},{5,7},{6,4},{7,5},{8,10},{9,11},{10,... | collective-permute-start | bytes 983048 | tf_op jit(solution)/shard_map/ppermute | solution.py:36
  135.4 9.0 %collective-permute-start.22 = (bf16[80,2048]{1,0:T(8,128)(2,1)S(1)}, bf16[80,2048]{1,0:T(8,128)(2,1)S(1)}, u32[]{:S(2)}, u32[]{:S(2)}) collective-permute-start(bf16[80,2048]{1,0:T(8,128)(2,1)S(1)} %get-tuple-element.56), channel_id=1, source_target_pairs={{0,1},{1,0},{2,3},{3,2},{4,5},{5,4},{6,7},{7,6},{8,9},{9,8},{10,11... | collective-permute-start | bytes 983048 | tf_op jit(solution)/shard_map/ppermute | solution.py:36
  135.4 9.7 %collective-permute-start.21 = (bf16[80,2048]{1,0:T(8,128)(2,1)S(1)}, bf16[80,2048]{1,0:T(8,128)(2,1)S(1)}, u32[]{:S(2)}, u32[]{:S(2)}) collective-permute-start(bf16[80,2048]{1,0:T(8,128)(2,1)S(1)} %get-tuple-element.54), channel_id=1, source_target_pairs={{0,1},{1,0},{2,3},{3,2},{4,5},{5,4},{6,7},{7,6},{8,9},{9,8},{10,11... | collective-permute-start | bytes 983048 | tf_op jit(solution)/shard_map/ppermute | solution.py:36
  135.9 18.4 %collective-permute-start.47 = (bf16[80,2048]{1,0:T(8,128)(2,1)S(1)}, bf16[80,2048]{1,0:T(8,128)(2,1)S(1)}, u32[]{:S(2)}, u32[]{:S(2)}) collective-permute-start(bf16[80,2048]{1,0:T(8,128)(2,1)S(1)} %add.13.refs_2_), channel_id=1, source_target_pairs={{0,8},{1,9},{2,10},{3,11},{4,12},{5,13},{6,14},{7,15},{8,0},{9,1},... | collective-permute-start | bytes 983048 | tf_op jit(solution)/shard_map/ppermute | solution.py:36
  142.7 12.9 %collective-permute-start.46 = (bf16[80,2048]{1,0:T(8,128)(2,1)S(1)}, bf16[80,2048]{1,0:T(8,128)(2,1)S(1)}, u32[]{:S(2)}, u32[]{:S(2)}) collective-permute-start(bf16[80,2048]{1,0:T(8,128)(2,1)S(1)} %add.15.refs_2_), channel_id=1, source_target_pairs={{0,4},{1,5},{2,6},{3,7},{4,0},{5,1},{6,2},{7,3},{8,12},{9,13},{10,... | collective-permute-start | bytes 983048 | tf_op jit(solution)/shard_map/ppermute | solution.py:36
  144.5 11.1 %collective-permute-start.45 = (bf16[80,2048]{1,0:T(8,128)(2,1)S(1)}, bf16[80,2048]{1,0:T(8,128)(2,1)S(1)}, u32[]{:S(2)}, u32[]{:S(2)}) collective-permute-start(bf16[80,2048]{1,0:T(8,128)(2,1)S(1)} %add.16), channel_id=1, source_target_pairs={{0,2},{1,3},{2,0},{3,1},{4,6},{5,7},{6,4},{7,5},{8,10},{9,11},{10,... | collective-permute-start | bytes 983048 | tf_op jit(solution)/shard_map/ppermute | solution.py:36
  (11 other events, 212.8 us)

commit v5 on v4

--- a/solution.py
+++ b/solution.py
@@ -24,8 +24,8 @@
     "mtok": ["pq"],
     "cgate": ["q1", "q2", "q3"],
     "pgate": ["cb"],
-    "att": [3, 2, 1, "add", 0, "sel"],
-    "atok": ["q1", "q2"],
+    "att": [3, 1, 2, "add", 0, "sel"],
+    "atok": ["q2"],
 }
 NT = (((1,), (1,)), ((), ()))
 ANY = pl.BlockSpec(memory_space=pl.ANY)
@@ -202,7 +202,7 @@
     factor = HEAD_SIZE ** (-0.5) * math.log2(math.e)
     own_key = qf[group * rows : (group + 1) * rows, :].astype(F32)
     own_value = qf[(group + 1) * rows :, :].astype(F32)
-    step = max(1, group // 2)
+    step = max(1, group // 4)
     for h0 in range(0, group, step):
         query = qf[h0 * rows : (h0 + step) * rows, :]
         own = jnp.sum(

time: 157 us -> 157 us (level)
  transfers between devices with their start and end apart: 48 -> 48, of which waited for: 21 -> 21; matrix products, arithmetic and copies ran while one was open for 0% -> 0% of each run, Pallas kernels for 21% -> 22%
where the time goes in v5:
time: 157 us; the launch traced here: 156 us
  waiting for transfers between devices  70.5 us (45%)
  starting transfers between devices  44.8 us (29%)
  Pallas kernels  38.9 us (25%)
    ppermute x48, waiting for transfers between devices, swap(): return lax.ppermute(array, 'ctx', [(i, i ^ offset) for i in range(n)])  70.5 us
    ppermute x48, starting transfers between devices, swap(): return lax.ppermute(array, 'ctx', [(i, i ^ offset) for i in range(n)])  44.8 us
    pallas_call x23, Pallas kernels, call(): pl.pallas_call(body, out_shape=outs, in_specs=list(specs) + [ANY] * len(t...  38.9 us
  transfers between devices with their start and end apart: 48, of which 21 were waited for; matrix products, arithmetic and copies ran while one was open for 0% of the time, Pallas kernels for 22%

profile of v5, /device:TPU:0, one launch (start us, length us, event | category | flops | bytes accessed | tf_op | source)
XLA Modules:
  0.0 156.2 jit_solution(7915493355555037230)
XLA Ops:
  0.6 3.0 %collective-permute-start.13 = (bf16[256,2048]{1,0:T(8,128)(2,1)}, bf16[256,2048]{1,0:T(8,128)(2,1)S(1)}, u32[]{:S(2)}, u32[]{:S(2)}) collective-permute-start(bf16[256,2048]{1,0:T(8,128)(2,1)} %refs_9_.7), channel_id=1, source_target_pairs={{0,2},{1,3},{2,0},{3,1},{4,6},{5,7},{6,4},{7,5},{8,10},{9,11},{10,... | collective-permute-start | bytes 3145736 | tf_op jit(solution)/shard_map/ppermute | solution.py:36
  3.7 1.9 %pack_cache.1 = (bf16[272,128]{1,0:T(8,128)(2,1)}, bf16[272,128]{1,0:T(8,128)(2,1)}, bf16[272,128]{1,0:T(8,128)(2,1)}, bf16[272,128]{1,0:T(8,128)(2,1)}) custom-call(bf16[2,128,512]{2,1,0:T(8,128)(2,1)} %refs_0_.3, s32[8,80]{1,0:T(8,128)} %bitcast.9, f32[8,80]{1,0:T(8,128)} %bitcast.10, s32[1,32]{1,0:T(1,128)} %bitcast.11), custom_call_target="tpu_custom_call" | custom-call | flops 1 | bytes 1 | tf_op jit(solution)/shard_map/pack_cache/pallas_call | solution.py:72
  5.5 1.6 %collective-permute-start = (bf16[272,128]{1,0:T(8,128)(2,1)}, bf16[272,128]{1,0:T(8,128)(2,1)S(1)}, u32[]{:S(2)}, u32[]{:S(2)}) collective-permute-start(bf16[272,128]{1,0:T(8,128)(2,1)} %get-tuple-element.39), channel_id=1, source_target_pairs={{0,4},{1,5},{2,6},{3,7},{4,0},{5,1},{6,2},{7,3},{8,12},{9,13},{10,... | collective-permute-start | bytes 208904 | tf_op jit(solution)/shard_map/ppermute | solution.py:36
  7.2 2.6 %collective-permute-start.7 = (bf16[272,128]{1,0:T(8,128)(2,1)}, bf16[272,128]{1,0:T(8,128)(2,1)S(1)}, u32[]{:S(2)}, u32[]{:S(2)}) collective-permute-start(bf16[272,128]{1,0:T(8,128)(2,1)} %get-tuple-element.44), channel_id=1, source_target_pairs={{0,8},{1,9},{2,10},{3,11},{4,12},{5,13},{6,14},{7,15},{8,0},{9,1},... | collective-permute-start | bytes 208904 | tf_op jit(solution)/shard_map/ppermute | solution.py:36
  10.0 2.1 %pack_queries.1 = (bf16[800,128]{1,0:T(8,128)(2,1)}, bf16[800,128]{1,0:T(8,128)(2,1)}, bf16[800,128]{1,0:T(8,128)(2,1)}, bf16[800,128]{1,0:T(8,128)(2,1)}) custom-call(bf16[80,4096]{1,0:T(8,128)(2,1)} %refs_0_.4, bf16[2,80,512]{2,1,0:T(8,128)(2,1)} %refs_1_.1, bf16[272,128]{1,0:T(8,128)(2,1)} %get-tuple-element.37.refs_2_.refs_0_), custom_call_target="tpu_custom_call" | custom-call | flops 6000000000 | bytes 1 | tf_op jit(solution)/shard_map/pack_queries/pallas_call | solution.py:72
  12.8 3.5 %collective-permute-start.4 = (bf16[800,128]{1,0:T(8,128)(2,1)}, bf16[800,128]{1,0:T(8,128)(2,1)S(1)}, u32[]{:S(2)}, u32[]{:S(2)}) collective-permute-start(bf16[800,128]{1,0:T(8,128)(2,1)} %get-tuple-element.41), channel_id=1, source_target_pairs={{0,8},{1,9},{2,10},{3,11},{4,12},{5,13},{6,14},{7,15},{8,0},{9,1},... | collective-permute-start | bytes 614408 | tf_op jit(solution)/shard_map/ppermute | solution.py:36
  16.3 1.6 %collective-permute-start.5 = (bf16[800,128]{1,0:T(8,128)(2,1)}, bf16[800,128]{1,0:T(8,128)(2,1)S(1)}, u32[]{:S(2)}, u32[]{:S(2)}) collective-permute-start(bf16[800,128]{1,0:T(8,128)(2,1)} %get-tuple-element.42), channel_id=1, source_target_pairs={{0,12},{1,13},{2,14},{3,15},{4,8},{5,9},{6,10},{7,11},{8,4},{9,5},... | collective-permute-start | bytes 614408 | tf_op jit(solution)/shard_map/ppermute | solution.py:36
  17.9 0.9 copy-done
  19.9 3.1 %collective-permute-done.3.refs_0_ = bf16[800,128]{1,0:T(8,128)(2,1)S(1)} collective-permute-done((bf16[800,128]{1,0:T(8,128)(2,1)}, bf16[800,128]{1,0:T(8,128)(2,1)S(1)}, u32[]{:S(2)}, u32[]{:S(2)}) %collective-permute-start.3) | collective-permute-done | bytes 204832 | tf_op jit(solution)/shard_map/ppermute | solution.py:36
  23.1 8.3 %collective-permute-done.4.refs_13_.refs_0_ = bf16[800,128]{1,0:T(8,128)(2,1)S(1)} collective-permute-done((bf16[800,128]{1,0:T(8,128)(2,1)}, bf16[800,128]{1,0:T(8,128)(2,1)S(1)}, u32[]{:S(2)}, u32[]{:S(2)}) %collective-permute-start.4) | collective-permute-done | bytes 204832 | tf_op jit(solution)/shard_map/ppermute | solution.py:36
  33.9 4.9 %collective-permute-done.2.refs_3_.refs_2_ = bf16[544,128]{1,0:T(8,128)(2,1)S(1)} collective-permute-done((bf16[544,128]{1,0:T(8,128)(2,1)S(1)}, bf16[544,128]{1,0:T(8,128)(2,1)S(1)}, u32[]{:S(2)}, u32[]{:S(2)}) %collective-permute-start.2) | collective-permute-done | bytes 139296 | tf_op jit(solution)/shard_map/ppermute | solution.py:36
  38.8 1.3 collective-permute-done.6.refs_4_.refs_3_
  40.2 3.4 %attention.4.refs_13_ = bf16[80,2048]{1,0:T(8,128)(2,1)S(1)} custom-call(bf16[800,128]{1,0:T(8,128)(2,1)S(1)} %collective-permute-done.5.refs_0_, bf16[544,128]{1,0:T(8,128)(2,1)S(1)} %merge.2.refs_2_.refs_1_.refs_0_, bf16[544,128]{1,0:T(8,128)(2,1)S(1)} %collective-permute-done.1.refs_2_.refs_1_, ...), custom_call_target="tpu_custom_call" | custom-call | flops 3000000000 | bytes 1 | tf_op jit(solution)/shard_map/attention/pallas_call | solution.py:72
  43.5 3.1 %collective-permute-start.15 = (bf16[80,2048]{1,0:T(8,128)(2,1)S(1)}, bf16[80,2048]{1,0:T(8,128)(2,1)S(1)}, u32[]{:S(2)}, u32[]{:S(2)}) collective-permute-start(bf16[80,2048]{1,0:T(8,128)(2,1)S(1)} %attention.4.refs_13_), channel_id=1, source_target_pairs={{0,4},{1,5},{2,6},{3,7},{4,0},{5,1},{6,2},{7,3},{8,12},{9,13},{10,... | collective-permute-start | bytes 983048 | tf_op jit(solution)/shard_map/ppermute | solution.py:36
  46.6 3.4 %attention.5.refs_13_ = bf16[80,2048]{1,0:T(8,128)(2,1)S(1)} custom-call(bf16[800,128]{1,0:T(8,128)(2,1)S(1)} %collective-permute-done.3.refs_0_, bf16[544,128]{1,0:T(8,128)(2,1)S(1)} %merge.2.refs_2_.refs_1_.refs_0_, bf16[544,128]{1,0:T(8,128)(2,1)S(1)} %collective-permute-done.1.refs_2_.refs_1_, ...), custom_call_target="tpu_custom_call" | custom-call | flops 3000000000 | bytes 1 | tf_op jit(solution)/shard_map/attention/pallas_call | solution.py:72
  50.1 3.4 %attention.6.refs_0_.refs_2_ = f32[80,2048]{1,0:T(8,128)S(1)} custom-call(bf16[800,128]{1,0:T(8,128)(2,1)S(1)} %collective-permute-done.4.refs_13_.refs_0_, bf16[544,128]{1,0:T(8,128)(2,1)S(1)} %merge.2.refs_2_.refs_1_.refs_0_, bf16[544,128]{1,0:T(8,128)(2,1)S(1)} %collective-permute-done.1.refs_2_.refs_1_, ...), custom_call_target="tpu_custom_call" | custom-call | flops 3000000000 | bytes 1 | tf_op jit(solution)/shard_map/attention/pallas_call | solution.py:72
  53.5 1.6 %collective-permute-done.15.refs_1_ = bf16[80,2048]{1,0:T(8,128)(2,1)S(1)} collective-permute-done((bf16[80,2048]{1,0:T(8,128)(2,1)S(1)}, bf16[80,2048]{1,0:T(8,128)(2,1)S(1)}, u32[]{:S(2)}, u32[]{:S(2)}) %collective-permute-start.15) | collective-permute-done | bytes 327712 | tf_op jit(solution)/shard_map/ppermute | solution.py:36
  55.2 3.0 %collective-permute-start.17 = (bf16[80,2048]{1,0:T(8,128)(2,1)S(1)}, bf16[80,2048]{1,0:T(8,128)(2,1)S(1)}, u32[]{:S(2)}, u32[]{:S(2)}) collective-permute-start(bf16[80,2048]{1,0:T(8,128)(2,1)S(1)} %add.9.refs_13_), channel_id=1, source_target_pairs={{0,8},{1,9},{2,10},{3,11},{4,12},{5,13},{6,14},{7,15},{8,0},{9,1},... | collective-permute-start | bytes 983048 | tf_op jit(solution)/shard_map/ppermute | solution.py:36
  58.3 3.5 %attention.7.refs_8_.refs_2_ = f32[80,2048]{1,0:T(8,128)S(1)} custom-call(bf16[800,128]{1,0:T(8,128)(2,1)S(1)} %copy-done.1, bf16[544,128]{1,0:T(8,128)(2,1)S(1)} %merge.2.refs_2_.refs_1_.refs_0_, bf16[544,128]{1,0:T(8,128)(2,1)S(1)} %collective-permute-done.1.refs_2_.refs_1_, bf16[544,128]{1,0:T(8,128)(2,1)S(1)} %collective-permute-done.2.refs_3_.refs_2_, ...), custom_call_target="tpu_custom_call" | custom-call | flops 3000000000 | bytes 1 | tf_op jit(solution)/shard_map/attention/pallas_call | solution.py:72
  61.8 3.2 %select.1 = (bf16[4,256,320]{2,1,0:T(8,128)(2,1)S(1)}, bf16[4,320,256]{2,1,0:T(8,128)(2,1)S(1)}, f32[4,256,128]{2,1,0:T(8,128)S(1)}) custom-call(bf16[544,128]{1,0:T(8,128)(2,1)S(1)} %merge.2.refs_2_.refs_1_.refs_0_, bf16[544,128]{1,0:T(8,128)(2,1)S(1)} %collective-permute-done.1.refs_2_.refs_1_, ...), custom_call_target="tpu_custom_call" | custom-call | flops 1 | bytes 1 | tf_op jit(solution)/shard_map/select/pallas_call | solution.py:72
  65.1 2.5 %collective-permute-done.16.refs_3_ = bf16[80,2048]{1,0:T(8,128)(2,1)S(1)} collective-permute-done((bf16[80,2048]{1,0:T(8,128)(2,1)S(1)}, bf16[80,2048]{1,0:T(8,128)(2,1)S(1)}, u32[]{:S(2)}, u32[]{:S(2)}) %collective-permute-start.16) | collective-permute-done | bytes 327712 | tf_op jit(solution)/shard_map/ppermute | solution.py:36
  67.6 4.5 %collective-permute-done.17.refs_4_ = bf16[80,2048]{1,0:T(8,128)(2,1)S(1)} collective-permute-done((bf16[80,2048]{1,0:T(8,128)(2,1)S(1)}, bf16[80,2048]{1,0:T(8,128)(2,1)S(1)}, u32[]{:S(2)}, u32[]{:S(2)}) %collective-permute-start.17) | collective-permute-done | bytes 327712 | tf_op jit(solution)/shard_map/ppermute | solution.py:36
  73.5 2.8 %collective-permute-start.27 = (bf16[80,2048]{1,0:T(8,128)(2,1)S(1)}, bf16[80,2048]{1,0:T(8,128)(2,1)S(1)}, u32[]{:S(2)}, u32[]{:S(2)}) collective-permute-start(bf16[80,2048]{1,0:T(8,128)(2,1)S(1)} %get-tuple-element.50.refs_0_), channel_id=1, source_target_pairs={{0,8},{1,9},{2,10},{3,11},{4,12},{5,13},{6,14},{7,15},{8,0},{9,1},... | collective-permute-start | bytes 983048 | tf_op jit(solution)/shard_map/ppermute | solution.py:36
  76.3 3.7 %collective-permute-done.19.refs_2_ = bf16[80,2048]{1,0:T(8,128)(2,1)S(1)} collective-permute-done((bf16[80,2048]{1,0:T(8,128)(2,1)S(1)}, bf16[80,2048]{1,0:T(8,128)(2,1)S(1)}, u32[]{:S(2)}, u32[]{:S(2)}) %collective-permute-start.19) | collective-permute-done | bytes 327712 | tf_op jit(solution)/shard_map/ppermute | solution.py:36
  80.0 6.2 %collective-permute-done.23.refs_0_ = bf16[80,2048]{1,0:T(8,128)(2,1)S(1)} collective-permute-done((bf16[80,2048]{1,0:T(8,128)(2,1)S(1)}, bf16[80,2048]{1,0:T(8,128)(2,1)S(1)}, u32[]{:S(2)}, u32[]{:S(2)}) %collective-permute-start.23) | collective-permute-done | bytes 327712 | tf_op jit(solution)/shard_map/ppermute | solution.py:36
  86.2 1.7 %collective-permute-start.25 = (bf16[80,2048]{1,0:T(8,128)(2,1)S(1)}, bf16[80,2048]{1,0:T(8,128)(2,1)S(1)}, u32[]{:S(2)}, u32[]{:S(2)}) collective-permute-start(bf16[80,2048]{1,0:T(8,128)(2,1)S(1)} %collective-permute-done.23.refs_0_), channel_id=1, source_target_pairs={{0,2},{1,3},{2,0},{3,1},{4,6},{5,7},{6,4},{7,5},{8,10},{9,11},{10,... | collective-permute-start | bytes 983048 | tf_op jit(solution)/shard_map/ppermute | solution.py:36
  87.9 1.4 collective-permute-done.27.refs_10_.refs_0_
  89.4 3.7 %experts.4 = (bf16[80,2048]{1,0:T(8,128)(2,1)S(1)}, bf16[80,2048]{1,0:T(8,128)(2,1)S(1)}, bf16[80,2048]{1,0:T(8,128)(2,1)S(1)}, bf16[80,2048]{1,0:T(8,128)(2,1)S(1)}) custom-call(bf16[80,2048]{1,0:T(8,128)(2,1)S(1)} %get-tuple-element.50.refs_0_, bf16[80,2048]{1,0:T(8,128)(2,1)S(1)} %collective-permute-done.18.refs_1_, ...), custom_call_target="tpu_custom_call" | custom-call | flops 1 | bytes 1 | tf_op jit(solution)/shard_map/experts/pallas_call | solution.py:72
  93.7 2.7 %collective-permute-done.32.refs_0_ = bf16[80,2048]{1,0:T(8,128)(2,1)S(1)} collective-permute-done((bf16[80,2048]{1,0:T(8,128)(2,1)S(1)}, bf16[80,2048]{1,0:T(8,128)(2,1)S(1)}, u32[]{:S(2)}, u32[]{:S(2)}) %collective-permute-start.32) | collective-permute-done | bytes 327712 | tf_op jit(solution)/shard_map/ppermute | solution.py:36
  96.4 1.5 collective-permute-start.34
  97.9 3.7 %experts.5 = (bf16[80,2048]{1,0:T(8,128)(2,1)S(1)}, bf16[80,2048]{1,0:T(8,128)(2,1)S(1)}, bf16[80,2048]{1,0:T(8,128)(2,1)S(1)}, bf16[80,2048]{1,0:T(8,128)(2,1)S(1)}) custom-call(bf16[80,2048]{1,0:T(8,128)(2,1)S(1)} %collective-permute-done.23.refs_0_, bf16[80,2048]{1,0:T(8,128)(2,1)S(1)} %collective-permute-done.24.refs_1_, ...), custom_call_target="tpu_custom_call" | custom-call | flops 1 | bytes 1 | tf_op jit(solution)/shard_map/experts/pallas_call | solution.py:72
  101.6 1.9 %collective-permute-done.34.refs_2_ = bf16[80,2048]{1,0:T(8,128)(2,1)S(1)} collective-permute-done((bf16[80,2048]{1,0:T(8,128)(2,1)S(1)}, bf16[80,2048]{1,0:T(8,128)(2,1)S(1)}, u32[]{:S(2)}, u32[]{:S(2)}) %collective-permute-start.34) | collective-permute-done | bytes 327712 | tf_op jit(solution)/shard_map/ppermute | solution.py:36
  103.5 1.7 %collective-permute-start.31 = (bf16[80,2048]{1,0:T(8,128)(2,1)S(1)}, bf16[80,2048]{1,0:T(8,128)(2,1)S(1)}, u32[]{:S(2)}, u32[]{:S(2)}) collective-permute-start(bf16[80,2048]{1,0:T(8,128)(2,1)S(1)} %collective-permute-done.27.refs_10_.refs_0_), channel_id=1, source_target_pairs={{0,2},{1,3},{2,0},{3,1},{4,6},{5,7},{6,4},{7,5},{8,10},{9,11},{10,... | collective-permute-start | bytes 983048 | tf_op jit(solution)/shard_map/ppermute | solution.py:36
  105.4 3.7 %experts.6 = (bf16[80,2048]{1,0:T(8,128)(2,1)S(1)}, bf16[80,2048]{1,0:T(8,128)(2,1)S(1)}, bf16[80,2048]{1,0:T(8,128)(2,1)S(1)}, bf16[80,2048]{1,0:T(8,128)(2,1)S(1)}) custom-call(bf16[80,2048]{1,0:T(8,128)(2,1)S(1)} %collective-permute-done.32.refs_0_, bf16[80,2048]{1,0:T(8,128)(2,1)S(1)} %collective-permute-done.33.refs_1_, ...), custom_call_target="tpu_custom_call" | custom-call | flops 1 | bytes 1 | tf_op jit(solution)/shard_map/experts/pallas_call | solution.py:72
  109.4 4.2 %collective-permute-done.31.refs_2_ = bf16[80,2048]{1,0:T(8,128)(2,1)S(1)} collective-permute-done((bf16[80,2048]{1,0:T(8,128)(2,1)S(1)}, bf16[80,2048]{1,0:T(8,128)(2,1)S(1)}, u32[]{:S(2)}, u32[]{:S(2)}) %collective-permute-start.31) | collective-permute-done | bytes 327712 | tf_op jit(solution)/shard_map/ppermute | solution.py:36
  114.2 1.7 %collective-permute-start.41 = (bf16[80,2048]{1,0:T(8,128)(2,1)S(1)}, bf16[80,2048]{1,0:T(8,128)(2,1)S(1)}, u32[]{:S(2)}, u32[]{:S(2)}) collective-permute-start(bf16[80,2048]{1,0:T(8,128)(2,1)S(1)} %add.10.refs_9_), channel_id=1, source_target_pairs={{0,2},{1,3},{2,0},{3,1},{4,6},{5,7},{6,4},{7,5},{8,10},{9,11},{10,... | collective-permute-start | bytes 983048 | tf_op jit(solution)/shard_map/ppermute | solution.py:36
  115.9 3.9 %experts.7 = (bf16[80,2048]{1,0:T(8,128)(2,1)S(1)}, bf16[80,2048]{1,0:T(8,128)(2,1)S(1)}, bf16[80,2048]{1,0:T(8,128)(2,1)S(1)}, bf16[80,2048]{1,0:T(8,128)(2,1)S(1)}) custom-call(bf16[80,2048]{1,0:T(8,128)(2,1)S(1)} %collective-permute-done.27.refs_10_.refs_0_, bf16[80,2048]{1,0:T(8,128)(2,1)S(1)} %collective-permute-done.30.refs_1_, ...), custom_call_target="tpu_custom_call" | custom-call | flops 1 | bytes 1 | tf_op jit(solution)/shard_map/experts/pallas_call | solution.py:72
  120.4 3.5 %collective-permute-done.41.refs_2_ = bf16[80,2048]{1,0:T(8,128)(2,1)S(1)} collective-permute-done((bf16[80,2048]{1,0:T(8,128)(2,1)S(1)}, bf16[80,2048]{1,0:T(8,128)(2,1)S(1)}, u32[]{:S(2)}, u32[]{:S(2)}) %collective-permute-start.41) | collective-permute-done | bytes 327712 | tf_op jit(solution)/shard_map/ppermute | solution.py:36
  124.1 1.7 %collective-permute-start.42 = (bf16[80,2048]{1,0:T(8,128)(2,1)S(1)}, bf16[80,2048]{1,0:T(8,128)(2,1)S(1)}, u32[]{:S(2)}, u32[]{:S(2)}) collective-permute-start(bf16[80,2048]{1,0:T(8,128)(2,1)S(1)} %add.12.refs_4_), channel_id=1, source_target_pairs={{0,2},{1,3},{2,0},{3,1},{4,6},{5,7},{6,4},{7,5},{8,10},{9,11},{10,... | collective-permute-start | bytes 983048 | tf_op jit(solution)/shard_map/ppermute | solution.py:36
  125.8 1.8 %collective-permute-start.43 = (bf16[80,2048]{1,0:T(8,128)(2,1)S(1)}, bf16[80,2048]{1,0:T(8,128)(2,1)S(1)}, u32[]{:S(2)}, u32[]{:S(2)}) collective-permute-start(bf16[80,2048]{1,0:T(8,128)(2,1)S(1)} %add.11.refs_2_), channel_id=1, source_target_pairs={{0,4},{1,5},{2,6},{3,7},{4,0},{5,1},{6,2},{7,3},{8,12},{9,13},{10,... | collective-permute-start | bytes 983048 | tf_op jit(solution)/shard_map/ppermute | solution.py:36
  128.1 4.8 %collective-permute-done.42.refs_2_ = bf16[80,2048]{1,0:T(8,128)(2,1)S(1)} collective-permute-done((bf16[80,2048]{1,0:T(8,128)(2,1)S(1)}, bf16[80,2048]{1,0:T(8,128)(2,1)S(1)}, u32[]{:S(2)}, u32[]{:S(2)}) %collective-permute-start.42) | collective-permute-done | bytes 327712 | tf_op jit(solution)/shard_map/ppermute | solution.py:36
  132.9 1.4 collective-permute-done.43.refs_3_
  135.7 3.5 %collective-permute-start.47 = (bf16[80,2048]{1,0:T(8,128)(2,1)S(1)}, bf16[80,2048]{1,0:T(8,128)(2,1)S(1)}, u32[]{:S(2)}, u32[]{:S(2)}) collective-permute-start(bf16[80,2048]{1,0:T(8,128)(2,1)S(1)} %add.13.refs_2_), channel_id=1, source_target_pairs={{0,8},{1,9},{2,10},{3,11},{4,12},{5,13},{6,14},{7,15},{8,0},{9,1},... | collective-permute-start | bytes 983048 | tf_op jit(solution)/shard_map/ppermute | solution.py:36
  139.2 3.1 %collective-permute-done.44.refs_2_ = bf16[80,2048]{1,0:T(8,128)(2,1)S(1)} collective-permute-done((bf16[80,2048]{1,0:T(8,128)(2,1)S(1)}, bf16[80,2048]{1,0:T(8,128)(2,1)S(1)}, u32[]{:S(2)}, u32[]{:S(2)}) %collective-permute-start.44) | collective-permute-done | bytes 327712 | tf_op jit(solution)/shard_map/ppermute | solution.py:36
  142.3 1.8 %collective-permute-start.46 = (bf16[80,2048]{1,0:T(8,128)(2,1)S(1)}, bf16[80,2048]{1,0:T(8,128)(2,1)S(1)}, u32[]{:S(2)}, u32[]{:S(2)}) collective-permute-start(bf16[80,2048]{1,0:T(8,128)(2,1)S(1)} %add.15.refs_2_), channel_id=1, source_target_pairs={{0,4},{1,5},{2,6},{3,7},{4,0},{5,1},{6,2},{7,3},{8,12},{9,13},{10,... | collective-permute-start | bytes 983048 | tf_op jit(solution)/shard_map/ppermute | solution.py:36
  144.9 9.3 %collective-permute-done.47.refs_4_ = bf16[80,2048]{1,0:T(8,128)(2,1)S(1)} collective-permute-done((bf16[80,2048]{1,0:T(8,128)(2,1)S(1)}, bf16[80,2048]{1,0:T(8,128)(2,1)S(1)}, u32[]{:S(2)}, u32[]{:S(2)}) %collective-permute-start.47) | collective-permute-done | bytes 327712 | tf_op jit(solution)/shard_map/ppermute | solution.py:36
  154.2 1.1 collective-permute-done.46.refs_3_
  155.2 0.9 add.17
  (95 shorter events, 11.4 us)
Async XLA Ops:
  0.6 32.1 %collective-permute-start.13 = (bf16[256,2048]{1,0:T(8,128)(2,1)}, bf16[256,2048]{1,0:T(8,128)(2,1)S(1)}, u32[]{:S(2)}, u32[]{:S(2)}) collective-permute-start(bf16[256,2048]{1,0:T(8,128)(2,1)} %refs_9_.7), channel_id=1, source_target_pairs={{0,2},{1,3},{2,0},{3,1},{4,6},{5,7},{6,4},{7,5},{8,10},{9,11},{10,... | collective-permute-start | bytes 3145736 | tf_op jit(solution)/shard_map/ppermute | solution.py:36
  5.5 7.3 %collective-permute-start = (bf16[272,128]{1,0:T(8,128)(2,1)}, bf16[272,128]{1,0:T(8,128)(2,1)S(1)}, u32[]{:S(2)}, u32[]{:S(2)}) collective-permute-start(bf16[272,128]{1,0:T(8,128)(2,1)} %get-tuple-element.39), channel_id=1, source_target_pairs={{0,4},{1,5},{2,6},{3,7},{4,0},{5,1},{6,2},{7,3},{8,12},{9,13},{10,... | collective-permute-start | bytes 208904 | tf_op jit(solution)/shard_map/ppermute | solution.py:36
  7.2 9.2 %collective-permute-start.7 = (bf16[272,128]{1,0:T(8,128)(2,1)}, bf16[272,128]{1,0:T(8,128)(2,1)S(1)}, u32[]{:S(2)}, u32[]{:S(2)}) collective-permute-start(bf16[272,128]{1,0:T(8,128)(2,1)} %get-tuple-element.44), channel_id=1, source_target_pairs={{0,8},{1,9},{2,10},{3,11},{4,12},{5,13},{6,14},{7,15},{8,0},{9,1},... | collective-permute-start | bytes 208904 | tf_op jit(solution)/shard_map/ppermute | solution.py:36
  9.8 9.3 %collective-permute-start.8 = (bf16[272,128]{1,0:T(8,128)(2,1)}, bf16[272,128]{1,0:T(8,128)(2,1)S(1)}, u32[]{:S(2)}, u32[]{:S(2)}) collective-permute-start(bf16[272,128]{1,0:T(8,128)(2,1)} %get-tuple-element.45), channel_id=1, source_target_pairs={{0,12},{1,13},{2,14},{3,15},{4,8},{5,9},{6,10},{7,11},{8,4},{9,5},... | collective-permute-start | bytes 208904 | tf_op jit(solution)/shard_map/ppermute | solution.py:36
  12.1 11.0 %collective-permute-start.3 = (bf16[800,128]{1,0:T(8,128)(2,1)}, bf16[800,128]{1,0:T(8,128)(2,1)S(1)}, u32[]{:S(2)}, u32[]{:S(2)}) collective-permute-start(bf16[800,128]{1,0:T(8,128)(2,1)} %get-tuple-element.40), channel_id=1, source_target_pairs={{0,4},{1,5},{2,6},{3,7},{4,0},{5,1},{6,2},{7,3},{8,12},{9,13},{10,... | collective-permute-start | bytes 614408 | tf_op jit(solution)/shard_map/ppermute | solution.py:36
  12.8 18.5 %collective-permute-start.4 = (bf16[800,128]{1,0:T(8,128)(2,1)}, bf16[800,128]{1,0:T(8,128)(2,1)S(1)}, u32[]{:S(2)}, u32[]{:S(2)}) collective-permute-start(bf16[800,128]{1,0:T(8,128)(2,1)} %get-tuple-element.41), channel_id=1, source_target_pairs={{0,8},{1,9},{2,10},{3,11},{4,12},{5,13},{6,14},{7,15},{8,0},{9,1},... | collective-permute-start | bytes 614408 | tf_op jit(solution)/shard_map/ppermute | solution.py:36
  16.3 15.0 %collective-permute-start.5 = (bf16[800,128]{1,0:T(8,128)(2,1)}, bf16[800,128]{1,0:T(8,128)(2,1)S(1)}, u32[]{:S(2)}, u32[]{:S(2)}) collective-permute-start(bf16[800,128]{1,0:T(8,128)(2,1)} %get-tuple-element.42), channel_id=1, source_target_pairs={{0,12},{1,13},{2,14},{3,15},{4,8},{5,9},{6,10},{7,11},{8,4},{9,5},... | collective-permute-start | bytes 614408 | tf_op jit(solution)/shard_map/ppermute | solution.py:36
  19.3 12.0 %collective-permute-start.10 = (bf16[544,128]{1,0:T(8,128)(2,1)S(1)}, bf16[544,128]{1,0:T(8,128)(2,1)S(1)}, u32[]{:S(2)}, u32[]{:S(2)}) collective-permute-start(bf16[544,128]{1,0:T(8,128)(2,1)S(1)} %merge.3.refs_5_.refs_4_), channel_id=1, source_target_pairs={{0,2},{1,3},{2,0},{3,1},{4,6},{5,7},{6,4},{7,5},{8,10},{9,11},{10,... | collective-permute-start | bytes 417800 | tf_op jit(solution)/shard_map/ppermute | solution.py:36
  31.3 1.4 collective-permute-start.11
  31.3 8.8 %collective-permute-start.12 = (bf16[256,2048]{1,0:T(8,128)(2,1)S(1)}, bf16[256,2048]{1,0:T(8,128)(2,1)S(1)}, u32[]{:S(2)}, u32[]{:S(2)}) collective-permute-start(bf16[256,2048]{1,0:T(8,128)(2,1)S(1)} %copy-done.3), channel_id=1, source_target_pairs={{0,1},{1,0},{2,3},{3,2},{4,5},{5,4},{6,7},{7,6},{8,9},{9,8},{10,11... | collective-permute-start | bytes 3145736 | tf_op jit(solution)/shard_map/ppermute | solution.py:36
  32.7 7.5 %collective-permute-start.14 = (bf16[256,2048]{1,0:T(8,128)(2,1)S(1)}, bf16[256,2048]{1,0:T(8,128)(2,1)S(1)}, u32[]{:S(2)}, u32[]{:S(2)}) collective-permute-start(bf16[256,2048]{1,0:T(8,128)(2,1)S(1)} %collective-permute-done.13.refs_11_), channel_id=1, source_target_pairs={{0,1},{1,0},{2,3},{3,2},{4,5},{5,4},{6,7},{7,6},{8,9},{9,8},{10,11... | collective-permute-start | bytes 3145736 | tf_op jit(solution)/shard_map/ppermute | solution.py:36
  32.8 5.9 %collective-permute-start.2 = (bf16[544,128]{1,0:T(8,128)(2,1)S(1)}, bf16[544,128]{1,0:T(8,128)(2,1)S(1)}, u32[]{:S(2)}, u32[]{:S(2)}) collective-permute-start(bf16[544,128]{1,0:T(8,128)(2,1)S(1)} %merge.2.refs_2_.refs_1_.refs_0_), channel_id=1, source_target_pairs={{0,2},{1,3},{2,0},{3,1},{4,6},{5,7},{6,4},{7,5},{8,10},{9,11},{10,... | collective-permute-start | bytes 417800 | tf_op jit(solution)/shard_map/ppermute | solution.py:36
  33.4 5.4 %collective-permute-start.9 = (bf16[544,128]{1,0:T(8,128)(2,1)S(1)}, bf16[544,128]{1,0:T(8,128)(2,1)S(1)}, u32[]{:S(2)}, u32[]{:S(2)}) collective-permute-start(bf16[544,128]{1,0:T(8,128)(2,1)S(1)} %merge.3.refs_5_.refs_4_), channel_id=1, source_target_pairs={{0,1},{1,0},{2,3},{3,2},{4,5},{5,4},{6,7},{7,6},{8,9},{9,8},{10,11... | collective-permute-start | bytes 417800 | tf_op jit(solution)/shard_map/ppermute | solution.py:36
  33.4 5.4 %collective-permute-start.1 = (bf16[544,128]{1,0:T(8,128)(2,1)S(1)}, bf16[544,128]{1,0:T(8,128)(2,1)S(1)}, u32[]{:S(2)}, u32[]{:S(2)}) collective-permute-start(bf16[544,128]{1,0:T(8,128)(2,1)S(1)} %merge.2.refs_2_.refs_1_.refs_0_), channel_id=1, source_target_pairs={{0,1},{1,0},{2,3},{3,2},{4,5},{5,4},{6,7},{7,6},{8,9},{9,8},{10,11... | collective-permute-start | bytes 417800 | tf_op jit(solution)/shard_map/ppermute | solution.py:36
  38.8 1.4 collective-permute-start.6
  43.5 11.6 %collective-permute-start.15 = (bf16[80,2048]{1,0:T(8,128)(2,1)S(1)}, bf16[80,2048]{1,0:T(8,128)(2,1)S(1)}, u32[]{:S(2)}, u32[]{:S(2)}) collective-permute-start(bf16[80,2048]{1,0:T(8,128)(2,1)S(1)} %attention.4.refs_13_), channel_id=1, source_target_pairs={{0,4},{1,5},{2,6},{3,7},{4,0},{5,1},{6,2},{7,3},{8,12},{9,13},{10,... | collective-permute-start | bytes 983048 | tf_op jit(solution)/shard_map/ppermute | solution.py:36
  50.1 17.5 %collective-permute-start.16 = (bf16[80,2048]{1,0:T(8,128)(2,1)S(1)}, bf16[80,2048]{1,0:T(8,128)(2,1)S(1)}, u32[]{:S(2)}, u32[]{:S(2)}) collective-permute-start(bf16[80,2048]{1,0:T(8,128)(2,1)S(1)} %attention.5.refs_13_), channel_id=1, source_target_pairs={{0,4},{1,5},{2,6},{3,7},{4,0},{5,1},{6,2},{7,3},{8,12},{9,13},{10,... | collective-permute-start | bytes 983048 | tf_op jit(solution)/shard_map/ppermute | solution.py:36
  55.2 16.8 %collective-permute-start.17 = (bf16[80,2048]{1,0:T(8,128)(2,1)S(1)}, bf16[80,2048]{1,0:T(8,128)(2,1)S(1)}, u32[]{:S(2)}, u32[]{:S(2)}) collective-permute-start(bf16[80,2048]{1,0:T(8,128)(2,1)S(1)} %add.9.refs_13_), channel_id=1, source_target_pairs={{0,8},{1,9},{2,10},{3,11},{4,12},{5,13},{6,14},{7,15},{8,0},{9,1},... | collective-permute-start | bytes 983048 | tf_op jit(solution)/shard_map/ppermute | solution.py:36
  72.9 7.1 %collective-permute-start.19 = (bf16[80,2048]{1,0:T(8,128)(2,1)S(1)}, bf16[80,2048]{1,0:T(8,128)(2,1)S(1)}, u32[]{:S(2)}, u32[]{:S(2)}) collective-permute-start(bf16[80,2048]{1,0:T(8,128)(2,1)S(1)} %get-tuple-element.50.refs_0_), channel_id=1, source_target_pairs={{0,2},{1,3},{2,0},{3,1},{4,6},{5,7},{6,4},{7,5},{8,10},{9,11},{10,... | collective-permute-start | bytes 983048 | tf_op jit(solution)/shard_map/ppermute | solution.py:36
  73.5 12.7 %collective-permute-start.23 = (bf16[80,2048]{1,0:T(8,128)(2,1)S(1)}, bf16[80,2048]{1,0:T(8,128)(2,1)S(1)}, u32[]{:S(2)}, u32[]{:S(2)}) collective-permute-start(bf16[80,2048]{1,0:T(8,128)(2,1)S(1)} %get-tuple-element.50.refs_0_), channel_id=1, source_target_pairs={{0,4},{1,5},{2,6},{3,7},{4,0},{5,1},{6,2},{7,3},{8,12},{9,13},{10,... | collective-permute-start | bytes 983048 | tf_op jit(solution)/shard_map/ppermute | solution.py:36
  73.5 15.9 %collective-permute-start.27 = (bf16[80,2048]{1,0:T(8,128)(2,1)S(1)}, bf16[80,2048]{1,0:T(8,128)(2,1)S(1)}, u32[]{:S(2)}, u32[]{:S(2)}) collective-permute-start(bf16[80,2048]{1,0:T(8,128)(2,1)S(1)} %get-tuple-element.50.refs_0_), channel_id=1, source_target_pairs={{0,8},{1,9},{2,10},{3,11},{4,12},{5,13},{6,14},{7,15},{8,0},{9,1},... | collective-permute-start | bytes 983048 | tf_op jit(solution)/shard_map/ppermute | solution.py:36
  76.3 13.0 %collective-permute-start.18 = (bf16[80,2048]{1,0:T(8,128)(2,1)S(1)}, bf16[80,2048]{1,0:T(8,128)(2,1)S(1)}, u32[]{:S(2)}, u32[]{:S(2)}) collective-permute-start(bf16[80,2048]{1,0:T(8,128)(2,1)S(1)} %get-tuple-element.50.refs_0_), channel_id=1, source_target_pairs={{0,1},{1,0},{2,3},{3,2},{4,5},{5,4},{6,7},{7,6},{8,9},{9,8},{10,11... | collective-permute-start | bytes 983048 | tf_op jit(solution)/shard_map/ppermute | solution.py:36
  80.0 9.3 %collective-permute-start.20 = (bf16[80,2048]{1,0:T(8,128)(2,1)S(1)}, bf16[80,2048]{1,0:T(8,128)(2,1)S(1)}, u32[]{:S(2)}, u32[]{:S(2)}) collective-permute-start(bf16[80,2048]{1,0:T(8,128)(2,1)S(1)} %collective-permute-done.19.refs_2_), channel_id=1, source_target_pairs={{0,1},{1,0},{2,3},{3,2},{4,5},{5,4},{6,7},{7,6},{8,9},{9,8},{10,11... | collective-permute-start | bytes 983048 | tf_op jit(solution)/shard_map/ppermute | solution.py:36
  86.2 7.1 %collective-permute-start.25 = (bf16[80,2048]{1,0:T(8,128)(2,1)S(1)}, bf16[80,2048]{1,0:T(8,128)(2,1)S(1)}, u32[]{:S(2)}, u32[]{:S(2)}) collective-permute-start(bf16[80,2048]{1,0:T(8,128)(2,1)S(1)} %collective-permute-done.23.refs_0_), channel_id=1, source_target_pairs={{0,2},{1,3},{2,0},{3,1},{4,6},{5,7},{6,4},{7,5},{8,10},{9,11},{10,... | collective-permute-start | bytes 983048 | tf_op jit(solution)/shard_map/ppermute | solution.py:36
  89.3 7.1 %collective-permute-start.32 = (bf16[80,2048]{1,0:T(8,128)(2,1)S(1)}, bf16[80,2048]{1,0:T(8,128)(2,1)S(1)}, u32[]{:S(2)}, u32[]{:S(2)}) collective-permute-start(bf16[80,2048]{1,0:T(8,128)(2,1)S(1)} %collective-permute-done.27.refs_10_.refs_0_), channel_id=1, source_target_pairs={{0,4},{1,5},{2,6},{3,7},{4,0},{5,1},{6,2},{7,3},{8,12},{9,13},{10,... | collective-permute-start | bytes 983048 | tf_op jit(solution)/shard_map/ppermute | solution.py:36
  89.3 8.6 %collective-permute-start.24 = (bf16[80,2048]{1,0:T(8,128)(2,1)S(1)}, bf16[80,2048]{1,0:T(8,128)(2,1)S(1)}, u32[]{:S(2)}, u32[]{:S(2)}) collective-permute-start(bf16[80,2048]{1,0:T(8,128)(2,1)S(1)} %collective-permute-done.23.refs_0_), channel_id=1, source_target_pairs={{0,1},{1,0},{2,3},{3,2},{4,5},{5,4},{6,7},{7,6},{8,9},{9,8},{10,11... | collective-permute-start | bytes 983048 | tf_op jit(solution)/shard_map/ppermute | solution.py:36
  93.3 4.6 %collective-permute-start.26 = (bf16[80,2048]{1,0:T(8,128)(2,1)S(1)}, bf16[80,2048]{1,0:T(8,128)(2,1)S(1)}, u32[]{:S(2)}, u32[]{:S(2)}) collective-permute-start(bf16[80,2048]{1,0:T(8,128)(2,1)S(1)} %collective-permute-done.25.refs_2_), channel_id=1, source_target_pairs={{0,1},{1,0},{2,3},{3,2},{4,5},{5,4},{6,7},{7,6},{8,9},{9,8},{10,11... | collective-permute-start | bytes 983048 | tf_op jit(solution)/shard_map/ppermute | solution.py:36
  96.4 7.1 %collective-permute-start.34 = (bf16[80,2048]{1,0:T(8,128)(2,1)S(1)}, bf16[80,2048]{1,0:T(8,128)(2,1)S(1)}, u32[]{:S(2)}, u32[]{:S(2)}) collective-permute-start(bf16[80,2048]{1,0:T(8,128)(2,1)S(1)} %collective-permute-done.32.refs_0_), channel_id=1, source_target_pairs={{0,2},{1,3},{2,0},{3,1},{4,6},{5,7},{6,4},{7,5},{8,10},{9,11},{10,... | collective-permute-start | bytes 983048 | tf_op jit(solution)/shard_map/ppermute | solution.py:36
  97.9 7.5 %collective-permute-start.33 = (bf16[80,2048]{1,0:T(8,128)(2,1)S(1)}, bf16[80,2048]{1,0:T(8,128)(2,1)S(1)}, u32[]{:S(2)}, u32[]{:S(2)}) collective-permute-start(bf16[80,2048]{1,0:T(8,128)(2,1)S(1)} %collective-permute-done.32.refs_0_), channel_id=1, source_target_pairs={{0,1},{1,0},{2,3},{3,2},{4,5},{5,4},{6,7},{7,6},{8,9},{9,8},{10,11... | collective-permute-start | bytes 983048 | tf_op jit(solution)/shard_map/ppermute | solution.py:36
  103.5 1.9 %collective-permute-start.35 = (bf16[80,2048]{1,0:T(8,128)(2,1)S(1)}, bf16[80,2048]{1,0:T(8,128)(2,1)S(1)}, u32[]{:S(2)}, u32[]{:S(2)}) collective-permute-start(bf16[80,2048]{1,0:T(8,128)(2,1)S(1)} %collective-permute-done.34.refs_2_), channel_id=1, source_target_pairs={{0,1},{1,0},{2,3},{3,2},{4,5},{5,4},{6,7},{7,6},{8,9},{9,8},{10,11... | collective-permute-start | bytes 983048 | tf_op jit(solution)/shard_map/ppermute | solution.py:36
  103.5 10.1 %collective-permute-start.31 = (bf16[80,2048]{1,0:T(8,128)(2,1)S(1)}, bf16[80,2048]{1,0:T(8,128)(2,1)S(1)}, u32[]{:S(2)}, u32[]{:S(2)}) collective-permute-start(bf16[80,2048]{1,0:T(8,128)(2,1)S(1)} %collective-permute-done.27.refs_10_.refs_0_), channel_id=1, source_target_pairs={{0,2},{1,3},{2,0},{3,1},{4,6},{5,7},{6,4},{7,5},{8,10},{9,11},{10,... | collective-permute-start | bytes 983048 | tf_op jit(solution)/shard_map/ppermute | solution.py:36
  105.1 10.8 %collective-permute-start.30 = (bf16[80,2048]{1,0:T(8,128)(2,1)S(1)}, bf16[80,2048]{1,0:T(8,128)(2,1)S(1)}, u32[]{:S(2)}, u32[]{:S(2)}) collective-permute-start(bf16[80,2048]{1,0:T(8,128)(2,1)S(1)} %collective-permute-done.27.refs_10_.refs_0_), channel_id=1, source_target_pairs={{0,1},{1,0},{2,3},{3,2},{4,5},{5,4},{6,7},{7,6},{8,9},{9,8},{10,11... | collective-permute-start | bytes 983048 | tf_op jit(solution)/shard_map/ppermute | solution.py:36
  109.0 5.1 %collective-permute-start.37 = (bf16[80,2048]{1,0:T(8,128)(2,1)S(1)}, bf16[80,2048]{1,0:T(8,128)(2,1)S(1)}, u32[]{:S(2)}, u32[]{:S(2)}) collective-permute-start(bf16[80,2048]{1,0:T(8,128)(2,1)S(1)} %get-tuple-element.66), channel_id=1, source_target_pairs={{0,1},{1,0},{2,3},{3,2},{4,5},{5,4},{6,7},{7,6},{8,9},{9,8},{10,11... | collective-permute-start | bytes 983048 | tf_op jit(solution)/shard_map/ppermute | solution.py:36
  113.6 2.3 %collective-permute-start.36 = (bf16[80,2048]{1,0:T(8,128)(2,1)S(1)}, bf16[80,2048]{1,0:T(8,128)(2,1)S(1)}, u32[]{:S(2)}, u32[]{:S(2)}) collective-permute-start(bf16[80,2048]{1,0:T(8,128)(2,1)S(1)} %collective-permute-done.31.refs_2_), channel_id=1, source_target_pairs={{0,1},{1,0},{2,3},{3,2},{4,5},{5,4},{6,7},{7,6},{8,9},{9,8},{10,11... | collective-permute-start | bytes 983048 | tf_op jit(solution)/shard_map/ppermute | solution.py:36
  113.6 6.8 %collective-permute-start.40 = (bf16[80,2048]{1,0:T(8,128)(2,1)S(1)}, bf16[80,2048]{1,0:T(8,128)(2,1)S(1)}, u32[]{:S(2)}, u32[]{:S(2)}) collective-permute-start(bf16[80,2048]{1,0:T(8,128)(2,1)S(1)} %get-tuple-element.71), channel_id=1, source_target_pairs={{0,1},{1,0},{2,3},{3,2},{4,5},{5,4},{6,7},{7,6},{8,9},{9,8},{10,11... | collective-permute-start | bytes 983048 | tf_op jit(solution)/shard_map/ppermute | solution.py:36
  114.2 9.7 %collective-permute-start.41 = (bf16[80,2048]{1,0:T(8,128)(2,1)S(1)}, bf16[80,2048]{1,0:T(8,128)(2,1)S(1)}, u32[]{:S(2)}, u32[]{:S(2)}) collective-permute-start(bf16[80,2048]{1,0:T(8,128)(2,1)S(1)} %add.10.refs_9_), channel_id=1, source_target_pairs={{0,2},{1,3},{2,0},{3,1},{4,6},{5,7},{6,4},{7,5},{8,10},{9,11},{10,... | collective-permute-start | bytes 983048 | tf_op jit(solution)/shard_map/ppermute | solution.py:36
  119.8 4.2 %collective-permute-start.39 = (bf16[80,2048]{1,0:T(8,128)(2,1)S(1)}, bf16[80,2048]{1,0:T(8,128)(2,1)S(1)}, u32[]{:S(2)}, u32[]{:S(2)}) collective-permute-start(bf16[80,2048]{1,0:T(8,128)(2,1)S(1)} %get-tuple-element.70), channel_id=1, source_target_pairs={{0,1},{1,0},{2,3},{3,2},{4,5},{5,4},{6,7},{7,6},{8,9},{9,8},{10,11... | collective-permute-start | bytes 983048 | tf_op jit(solution)/shard_map/ppermute | solution.py:36
  119.9 8.2 %collective-permute-start.38 = (bf16[80,2048]{1,0:T(8,128)(2,1)S(1)}, bf16[80,2048]{1,0:T(8,128)(2,1)S(1)}, u32[]{:S(2)}, u32[]{:S(2)}) collective-permute-start(bf16[80,2048]{1,0:T(8,128)(2,1)S(1)} %get-tuple-element.68), channel_id=1, source_target_pairs={{0,1},{1,0},{2,3},{3,2},{4,5},{5,4},{6,7},{7,6},{8,9},{9,8},{10,11... | collective-permute-start | bytes 983048 | tf_op jit(solution)/shard_map/ppermute | solution.py:36
  124.1 8.8 %collective-permute-start.42 = (bf16[80,2048]{1,0:T(8,128)(2,1)S(1)}, bf16[80,2048]{1,0:T(8,128)(2,1)S(1)}, u32[]{:S(2)}, u32[]{:S(2)}) collective-permute-start(bf16[80,2048]{1,0:T(8,128)(2,1)S(1)} %add.12.refs_4_), channel_id=1, source_target_pairs={{0,2},{1,3},{2,0},{3,1},{4,6},{5,7},{6,4},{7,5},{8,10},{9,11},{10,... | collective-permute-start | bytes 983048 | tf_op jit(solution)/shard_map/ppermute | solution.py:36
  125.8 8.5 %collective-permute-start.43 = (bf16[80,2048]{1,0:T(8,128)(2,1)S(1)}, bf16[80,2048]{1,0:T(8,128)(2,1)S(1)}, u32[]{:S(2)}, u32[]{:S(2)}) collective-permute-start(bf16[80,2048]{1,0:T(8,128)(2,1)S(1)} %add.11.refs_2_), channel_id=1, source_target_pairs={{0,4},{1,5},{2,6},{3,7},{4,0},{5,1},{6,2},{7,3},{8,12},{9,13},{10,... | collective-permute-start | bytes 983048 | tf_op jit(solution)/shard_map/ppermute | solution.py:36
  127.6 6.9 %collective-permute-start.29 = (bf16[80,2048]{1,0:T(8,128)(2,1)S(1)}, bf16[80,2048]{1,0:T(8,128)(2,1)S(1)}, u32[]{:S(2)}, u32[]{:S(2)}) collective-permute-start(bf16[80,2048]{1,0:T(8,128)(2,1)S(1)} %get-tuple-element.61), channel_id=1, source_target_pairs={{0,1},{1,0},{2,3},{3,2},{4,5},{5,4},{6,7},{7,6},{8,9},{9,8},{10,11... | collective-permute-start | bytes 983048 | tf_op jit(solution)/shard_map/ppermute | solution.py:36
  127.6 11.6 %collective-permute-start.28 = (bf16[80,2048]{1,0:T(8,128)(2,1)S(1)}, bf16[80,2048]{1,0:T(8,128)(2,1)S(1)}, u32[]{:S(2)}, u32[]{:S(2)}) collective-permute-start(bf16[80,2048]{1,0:T(8,128)(2,1)S(1)} %get-tuple-element.59), channel_id=1, source_target_pairs={{0,1},{1,0},{2,3},{3,2},{4,5},{5,4},{6,7},{7,6},{8,9},{9,8},{10,11... | collective-permute-start | bytes 983048 | tf_op jit(solution)/shard_map/ppermute | solution.py:36
  134.6 7.6 %collective-permute-start.44 = (bf16[80,2048]{1,0:T(8,128)(2,1)S(1)}, bf16[80,2048]{1,0:T(8,128)(2,1)S(1)}, u32[]{:S(2)}, u32[]{:S(2)}) collective-permute-start(bf16[80,2048]{1,0:T(8,128)(2,1)S(1)} %add.14.refs_3_), channel_id=1, source_target_pairs={{0,2},{1,3},{2,0},{3,1},{4,6},{5,7},{6,4},{7,5},{8,10},{9,11},{10,... | collective-permute-start | bytes 983048 | tf_op jit(solution)/shard_map/ppermute | solution.py:36
  135.2 9.0 %collective-permute-start.22 = (bf16[80,2048]{1,0:T(8,128)(2,1)S(1)}, bf16[80,2048]{1,0:T(8,128)(2,1)S(1)}, u32[]{:S(2)}, u32[]{:S(2)}) collective-permute-start(bf16[80,2048]{1,0:T(8,128)(2,1)S(1)} %get-tuple-element.56), channel_id=1, source_target_pairs={{0,1},{1,0},{2,3},{3,2},{4,5},{5,4},{6,7},{7,6},{8,9},{9,8},{10,11... | collective-permute-start | bytes 983048 | tf_op jit(solution)/shard_map/ppermute | solution.py:36
  135.2 9.7 %collective-permute-start.21 = (bf16[80,2048]{1,0:T(8,128)(2,1)S(1)}, bf16[80,2048]{1,0:T(8,128)(2,1)S(1)}, u32[]{:S(2)}, u32[]{:S(2)}) collective-permute-start(bf16[80,2048]{1,0:T(8,128)(2,1)S(1)} %get-tuple-element.54), channel_id=1, source_target_pairs={{0,1},{1,0},{2,3},{3,2},{4,5},{5,4},{6,7},{7,6},{8,9},{9,8},{10,11... | collective-permute-start | bytes 983048 | tf_op jit(solution)/shard_map/ppermute | solution.py:36
  135.7 18.5 %collective-permute-start.47 = (bf16[80,2048]{1,0:T(8,128)(2,1)S(1)}, bf16[80,2048]{1,0:T(8,128)(2,1)S(1)}, u32[]{:S(2)}, u32[]{:S(2)}) collective-permute-start(bf16[80,2048]{1,0:T(8,128)(2,1)S(1)} %add.13.refs_2_), channel_id=1, source_target_pairs={{0,8},{1,9},{2,10},{3,11},{4,12},{5,13},{6,14},{7,15},{8,0},{9,1},... | collective-permute-start | bytes 983048 | tf_op jit(solution)/shard_map/ppermute | solution.py:36
  142.3 12.9 %collective-permute-start.46 = (bf16[80,2048]{1,0:T(8,128)(2,1)S(1)}, bf16[80,2048]{1,0:T(8,128)(2,1)S(1)}, u32[]{:S(2)}, u32[]{:S(2)}) collective-permute-start(bf16[80,2048]{1,0:T(8,128)(2,1)S(1)} %add.15.refs_2_), channel_id=1, source_target_pairs={{0,4},{1,5},{2,6},{3,7},{4,0},{5,1},{6,2},{7,3},{8,12},{9,13},{10,... | collective-permute-start | bytes 983048 | tf_op jit(solution)/shard_map/ppermute | solution.py:36
  144.2 11.0 %collective-permute-start.45 = (bf16[80,2048]{1,0:T(8,128)(2,1)S(1)}, bf16[80,2048]{1,0:T(8,128)(2,1)S(1)}, u32[]{:S(2)}, u32[]{:S(2)}) collective-permute-start(bf16[80,2048]{1,0:T(8,128)(2,1)S(1)} %add.16), channel_id=1, source_target_pairs={{0,2},{1,3},{2,0},{3,1},{4,6},{5,7},{6,4},{7,5},{8,10},{9,11},{10,... | collective-permute-start | bytes 983048 | tf_op jit(solution)/shard_map/ppermute | solution.py:36
  (11 other events, 209.8 us)
